TPU v7x, 256 devices: a whole 4x4x8 slice. The times are simulated.
256 devices in a mesh: dp: 16 (over z, core), fsdp: 16 (over x, y).
Axes of the slice: x: 4, y: 4, z: 8, core: 2. Of those that a mesh axis runs over, the one named last changes fastest.
Arguments:
- activations: bfloat16 [131072, 4096], P(('dp', 'fsdp'))
- cotangent: bfloat16 [131072, 1024], P(('dp', 'fsdp'))
- value_weights: bfloat16 [4096, 1024], P('fsdp'), may hold values from -0.09375 to 0.09375
- sign_flips: int32 [4096, 1024], P('fsdp'), may hold values from -1 to 1, as said below
- level_count: int32 [], replicated, may hold values from 48 to 96
Outputs:
- input_grad: bfloat16 [131072, 4096], P(('dp', 'fsdp'))
- weight_grad: float32 [4096, 1024], P('fsdp')
Inputs may be any that keep to these rules, and one draw needn't show every extreme that they name: `sign_flips`: each entry is -1 or 1.
All inputs are finite; a program needn't handle non-finite values. Where the computation divides by a largest or mean magnitude, that divisor is 1e-20 or more.
Results may differ from a plain program's by a relative error of at most 0.0035.
Values may be sent and summed in bfloat16 or wider, within the bound.
No kernel may reach another device: no remote copies, remote signals or barrier semaphores. Data moves between devices by JAX's collectives and lax.ppermute only.
A program may use at most 128 MiB of HBM per device.

v0:
```python
import math

import jax
import jax.numpy as jnp
from jax import lax
from jax.sharding import PartitionSpec as P

BLOCK = 4096


def hadamard(matrix_size):
    positions = jnp.arange(matrix_size, dtype=jnp.int32)
    common_bits = jnp.bitwise_and(positions[:, None], positions[None, :])
    parity = jnp.zeros((matrix_size, matrix_size), jnp.int32)
    for bit_pos in range(max(matrix_size.bit_length() - 1, 0)):
        parity = parity + jnp.bitwise_and(jnp.right_shift(common_bits, bit_pos), 1)
    return (1 - 2 * jnp.bitwise_and(parity, 1)).astype(jnp.float32)


def transform(values, block_size):
    outer_size = block_size // 128
    outer_matrix = hadamard(outer_size)
    inner_matrix = hadamard(128)
    shaped = values.reshape(-1, outer_size, 128)
    step_one = jnp.einsum("bij,jk->bik", shaped, inner_matrix, precision=lax.Precision.HIGHEST)
    step_two = jnp.einsum("li,bik->blk", outer_matrix, step_one, precision=lax.Precision.HIGHEST)
    return step_two.reshape(values.shape) / math.sqrt(block_size)


def shards(activations, cotangent, value_weights, sign_flips, level_count):
    rows_here = value_weights.shape[0]
    kv_width = value_weights.shape[1]
    input_grad = lax.dot_general(
        cotangent,
        lax.all_gather(value_weights, "fsdp", axis=0, tiled=True),
        (((1,), (1,)), ((), ())),
        preferred_element_type=jnp.float32,
    ).astype(jnp.bfloat16)
    partial_sum = lax.psum_scatter(
        lax.dot_general(
            activations, cotangent, (((0,), (0,)), ((), ())), preferred_element_type=jnp.float32
        ),
        "fsdp",
        scatter_dimension=0,
        tiled=True,
    )
    signs_float = sign_flips.astype(jnp.float32)
    rotated = transform(signs_float * partial_sum, BLOCK)
    count_blocks = rows_here * kv_width // BLOCK
    by_block = rotated.reshape(count_blocks, BLOCK)
    local_peak = jnp.max(jnp.abs(by_block), axis=1)
    block_peak = lax.pmax(local_peak, "dp") + 1e-06
    level_float = level_count.astype(jnp.float32)
    levels = jnp.floor(by_block * (level_float / block_peak)[:, None] + 0.5).astype(jnp.bfloat16)
    totals = lax.psum(levels, "dp").astype(jnp.float32)
    decoded = totals * (block_peak / level_float)[:, None]
    weight_grad = signs_float * transform(decoded.reshape(rows_here, kv_width), BLOCK)
    return (input_grad, weight_grad)


def solution(mesh):
    placed = (
        P(("dp", "fsdp"), None),
        P(("dp", "fsdp"), None),
        P("fsdp", None),
        P("fsdp", None),
        P(),
    )
    return jax.shard_map(
        shards,
        mesh=mesh,
        in_specs=placed,
        out_specs=(P(("dp", "fsdp"), None), P("fsdp", None)),
        check_vma=False,
    )
```

profile of v0, /device:TPU:1, one launch (start us, length us, event | category | flops | bytes accessed | tf_op | source)
XLA Modules:
  0.0 341.9 jit_solution(8882305637094356570)
XLA Ops:
  7.2 0.0 copy-start
  7.2 0.0 reduce-scatter.2.cloned.1.call-start
  7.2 1.2 copy-done
  8.4 10.4 %fusion.41 = f32[4096,1024]{1,0:T(8,128)} fusion(bf16[512,4096]{1,0:T(8,128)(2,1)} %param.5, bf16[512,1024]{1,0:T(8,128)(2,1)S(1)} %copy-done), kind=kOutput, calls=%fused_computation.52 | convolution fusion | flops 4294967296 | bytes 22020096 | tf_op jit(solution)/shard_map/dot_general | solution.py:40
  18.8 0.0 copy-start.1
  18.8 0.0 reduce-scatter.2.cloned.1.call-update
  18.8 0.0 all-gather.2.cloned.1.call-start
  18.8 0.7 all-gather.2.cloned.1.call-update
  19.5 0.0 all-reduce.2.cloned.1.call-start
  20.2 117.8 %reduce-scatter.2.cloned.1.call-done = f32[256,1024]{1,0:T(8,128)} async-done(((f32[4096,1024]{1,0:T(8,128)}), f32[256,1024]{1,0:T(8,128)}) %reduce-scatter.2.cloned.1.call-update) | async-done | bytes 1048592 | tf_op jit(solution)/shard_map/reduce_scatter | solution.py:39
  138.0 0.0 copy-done.1
  138.0 1.4 convert_multiply_fusion.1
  139.4 1.1 reshape.17
  140.5 2.2 fusion.8
  142.8 1.5 fusion.5
  144.2 25.2 %pmax.7 = f32[64]{0:T(128)S(1)} all-reduce(f32[64]{0:T(128)S(1)} %get-tuple-element.4), channel_id=1, replica_groups=mesh['dp'=16,'fsdp'=16] {'dp'}, use_global_device_ids=true, to_apply=%region_2.0 | all-reduce | flops 64 | bytes 512 | tf_op jit(solution)/shard_map/pmax | solution.py:52
  169.4 1.4 fusion.3
  170.9 0.0 all-reduce.2.cloned.1.call-update
  170.9 45.3 %all-gather.2.cloned.1.call-done = bf16[4096,1024]{1,0:T(8,128)(2,1)} async-done(((bf16[256,1024]{1,0:T(8,128)(2,1)}), bf16[4096,1024]{1,0:T(8,128)(2,1)}) %all-gather.2.cloned.1.call-update) | async-done | bytes 8388624 | tf_op jit(solution)/shard_map/all_gather | solution.py:35
  216.2 9.5 %convolution_convert_fusion = bf16[512,4096]{1,0:T(8,128)(2,1)} fusion(bf16[512,1024]{1,0:T(8,128)(2,1)S(1)} %copy-done, bf16[4096,1024]{1,0:T(8,128)(2,1)} %all-gather.2.cloned.1.call-done), kind=kOutput, calls=%fused_computation | convolution fusion | flops 4297064448 | bytes 13631488 | tf_op jit(solution)/shard_map/dot_general | solution.py:33
  225.7 102.8 %all-reduce.2.cloned.1.call-done = bf16[64,4096]{1,0:T(8,128)(2,1)} async-done(((bf16[64,4096]{1,0:T(8,128)(2,1)}), bf16[64,4096]{1,0:T(8,128)(2,1)}) %all-reduce.2.cloned.1.call-update) | async-done | bytes 524304 | tf_op jit(solution)/shard_map/psum | solution.py:55
  328.5 1.2 multiply_bitcast_fusion
  329.7 0.2 copy.8
  329.9 1.0 fusion.6
  330.9 2.0 fusion
  332.9 1.4 div.26
  334.3 1.1 convert_multiply_fusion
  (1 shorter events, 0.0 us)
Async XLA Ops:
  7.2 1.2 copy-start
  7.2 130.8 %reduce-scatter.2.cloned.1.call-start = ((), (), s32[]{:S(2)}) async-start(), calls=%async_computation.2 | async-start | bytes 17825792 | tf_op jit(solution)/shard_map/reduce_scatter | solution.py:39
  18.8 119.2 %copy-start.1 = (s32[256,1024]{1,0:T(8,128)S(1)}, s32[256,1024]{1,0:T(8,128)}, u32[]{:S(2)}) copy-start(s32[256,1024]{1,0:T(8,128)} %param.8) | copy-start | bytes 3145732
  18.8 197.4 %all-gather.2.cloned.1.call-start = ((), (), s32[]{:S(2)}) async-start(), calls=%async_computation.1 | async-start | bytes 8912896 | tf_op jit(solution)/shard_map/all_gather | solution.py:35
  19.5 308.9 %all-reduce.2.cloned.1.call-start = ((), (), s32[]{:S(2)}) async-start(), calls=%async_computation.3 | async-start | bytes 1048576 | tf_op jit(solution)/shard_map/psum | solution.py:55
Sparse Core Ops, SparseCore 0:
  18.9 119.0 reduce-scatter.1
  140.4 75.7 all-gather.1
  219.1 109.3 all-reduce.1
where the time goes:
time: 342 us
  waiting for transfers between devices  267 us (78%)
  matrix products  26.6 us (8%)
  blocking collectives  25.2 us (7%)
  between operations  14.4 us (4%)
  other arithmetic  5.12 us (1%)
  local copies, waits for them, and re-layouts  3.88 us (1%)
    reduce_scatter x1, waiting for transfers between devices, shards(): lax.psum_scatter(lax.dot_general(activations, cotangent, (((0,), (0,)), (...  118 us
    psum x1, waiting for transfers between devices, shards(): totals = lax.psum(levels, 'dp').astype(jnp.float32)  103 us
    all_gather x1, waiting for transfers between devices, shards(): lax.all_gather(value_weights, 'fsdp', axis=0, tiled=True)  45.3 us
    pmax x1, blocking collectives, shards(): block_peak = lax.pmax(local_peak, 'dp') + 1e-06  25.2 us
    dot_general x1, matrix products, shards(): lax.dot_general(activations, cotangent, (((0,), (0,)), ((), ())), preferr...  10.4 us
    dot_general x1, matrix products, shards(): lax.dot_general(cotangent, lax.all_gather(value_weights, 'fsdp', axis=0,...  9.45 us
  transfers between devices with their start and end apart: 3, of which 3 were waited for; matrix products, arithmetic and copies ran while one was open for 5% of the time, Pallas kernels for 0%

commit v1 on v0

v1 whole, which is shorter than its diff:
```python
import math

import jax
import jax.numpy as jnp
from jax import lax
from jax.sharding import Mesh, PartitionSpec as P

BLOCK = 4096


def hadamard(matrix_size):
    positions = jnp.arange(matrix_size, dtype=jnp.int32)
    common_bits = jnp.bitwise_and(positions[:, None], positions[None, :])
    parity = jnp.zeros((matrix_size, matrix_size), jnp.int32)
    for bit_pos in range(max(matrix_size.bit_length() - 1, 0)):
        parity = parity + jnp.bitwise_and(jnp.right_shift(common_bits, bit_pos), 1)
    return (1 - 2 * jnp.bitwise_and(parity, 1)).astype(jnp.float32)


def transform(values, block_size):
    outer_size = block_size // 128
    outer_matrix = hadamard(outer_size)
    inner_matrix = hadamard(128)
    shaped = values.reshape(-1, outer_size, 128)
    step_one = jnp.einsum("bij,jk->bik", shaped, inner_matrix, precision=lax.Precision.HIGHEST)
    step_two = jnp.einsum("li,bik->blk", outer_matrix, step_one, precision=lax.Precision.HIGHEST)
    return step_two.reshape(values.shape) / math.sqrt(block_size)


def shards(activations, cotangent, value_weights, sign_flips, level_count):
    rows_here = value_weights.shape[0]
    kv_width = value_weights.shape[1]
    dp = ("z", "core")
    fsdp = ("x", "y")
    input_grad = lax.dot_general(
        cotangent,
        lax.all_gather(value_weights, fsdp, axis=0, tiled=True),
        (((1,), (1,)), ((), ())),
        preferred_element_type=jnp.float32,
    ).astype(jnp.bfloat16)
    partial_sum = lax.psum_scatter(
        lax.dot_general(
            activations, cotangent, (((0,), (0,)), ((), ())), preferred_element_type=jnp.float32
        ),
        fsdp,
        scatter_dimension=0,
        tiled=True,
    )
    signs_float = sign_flips.astype(jnp.float32)
    rotated = transform(signs_float * partial_sum, BLOCK)
    groups = lax.all_to_all(rotated, dp, 0, 0, tiled=True)
    level_float = level_count.astype(jnp.float32)
    by_block = groups.reshape(16, rows_here // 16 * kv_width // BLOCK, BLOCK)
    block_peak = jnp.max(jnp.abs(by_block), axis=(0, 2)) + 1e-06
    levels = jnp.floor(by_block * (level_float / block_peak)[None, :, None] + 0.5)
    totals = jnp.sum(levels, axis=0)
    decoded = totals * (block_peak / level_float)[:, None]
    back = transform(decoded.reshape(rows_here // 16, kv_width), BLOCK)
    weight_grad = signs_float * lax.all_gather(back, dp, axis=0, tiled=True)
    return (input_grad, weight_grad)


def solution(mesh):
    torus = Mesh(mesh.devices.reshape(8, 2, 4, 4), ("z", "core", "x", "y"))
    rows = P(("z", "core", "x", "y"), None)
    part = P(("x", "y"), None)
    return jax.shard_map(
        shards,
        mesh=torus,
        in_specs=(rows, rows, part, part, P()),
        out_specs=(rows, part),
        check_vma=False,
    )
```

time: 342 us -> 267 us (0.78)
  waiting for transfers between devices: 267 us -> 212 us
  blocking collectives: 25.2 us -> 0 us
  starting transfers between devices: 0.12 us -> 8.14 us
    psum x1 -> x0, waiting for transfers between devices: 103 us -> none  [shards(): totals = lax.psum(levels, 'dp').astype(jnp.float32)]
    all_to_all x0 -> x1, waiting for transfers between devices: none -> 27.2 us  [shards(): groups = lax.all_to_all(rotated, dp, 0, 0, tiled=True)]
    pmax x1 -> x0, blocking collectives: 25.2 us -> none  [shards(): block_peak = lax.pmax(local_peak, 'dp') + 1e-06]
    all_gather x1 -> x2, waiting for transfers between devices: 45.3 us -> 65.1 us  [the longest x1 33.4 us: shards(): lax.all_gather(value_weights, fsdp, axis=0, tiled=True)]
    all_to_all x0 -> x1, starting transfers between devices: none -> 8.02 us  [shards(): groups = lax.all_to_all(rotated, dp, 0, 0, tiled=True)]
  transfers between devices with their start and end apart: 3 -> 4, of which waited for: 3 -> 4; matrix products, arithmetic and copies ran while one was open for 5% -> 7% of each run, Pallas kernels for 0% -> 0%
where the time goes in v1:
time: 267 us; the launch traced here: 266 us
  waiting for transfers between devices  212 us (79%)
  matrix products  23.5 us (9%)
  between operations  14.5 us (5%)
  starting transfers between devices  8.14 us (3%)
  local copies, waits for them, and re-layouts  4.35 us (2%)
  other arithmetic  4.3 us (2%)
    reduce_scatter x1, waiting for transfers between devices, shards(): lax.psum_scatter(lax.dot_general(activations, cotangent, (((0,), (0,)), (...  118 us
    all_gather x1, waiting for transfers between devices, shards(): lax.all_gather(value_weights, fsdp, axis=0, tiled=True)  33.4 us
    all_gather x1, waiting for transfers between devices, shards(): weight_grad = signs_float * lax.all_gather(back, dp, axis=0, tiled=True)  31.7 us
    all_to_all x1, waiting for transfers between devices, shards(): groups = lax.all_to_all(rotated, dp, 0, 0, tiled=True)  27.2 us
    dot_general x1, matrix products, shards(): lax.dot_general(activations, cotangent, (((0,), (0,)), ((), ())), preferr...  10.4 us
    dot_general x1, matrix products, shards(): lax.dot_general(cotangent, lax.all_gather(value_weights, fsdp, axis=0, ti...  9.45 us
    all_to_all x1, starting transfers between devices, shards(): groups = lax.all_to_all(rotated, dp, 0, 0, tiled=True)  8.02 us
  transfers between devices with their start and end apart: 4, of which 4 were waited for; matrix products, arithmetic and copies ran while one was open for 7% of the time, Pallas kernels for 0%

profile of v1, /device:TPU:1, one launch (start us, length us, event | category | flops | bytes accessed | tf_op | source)
XLA Modules:
  0.0 266.3 jit_solution(2936329043911034289)
XLA Ops:
  7.2 0.0 copy-start
  7.2 0.0 reduce-scatter.2.cloned.1.call-start
  7.2 1.2 copy-done
  8.4 10.4 %fusion.38 = f32[4096,1024]{1,0:T(8,128)} fusion(bf16[512,4096]{1,0:T(8,128)(2,1)} %param.5, bf16[512,1024]{1,0:T(8,128)(2,1)S(1)} %copy-done), kind=kOutput, calls=%fused_computation.49 | convolution fusion | flops 4294967296 | bytes 22020096 | tf_op jit(solution)/shard_map/dot_general | solution.py:42
  18.8 0.0 copy-start.1
  18.8 0.0 reduce-scatter.2.cloned.1.call-update
  18.8 0.0 all-gather.3.cloned.1.call-start
  18.8 0.7 all-gather.3.cloned.1.call-update
  19.5 118.4 %reduce-scatter.2.cloned.1.call-done = f32[256,1024]{1,0:T(8,128)} async-done(((f32[4096,1024]{1,0:T(8,128)}), f32[256,1024]{1,0:T(8,128)}) %reduce-scatter.2.cloned.1.call-update) | async-done | bytes 1048592 | tf_op jit(solution)/shard_map/reduce_scatter | solution.py:41
  138.0 0.0 copy-done.1
  138.0 1.4 convert_multiply_fusion.1
  139.4 1.1 reshape.36
  140.5 2.2 fusion.4
  142.7 1.0 fusion
  143.8 1.1 div.41
  144.9 8.0 %all-to-all-start = ((f32[16,16,1024]{2,1,0:T(8,128)}), f32[16,16,1024]{2,1,0:T(8,128)S(1)}, u32[]{:S(2)}, u32[]{:S(2)}) async-start(f32[16,16,1024]{2,1,0:T(8,128)} %div.41), calls=%async_computation.1 | async-start | bytes 2097152 | tf_op jit(solution)/shard_map/all_to_all | solution.py:51
  152.9 0.0 all-gather.5.cloned.1.call-start
  153.6 27.2 %all-to-all-done = f32[16,16,1024]{2,1,0:T(8,128)S(1)} async-done(((f32[16,16,1024]{2,1,0:T(8,128)}), f32[16,16,1024]{2,1,0:T(8,128)S(1)}, u32[]{:S(2)}, u32[]{:S(2)}) %all-to-all-start) | async-done | bytes 1048608 | tf_op jit(solution)/shard_map/all_to_all | solution.py:51
  180.9 0.2 abs_reduce_fusion
  181.0 0.1 reduce_max.14
  181.1 0.1 reduce_max.18
  181.2 0.1 mul.43
  181.3 0.1 mul.44
  181.4 0.2 floor_reduce_fusion
  181.6 0.3 fusion.2
  181.9 0.2 fusion.1
  182.1 0.6 div.48
  182.8 0.0 all-gather.5.cloned.1.call-update
  182.8 33.4 %all-gather.3.cloned.1.call-done = bf16[4096,1024]{1,0:T(8,128)(2,1)} async-done(((bf16[256,1024]{1,0:T(8,128)(2,1)}), bf16[4096,1024]{1,0:T(8,128)(2,1)}) %all-gather.3.cloned.1.call-update) | async-done | bytes 8388624 | tf_op jit(solution)/shard_map/all_gather | solution.py:37
  216.2 9.5 %convolution_convert_fusion = bf16[512,4096]{1,0:T(8,128)(2,1)} fusion(bf16[512,1024]{1,0:T(8,128)(2,1)S(1)} %copy-done, bf16[4096,1024]{1,0:T(8,128)(2,1)} %all-gather.3.cloned.1.call-done), kind=kOutput, calls=%fused_computation | convolution fusion | flops 4297064448 | bytes 13631488 | tf_op jit(solution)/shard_map/dot_general | solution.py:35
  225.7 31.7 %all-gather.5.cloned.1.call-done = f32[256,1024]{1,0:T(8,128)} async-done(((f32[16,1024]{1,0:T(8,128)}), f32[256,1024]{1,0:T(8,128)}) %all-gather.5.cloned.1.call-update) | async-done | bytes 1048592 | tf_op jit(solution)/shard_map/all_gather | solution.py:59
  257.4 2.4 convert_multiply_fusion
  (2 shorter events, 0.0 us)
Async XLA Ops:
  7.2 1.2 copy-start
  7.2 130.8 %reduce-scatter.2.cloned.1.call-start = ((), (), s32[]{:S(2)}) async-start(), calls=%async_computation.3 | async-start | bytes 17825792 | tf_op jit(solution)/shard_map/reduce_scatter | solution.py:41
  18.8 119.2 %copy-start.1 = (s32[256,1024]{1,0:T(8,128)S(1)}, s32[256,1024]{1,0:T(8,128)}, u32[]{:S(2)}) copy-start(s32[256,1024]{1,0:T(8,128)} %param.8) | copy-start | bytes 3145732
  18.8 197.4 %all-gather.3.cloned.1.call-start = ((), (), s32[]{:S(2)}) async-start(), calls=%async_computation.2 | async-start | bytes 8912896 | tf_op jit(solution)/shard_map/all_gather | solution.py:37
  144.9 36.0 %all-to-all-start = ((f32[16,16,1024]{2,1,0:T(8,128)}), f32[16,16,1024]{2,1,0:T(8,128)S(1)}, u32[]{:S(2)}, u32[]{:S(2)}) async-start(f32[16,16,1024]{2,1,0:T(8,128)} %div.41), calls=%async_computation.1 | async-start | bytes 2097152 | tf_op jit(solution)/shard_map/all_to_all | solution.py:51
  152.9 104.5 %all-gather.5.cloned.1.call-start = ((), (), s32[]{:S(2)}) async-start(), calls=%async_computation.4 | async-start | bytes 1114112 | tf_op jit(solution)/shard_map/all_gather | solution.py:59
Sparse Core Ops, SparseCore 0:
  18.9 119.0 reduce-scatter.1
  140.4 75.7 all-gather.2
  218.6 38.7 all-gather.4

commit v2 on v1

v2 whole, which is shorter than its diff:
```python
import jax
import jax.numpy as jnp
import numpy as np
from jax import lax
from jax.experimental import pallas as pl
from jax.experimental.pallas import tpu as pltpu
from jax.sharding import Mesh, PartitionSpec as P

NZ, NC, NX, NY = 8, 2, 4, 4
AXES = ("z", "core", "x", "y")
KV = 1024
TOK = 512
F32, BF16, I16, I32 = jnp.float32, jnp.bfloat16, jnp.int16, jnp.int32
VMEM = 56 * 1024 * 1024


def hadamard(size):
    positions = np.arange(size)
    common = positions[:, None] & positions[None, :]
    parity = np.zeros((size, size), np.int64)
    for bit in range(16):
        parity += (common >> bit) & 1
    return (1 - 2 * (parity & 1)).astype(np.float32)


def power(e):
    return jnp.exp2(e * 0.125)


def step_of(top, low):
    return jnp.ceil(jnp.log2(jnp.maximum(top, low)) * 8.0)


def encode(v, ce):
    u = v if ce is None else v * power(-ce)
    e = step_of(jnp.max(jnp.abs(u), axis=1, keepdims=True), 1e-30) - 119.0
    q = jnp.floor(u * power(-e) + 0.5)
    return q.astype(I32).astype(I16), e


def to_float(q):
    return q.astype(I32).astype(F32)


def eye():
    return lax.broadcasted_iota(I32, (128, 128), 0) == lax.broadcasted_iota(I32, (128, 128), 1)


def to_lanes(col):
    return jnp.sum(jnp.where(eye(), col, 0.0), axis=0, keepdims=True)


def to_rows(row):
    return jnp.sum(jnp.where(eye(), row, 0.0), axis=1, keepdims=True)


def decode(q, row_e, ce_own, ce_oth):
    v = to_float(q) * power(to_rows(row_e))
    half = q.shape[0] // 2
    return v[:half] * power(ce_own), v[half:] * power(ce_oth)


def product(a, c):
    return lax.dot_general(a, c, (((0,), (0,)), ((), ())), preferred_element_type=F32)


def column_steps(c):
    top = jnp.max(jnp.abs(c.astype(F32)), axis=0, keepdims=True)
    return jnp.clip(step_of(top, 1e-30), -800.0, 800.0)


def far_kernel(idx, a_own, a_oth, c_own, c_oth, up, down, ce_ref, ex_up, ex_down):
    k = pl.program_id(0)

    @pl.when(k == 0)
    def _():
        ce_ref[...] = jnp.zeros_like(ce_ref)
        ce_ref[1:2, :] = column_steps(c_own[...])
        ce_ref[2:3, :] = column_steps(c_oth[...])
        ex_up[...] = ce_ref[...]
        ex_down[...] = ce_ref[...]

    rows = pl.ds(pl.multiple_of(k * 128, 128), 128)
    lanes = rows
    q0, e0 = encode(product(a_own[...], c_own[...]), ce_ref[1:2, :])
    q1, e1 = encode(product(a_oth[...], c_oth[...]), ce_ref[2:3, :])
    up[rows, :] = jnp.concatenate([q0[:64], q1[:64]], 0)
    down[rows, :] = jnp.concatenate([q0[64:], q1[64:]], 0)
    ex_up[0:1, lanes] = to_lanes(jnp.concatenate([e0[:64], e1[:64]], 0))
    ex_down[0:1, lanes] = to_lanes(jnp.concatenate([e0[64:], e1[64:]], 0))

    @pl.when(k == 3)
    def _():
        up[512:528, :] = ex_up[...].astype(I32).astype(I16)
        down[512:528, :] = ex_down[...].astype(I32).astype(I16)


def near_kernel(first, idx, a_own, a_oth, c_own, c_oth, ce, msg, keep, ex):
    k = pl.program_id(0)

    @pl.when(k == 0)
    def _():
        ex[...] = ce[...]

    rows = pl.ds(pl.multiple_of(k * 128, 128), 128)
    p0 = product(a_own[...], c_own[...])
    p1 = product(a_oth[...], c_oth[...])
    kept, sent = (slice(0, 64), slice(64, 128)) if first else (slice(64, 128), slice(0, 64))
    keep[...] = jnp.concatenate([p0[kept], p1[kept]], 0)
    q0, e0 = encode(p0[sent], ce[1:2, :])
    q1, e1 = encode(p1[sent], ce[2:3, :])
    msg[rows, :] = jnp.concatenate([q0, q1], 0)
    ex[0:1, rows] = to_lanes(jnp.concatenate([e0, e1], 0))

    @pl.when(k == 3)
    def _():
        msg[512:528, :] = ex[...].astype(I32).astype(I16)


def own_kernel(idx, a_own, a_oth, c_own, c_oth, keep):
    keep[0:128, :] = product(a_own[...], c_own[...])
    keep[128:256, :] = product(a_oth[...], c_oth[...])


def relay_kernel(keep, ce, q, q_ex, msg, ex):
    k = pl.program_id(0)
    rows = pl.ds(pl.multiple_of(k * 128, 128), 128)
    came = to_float(q_ex[...])

    @pl.when(k == 0)
    def _():
        ex[...] = jnp.maximum(ce[...], came)

    row_e = to_float(q_ex[:, rows])[0:1, :]
    d0, d1 = decode(q[...], row_e, came[1:2, :], came[2:3, :])
    q0, e0 = encode(keep[0:64, :] + d0, ex[1:2, :])
    q1, e1 = encode(keep[64:128, :] + d1, ex[2:3, :])
    msg[rows, :] = jnp.concatenate([q0, q1], 0)
    ex[0:1, rows] = to_lanes(jnp.concatenate([e0, e1], 0))

    @pl.when(k == 3)
    def _():
        msg[512:528, :] = ex[...].astype(I32).astype(I16)


def cross_kernel(keep, ce, ua, ua_ex, ub, ub_ex, da, da_ex, db, db_ex, own, n1, n2, n3, ex):
    k = pl.program_id(0)
    lanes = pl.ds(pl.multiple_of(k * 128, 128), 128)
    steps = [to_float(r[...]) for r in (ua_ex, ub_ex, da_ex, db_ex)]

    def get(q, q_ex, came):
        return decode(q[...], to_float(q_ex[:, lanes])[0:1, :], came[1:2, :], came[2:3, :])

    ua0, ua1 = get(ua, ua_ex, steps[0])
    ub0, ub1 = get(ub, ub_ex, steps[1])
    da0, da1 = get(da, da_ex, steps[2])
    db0, db1 = get(db, db_ex, steps[3])
    s0 = keep[0:128, :] + jnp.concatenate([ua0 + da0, ub0 + db0], 0)
    s1 = keep[128:256, :] + jnp.concatenate([ua1 + da1, ub1 + db1], 0)

    @pl.when(k == 0)
    def _():
        own[0:128, :] = s0
        own[128:256, :] = s1

    for number, msg in ((1, n1), (2, n2), (3, n3)):

        @pl.when(k == number)
        def _(msg=msg):
            ex[...] = jnp.maximum(jnp.maximum(ce[...], steps[0]), jnp.maximum(steps[1], jnp.maximum(steps[2], steps[3])))
            q0, e0 = encode(s0, ex[1:2, :])
            q1, e1 = encode(s1, ex[2:3, :])
            msg[0:128, :] = q0
            msg[128:256, :] = q1
            ex[0:1, 0:128] = to_lanes(e0)
            ex[0:1, 128:256] = to_lanes(e1)
            msg[256:272, :] = ex[...].astype(I32).astype(I16)


def split_dot(x, m):
    hi = x.astype(BF16)
    rest = x - hi.astype(F32)
    mid = rest.astype(BF16)
    lo = (rest - mid.astype(F32)).astype(BF16)
    dot = lambda a: jnp.dot(a, m, preferred_element_type=F32)
    return dot(hi) + (dot(mid) + dot(lo))


def split_dot_left(m, x):
    hi = x.astype(BF16)
    rest = x - hi.astype(F32)
    mid = rest.astype(BF16)
    lo = (rest - mid.astype(F32)).astype(BF16)
    dot = lambda a: jnp.dot(m, a, preferred_element_type=F32)
    return dot(hi) + (dot(mid) + dot(lo))


def rotate(v, inner, rows):
    tiles = [v[:, k * 128 : (k + 1) * 128] for k in range(8)]
    for bit in (1, 2, 4):
        tiles = [tiles[k ^ bit] - tiles[k] if k & bit else tiles[k] + tiles[k ^ bit] for k in range(8)]
    mixed = jnp.concatenate([split_dot(t, inner) for t in tiles], 1)
    return split_dot_left(rows, mixed) * (1.0 / 64.0)


def rotate_kernel(core, own, signs, n1, n2, n3, inner, rows, out):
    total = [own[0:128, :], own[128:256, :]]
    for msg in (n1, n2, n3):
        extra = to_float(msg[256:272, :])
        for g in (0, 1):
            e = to_rows(extra[0:1, g * 128 : (g + 1) * 128])
            total[g] += to_float(msg[g * 128 : (g + 1) * 128, :]) * power(e) * power(extra[1 + g : 2 + g, :])
    flips = signs[...].astype(F32)
    for g in (0, 1):
        q, e = encode(rotate(total[g] * flips, inner[...], rows[...]), None)
        wide = jnp.broadcast_to(e, (128, 128)).astype(I32).astype(I16)
        for z in range(NZ):
            out[z * 32 + g * 16 : z * 32 + g * 16 + 16, 0:KV] = q[z * 16 : z * 16 + 16]
            out[z * 32 + g * 16 : z * 32 + g * 16 + 16, KV : KV + 128] = wide[z * 16 : z * 16 + 16]


def levels_kernel(count, x, inner, rows, out):
    level = count[0].astype(F32)

    def group(g):
        q = x[g * 16 : g * 16 + 16, :]
        e = to_float(q[:, KV : KV + 128])[:, 0:1]
        return to_float(q[:, 0:KV]) * power(e)

    groups = [group(g) for g in range(NZ * NC)]
    top = jnp.abs(groups[0])
    for v in groups[1:]:
        top = jnp.maximum(top, jnp.abs(v))
    top = jnp.max(top, axis=1, keepdims=True)
    block = lax.shift_right_logical(lax.broadcasted_iota(I32, (16, 1), 0), 2)
    peak = jnp.zeros((16, 1), F32)
    for b in range(4):
        peak = jnp.where(block == b, jnp.max(jnp.where(block == b, top, 0.0), axis=0, keepdims=True), peak)
    peak = peak + 1e-06
    scale = level / peak
    total = jnp.floor(groups[0] * scale + 0.5)
    for v in groups[1:]:
        total = total + jnp.floor(v * scale + 0.5)
    q, e = encode(rotate(total * (peak / level), inner[...], rows[...]), None)
    out[:, 0:KV] = q
    out[:, KV : KV + 128] = jnp.broadcast_to(e, (16, 128)).astype(I32).astype(I16)


def finish_kernel(q, signs, out):
    for z in range(NZ):
        for c in range(NC):
            came = q[(z * NC + c) * 16 : (z * NC + c) * 16 + 16, :]
            rows = slice(c * 128 + z * 16, c * 128 + z * 16 + 16)
            e = to_float(came[:, KV : KV + 128])[:, 0:1]
            out[rows, :] = signs[rows, :].astype(F32) * (to_float(came[:, 0:KV]) * power(e))


def input_grad_kernel(core, c, w_own, w_oth, out):
    def part(w):
        return lax.dot_general(c[...], w[...], (((1,), (1,)), ((), ())), preferred_element_type=F32).astype(BF16)

    here = pl.multiple_of(core[0] * 128, 128)
    there = pl.multiple_of(128 - core[0] * 128, 128)
    out[:, pl.ds(here, 128)] = part(w_own)
    out[:, pl.ds(there, 128)] = part(w_oth)


def pick_kernel(core, a, out, sems):
    copies = []
    for k in range(NX * NY):
        start = pl.multiple_of(k * 256 + 128 - core[0] * 128, 128)
        copies.append(pltpu.make_async_copy(a.at[:, pl.ds(start, 128)], out.at[:, k * 128 : (k + 1) * 128], sems.at[k]))
    for copy in copies:
        copy.start()
    for copy in copies:
        copy.wait()


def tie_kernel(w, after, out):
    del w, after, out


def params():
    return pltpu.CompilerParams(vmem_limit_bytes=VMEM)


def cost(flops, moved):
    return pl.CostEstimate(flops=int(flops), bytes_accessed=int(moved), transcendentals=0)


def whole(shape):
    return pl.BlockSpec(shape, lambda *_: (0,) * len(shape))


def shift(s, first):
    pairs = []
    for z in range(NZ):
        for c in range(NC):
            for x in range(NX):
                for y in range(NY):
                    along_x = (c == 0) == first
                    tx, ty = ((x + s) % NX, y) if along_x else (x, (y + s) % NY)
                    pairs.append((((z * NC + c) * NX + x) * NY + y, ((z * NC + c) * NX + tx) * NY + ty))
    return pairs


def shards(activations, cotangent, value_weights, sign_flips, level_count):
    core = lax.axis_index("core").astype(I32)
    x, y = lax.axis_index("x").astype(I32), lax.axis_index("y").astype(I32)
    core1 = core.reshape(1)
    swap = lambda v: lax.ppermute(v, "core", [(0, 1), (1, 0)])
    send = lambda v, s, first: lax.ppermute(v, AXES, shift(s, first))
    sds = jax.ShapeDtypeStruct

    picked = pl.pallas_call(
        pick_kernel,
        out_shape=sds((TOK, 2048), BF16),
        grid_spec=pltpu.PrefetchScalarGridSpec(
            num_scalar_prefetch=1,
            grid=(1,),
            in_specs=[pl.BlockSpec(memory_space=pl.ANY)],
            out_specs=pl.BlockSpec(memory_space=pl.ANY),
            scratch_shapes=[pltpu.SemaphoreType.DMA((NX * NY,))],
        ),
        compiler_params=params(),
        cost_estimate=cost(0, 4 << 20),
        name="pick",
    )(core1, activations)
    a_oth = swap(picked)
    c_oth = swap(cotangent)

    half_w = lax.dynamic_slice_in_dim(value_weights, core * 128, 128, 0)
    w_own = lax.all_gather(half_w, ("x", "y"), axis=0, tiled=True)

    def indices(dp):
        ids = []
        for dq in range(4):
            tx = jnp.where(core == 0, (x + dp) % NX, (x + dq) % NX)
            ty = jnp.where(core == 0, (y + dq) % NY, (y + dp) % NY)
            ids.append(tx * NY + ty)
        return jnp.stack(ids + [core]).astype(I32)

    operands = [
        pl.BlockSpec((TOK, 128), lambda k, idx: (0, 2 * idx[k] + idx[4])),
        pl.BlockSpec((TOK, 128), lambda k, idx: (0, idx[k])),
        whole((TOK, KV)),
        whole((TOK, KV)),
    ]
    inputs = (activations, a_oth, cotangent, c_oth)
    message = sds((528, KV), I16)
    extra = pltpu.VMEM((16, KV), F32)
    mm = 2 * 1024 * 1024 * 512

    up1, down1, ce = pl.pallas_call(
        far_kernel,
        out_shape=(message, message, sds((16, KV), F32)),
        grid_spec=pltpu.PrefetchScalarGridSpec(
            num_scalar_prefetch=1,
            grid=(4,),
            in_specs=operands,
            out_specs=(whole((528, KV)), whole((528, KV)), whole((16, KV))),
            scratch_shapes=[extra, extra],
        ),
        compiler_params=params(),
        cost_estimate=cost(mm, 6 << 20),
        name="far",
    )(indices(2), *inputs)
    got_up1 = send(up1, 1, True)
    got_down1 = send(down1, -1, True)

    def near(dp, first):
        return pl.pallas_call(
            lambda *refs: near_kernel(first, *refs),
            out_shape=(message, sds((512, KV), F32)),
            grid_spec=pltpu.PrefetchScalarGridSpec(
                num_scalar_prefetch=1,
                grid=(4,),
                in_specs=operands + [whole((16, KV))],
                out_specs=(whole((528, KV)), pl.BlockSpec((128, KV), lambda k, idx: (k, 0))),
                scratch_shapes=[extra],
            ),
            compiler_params=params(),
            cost_estimate=cost(mm, 7 << 20),
            name="near",
        )(indices(dp), *inputs, ce)

    up2, keep_up = near(1, True)
    down2, keep_down = near(-1, False)
    got_up2 = send(up2, 1, True)
    got_down2 = send(down2, -1, True)

    keep = pl.pallas_call(
        own_kernel,
        out_shape=sds((1024, KV), F32),
        grid_spec=pltpu.PrefetchScalarGridSpec(
            num_scalar_prefetch=1,
            grid=(4,),
            in_specs=operands,
            out_specs=pl.BlockSpec((256, KV), lambda k, idx: (k, 0)),
        ),
        compiler_params=params(),
        cost_estimate=cost(mm, 8 << 20),
        name="own",
    )(indices(0), *inputs)

    codes = [pl.BlockSpec((128, KV), lambda k: (k, 0)), pl.BlockSpec((16, KV), lambda k: (32, 0))]

    def relay(kept, got):
        return pl.pallas_call(
            relay_kernel,
            out_shape=message,
            grid=(4,),
            in_specs=[pl.BlockSpec((128, KV), lambda k: (k, 0)), whole((16, KV))] + codes,
            out_specs=whole((528, KV)),
            scratch_shapes=[extra],
            compiler_params=params(),
            cost_estimate=cost(1 << 20, 4 << 20),
            name="relay",
        )(kept, ce, got, got)

    got_up3 = send(relay(keep_up, got_up1), 1, True)
    got_down3 = send(relay(keep_down, got_down1), -1, True)

    short = sds((272, KV), I16)
    own, n1, n2, n3 = pl.pallas_call(
        cross_kernel,
        out_shape=(sds((256, KV), F32), short, short, short),
        grid=(4,),
        in_specs=[pl.BlockSpec((256, KV), lambda k: (k, 0)), whole((16, KV))] + codes * 4,
        out_specs=(whole((256, KV)), whole((272, KV)), whole((272, KV)), whole((272, KV))),
        scratch_shapes=[extra],
        compiler_params=params(),
        cost_estimate=cost(1 << 20, 10 << 20),
        name="cross",
    )(keep, ce, got_up3, got_up3, got_up2, got_up2, got_down2, got_down2, got_down3, got_down3)
    g1 = send(n1, 1, False)
    g3 = send(n3, -1, False)
    g2 = send(n2, 2, False)

    w_own = pl.pallas_call(
        tie_kernel,
        out_shape=sds((2048, KV), BF16),
        in_specs=[pl.BlockSpec(memory_space=pl.ANY)] * 2,
        out_specs=pl.BlockSpec(memory_space=pl.ANY),
        input_output_aliases={0: 0},
        name="tie",
    )(w_own, n1)
    w_oth = swap(w_own)

    inner = jnp.asarray(hadamard(128), BF16)
    quad = hadamard(4)
    spun = pl.pallas_call(
        rotate_kernel,
        out_shape=sds((256, KV + 128), I16),
        grid_spec=pltpu.PrefetchScalarGridSpec(
            num_scalar_prefetch=1,
            grid=(1,),
            in_specs=[
                whole((256, KV)),
                pl.BlockSpec((128, KV), lambda k, c: (c[0], 0)),
                whole((272, KV)),
                whole((272, KV)),
                whole((272, KV)),
                whole((128, 128)),
                whole((128, 128)),
            ],
            out_specs=whole((256, KV + 128)),
        ),
        compiler_params=params(),
        cost_estimate=cost(1 << 28, 4 << 20),
        name="rotate",
    )(core1, own, sign_flips, g1, g2, g3, inner, jnp.asarray(np.kron(np.eye(32), quad), BF16))
    groups = lax.all_to_all(spun, "z", 0, 0, tiled=True)

    back = pl.pallas_call(
        levels_kernel,
        out_shape=sds((16, KV + 128), I16),
        in_specs=[pl.BlockSpec(memory_space=pltpu.SMEM)] + [pl.BlockSpec(memory_space=pltpu.VMEM)] * 3,
        out_specs=pl.BlockSpec(memory_space=pltpu.VMEM),
        compiler_params=params(),
        cost_estimate=cost(1 << 26, 1 << 20),
        name="levels",
    )(level_count.reshape(1), groups, inner, jnp.asarray(np.kron(np.eye(4), quad), BF16))
    gathered = lax.all_gather(back, ("z", "core"), axis=0, tiled=True)
    weight_grad = pl.pallas_call(
        finish_kernel,
        out_shape=sds((256, KV), F32),
        in_specs=[pl.BlockSpec(memory_space=pltpu.VMEM)] * 2,
        out_specs=pl.BlockSpec(memory_space=pltpu.VMEM),
        compiler_params=params(),
        cost_estimate=cost(1 << 20, 3 << 20),
        name="finish",
    )(gathered, sign_flips)

    input_grad = pl.pallas_call(
        input_grad_kernel,
        out_shape=sds((TOK, 4096), BF16),
        grid_spec=pltpu.PrefetchScalarGridSpec(
            num_scalar_prefetch=1,
            grid=(16,),
            in_specs=[
                whole((TOK, KV)),
                pl.BlockSpec((128, KV), lambda k, c: (k, 0)),
                pl.BlockSpec((128, KV), lambda k, c: (k, 0)),
            ],
            out_specs=pl.BlockSpec((TOK, 256), lambda k, c: (0, k)),
        ),
        compiler_params=params(),
        cost_estimate=cost(4 * mm, 13 << 20),
        name="input_grad",
    )(core1, cotangent, w_own, w_oth)
    return (input_grad, weight_grad)


def solution(mesh):
    torus = Mesh(mesh.devices.reshape(NZ, NC, NX, NY), AXES)
    rows = P(AXES, None)
    part = P(("x", "y"), None)
    return jax.shard_map(
        shards,
        mesh=torus,
        in_specs=(rows, rows, part, part, P()),
        out_specs=(rows, part),
        check_vma=False,
    )
```

time: 267 us -> 246 us (0.921)
  waiting for transfers between devices: 212 us -> 43.2 us
  Pallas kernels: 0 us -> 135 us
  matrix products: 23.5 us -> 0 us
  blocking collectives: 0 us -> 21 us
  starting transfers between devices: 8.14 us -> 22.9 us
  other arithmetic: 4.3 us -> 0 us
  local copies, waits for them, and re-layouts: 4.35 us -> 7.35 us
    pallas_call x0 -> x13, Pallas kernels: none -> 135 us  [the longest x1 64.8 us: shards(): pl.pallas_call(pick_kernel, out_shape=sds((TOK, 2048), BF16), grid_spec=p...]
    reduce_scatter x1 -> x0, waiting for transfers between devices: 118 us -> none  [shards(): lax.psum_scatter(lax.dot_general(activations, cotangent, (((0,), (0,)), (...]
    all_gather x2 -> x1, waiting for transfers between devices: 65.1 us -> 0.01 us  [shards(): w_own = lax.all_gather(half_w, ('x', 'y'), axis=0, tiled=True)]
    ppermute x0 -> x12, waiting for transfers between devices: none -> 27.3 us  [the longest x9 22.6 us: shards(): send = lambda v, s, first: lax.ppermute(v, AXES, shift(s, first))]
    dot_general x6 -> x0, matrix products: 23.5 us -> none  [the longest x1 10.4 us: shards(): lax.dot_general(activations, cotangent, (((0,), (0,)), ((), ())), preferr...]
    all_gather x0 -> x1, blocking collectives: none -> 21 us  [shards(): gathered = lax.all_gather(back, ('z', 'core'), axis=0, tiled=True)]
    ppermute x0 -> x12, starting transfers between devices: none -> 14.7 us  [the longest x9 8.81 us: shards(): send = lambda v, s, first: lax.ppermute(v, AXES, shift(s, first))]
    all_to_all x1, waiting for transfers between devices: 27.2 us -> 15.9 us  [shards(): groups = lax.all_to_all(spun, 'z', 0, 0, tiled=True)]
  transfers between devices with their start and end apart: 4 -> 14, of which waited for: 4 -> 7; matrix products, arithmetic and copies ran while one was open for 7% -> 1% of each run, Pallas kernels for 0% -> 48%
where the time goes in v2:
time: 246 us; the launch traced here: 245 us
  Pallas kernels  135 us (55%)
  waiting for transfers between devices  43.2 us (18%)
  starting transfers between devices  22.9 us (9%)
  blocking collectives  21 us (9%)
  between operations  14.8 us (6%)
  local copies, waits for them, and re-layouts  7.35 us (3%)
    pallas_call x1, Pallas kernels, shards(): pl.pallas_call(pick_kernel, out_shape=sds((TOK, 2048), BF16), grid_spec=p...  64.8 us
    ppermute x9, waiting for transfers between devices, shards(): send = lambda v, s, first: lax.ppermute(v, AXES, shift(s, first))  22.6 us
    all_gather x1, blocking collectives, shards(): gathered = lax.all_gather(back, ('z', 'core'), axis=0, tiled=True)  21 us
    pallas_call x1, Pallas kernels, shards(): pl.pallas_call(input_grad_kernel, out_shape=sds((TOK, 4096), BF16), grid_...  16.9 us
    all_to_all x1, waiting for transfers between devices, shards(): groups = lax.all_to_all(spun, 'z', 0, 0, tiled=True)  15.9 us
    pallas_call x2, Pallas kernels, near(): pl.pallas_call(lambda *refs: near_kernel(first, *refs), out_shape=(messag...  13.6 us
    pallas_call x2, Pallas kernels, relay(): pl.pallas_call(relay_kernel, out_shape=message, grid=(4,), in_specs=[pl.B...  9.06 us
    ppermute x9, starting transfers between devices, shards(): send = lambda v, s, first: lax.ppermute(v, AXES, shift(s, first))  8.81 us
  transfers between devices with their start and end apart: 14, of which 7 were waited for; matrix products, arithmetic and copies ran while one was open for 1% of the time, Pallas kernels for 48%

profile of v2, /device:TPU:1, one launch (start us, length us, event | category | flops | bytes accessed | tf_op | source)
XLA Modules:
  0.0 244.5 jit_solution(9534498744961807227)
XLA Ops:
  7.2 0.0 copy-start
  7.2 0.0 all-gather.2.cloned.1.call-start
  7.2 1.0 copy-done
  8.2 0.7 constant_dynamic-slice_fusion
  8.9 0.0 all-gather.2.cloned.1.call-update
  9.0 64.8 %pick.1 = bf16[512,2048]{1,0:T(8,128)(2,1)} custom-call(s32[1]{0:T(128)} %bitcast.core, bf16[512,4096]{1,0:T(8,128)(2,1)} %refs_1_.3), custom_call_target="tpu_custom_call" | custom-call | bytes 4194304 | tf_op jit(solution)/shard_map/pick/pallas_call | solution.py:315
  73.7 3.3 %collective-permute-start = (bf16[512,2048]{1,0:T(8,128)(2,1)}, bf16[512,2048]{1,0:T(8,128)(2,1)S(1)}, u32[]{:S(2)}, u32[]{:S(2)}) collective-permute-start(bf16[512,2048]{1,0:T(8,128)(2,1)} %pick.1), channel_id=1, source_target_pairs={{0,16},{16,0},{1,17},{17,1},{2,18},{18,2},{3,19},{19,3},{4,20},{20... | collective-permute-start | bytes 6291464 | tf_op jit(solution)/shard_map/ppermute | solution.py:311
  77.1 0.1 collective-permute-start.1
  77.2 0.7 stack.73.idx
  77.8 4.7 %collective-permute-done.1.c_oth.refs_4_ = bf16[512,1024]{1,0:T(8,128)(2,1)} collective-permute-done((bf16[512,1024]{1,0:T(8,128)(2,1)}, bf16[512,1024]{1,0:T(8,128)(2,1)}, u32[]{:S(2)}, u32[]{:S(2)}) %collective-permute-start.1) | collective-permute-done | bytes 1048608 | tf_op jit(solution)/shard_map/ppermute | solution.py:311
  82.6 0.0 collective-permute-done.a_oth.refs_2_
  82.6 0.0 copy-start.1
  82.6 1.4 copy-done.1
  83.9 7.5 %far.1 = (s16[528,1024]{1,0:T(8,128)(2,1)}, s16[528,1024]{1,0:T(8,128)(2,1)}, f32[16,1024]{1,0:T(8,128)}) custom-call(s32[5]{0:T(128)} %stack.73.idx, bf16[512,4096]{1,0:T(8,128)(2,1)} %refs_1_.3, bf16[512,2048]{1,0:T(8,128)(2,1)} %copy-done.1, bf16[512,1024]{1,0:T(8,128)(2,1)} %c.1, bf16[512,1024]{1,0:T(8,128)(2,1)} %collective-permute-done.1.c_oth.refs_4_), custom_call_target="tpu_custom_call" | custom-call | flops 1073741824 | bytes 6291456 | tf_op jit(solution)/shard_map/far/pallas_call | solution.py:354
  91.4 1.0 collective-permute-start.6
  92.4 0.5 collective-permute-start.2
  92.9 0.6 stack.83.refs_0_
  93.5 0.7 stack.78.refs_0_
  94.1 6.8 %near.3 = (s16[528,1024]{1,0:T(8,128)(2,1)}, f32[512,1024]{1,0:T(8,128)}) custom-call(s32[5]{0:T(128)} %stack.83.refs_0_, bf16[512,4096]{1,0:T(8,128)(2,1)} %refs_1_.3, bf16[512,2048]{1,0:T(8,128)(2,1)} %copy-done.1, bf16[512,1024]{1,0:T(8,128)(2,1)} %c.1, bf16[512,1024]{1,0:T(8,128)(2,1)} %collective-permute-done.1.c_oth.refs_4_, ...), custom_call_target="tpu_custom_call" | custom-call | flops 1073741824 | bytes 7340032 | tf_op jit(solution)/shard_map/near/pallas_call | solution.py:372
  100.9 2.2 collective-permute-start.5
  103.1 6.8 %near.2 = (s16[528,1024]{1,0:T(8,128)(2,1)}, f32[512,1024]{1,0:T(8,128)}) custom-call(s32[5]{0:T(128)} %stack.78.refs_0_, bf16[512,4096]{1,0:T(8,128)(2,1)} %refs_1_.3, bf16[512,2048]{1,0:T(8,128)(2,1)} %copy-done.1, bf16[512,1024]{1,0:T(8,128)(2,1)} %c.1, bf16[512,1024]{1,0:T(8,128)(2,1)} %collective-permute-done.1.c_oth.refs_4_, ...), custom_call_target="tpu_custom_call" | custom-call | flops 1073741824 | bytes 7340032 | tf_op jit(solution)/shard_map/near/pallas_call | solution.py:372
  109.9 0.0 collective-permute-start.4
  109.9 0.0 collective-permute-done.6.q.q_ex
  110.0 4.5 %relay.3 = s16[528,1024]{1,0:T(8,128)(2,1)} custom-call(f32[512,1024]{1,0:T(8,128)} %get-tuple-element.18.keep, f32[16,1024]{1,0:T(8,128)} %get-tuple-element.13.refs_5_.ce, s16[528,1024]{1,0:T(8,128)(2,1)} %collective-permute-done.6.q.q_ex, s16[528,1024]{1,0:T(8,128)(2,1)} %collective-permute-done.6.q.q_ex), custom_call_target="tpu_custom_call" | custom-call | flops 1048576 | bytes 4194304 | tf_op jit(solution)/shard_map/relay/pallas_call | solution.py:409
  114.5 2.7 %collective-permute-start.7 = (s16[528,1024]{1,0:T(8,128)(2,1)}, s16[528,1024]{1,0:T(8,128)(2,1)}, u32[]{:S(2)}, u32[]{:S(2)}) collective-permute-start(s16[528,1024]{1,0:T(8,128)(2,1)} %relay.3), channel_id=1, source_target_pairs={{0,12},{1,13},{2,14},{3,15},{4,0},{5,1},{6,2},{7,3},{8,4},{9,5},{1... | collective-permute-start | bytes 3244040 | tf_op jit(solution)/shard_map/ppermute | solution.py:312
  117.1 0.0 collective-permute-done.2.q.q_ex
  117.1 4.5 %relay.2 = s16[528,1024]{1,0:T(8,128)(2,1)} custom-call(f32[512,1024]{1,0:T(8,128)} %get-tuple-element.14.keep, f32[16,1024]{1,0:T(8,128)} %get-tuple-element.13.refs_5_.ce, s16[528,1024]{1,0:T(8,128)(2,1)} %collective-permute-done.2.q.q_ex, s16[528,1024]{1,0:T(8,128)(2,1)} %collective-permute-done.2.q.q_ex), custom_call_target="tpu_custom_call" | custom-call | flops 1048576 | bytes 4194304 | tf_op jit(solution)/shard_map/relay/pallas_call | solution.py:409
  121.7 0.0 collective-permute-start.3
  121.7 0.6 stack.68.idx
  122.3 6.3 %own.1.keep = f32[1024,1024]{1,0:T(8,128)} custom-call(s32[5]{0:T(128)} %stack.68.idx, bf16[512,4096]{1,0:T(8,128)(2,1)} %refs_1_.3, bf16[512,2048]{1,0:T(8,128)(2,1)} %copy-done.1, bf16[512,1024]{1,0:T(8,128)(2,1)} %c.1, bf16[512,1024]{1,0:T(8,128)(2,1)} %collective-permute-done.1.c_oth.refs_4_), custom_call_target="tpu_custom_call" | custom-call | flops 1073741824 | bytes 8388608 | tf_op jit(solution)/shard_map/own/pallas_call | solution.py:392
  128.6 0.0 collective-permute-done.5.da.da_ex
  128.6 0.0 copy-start.2
  128.6 0.0 collective-permute-done.4.ub.ub_ex
  128.6 0.0 copy-start.3
  128.6 0.9 collective-permute-done.7.db.db_ex
  129.5 8.0 %collective-permute-done.3.ua.ua_ex = s16[528,1024]{1,0:T(8,128)(2,1)} collective-permute-done((s16[528,1024]{1,0:T(8,128)(2,1)}, s16[528,1024]{1,0:T(8,128)(2,1)}, u32[]{:S(2)}, u32[]{:S(2)}) %collective-permute-start.3) | collective-permute-done | bytes 1081376 | tf_op jit(solution)/shard_map/ppermute | solution.py:312
  137.5 0.0 copy-done.2
  137.5 0.0 copy-done.3
  137.5 7.1 %cross.1 = (f32[256,1024]{1,0:T(8,128)}, s16[272,1024]{1,0:T(8,128)(2,1)}, s16[272,1024]{1,0:T(8,128)(2,1)}, s16[272,1024]{1,0:T(8,128)(2,1)}) custom-call(f32[1024,1024]{1,0:T(8,128)} %own.1.keep, f32[16,1024]{1,0:T(8,128)} %get-tuple-element.13.refs_5_.ce, s16[528,1024]{1,0:T(8,128)(2,1)} %collective-permute-done.3.ua.ua_ex, ...), custom_call_target="tpu_custom_call" | custom-call | flops 1048576 | bytes 10485760 | tf_op jit(solution)/shard_map/cross/pallas_call | solution.py:425
  144.6 0.0 all-gather.2.cloned.1.call-done.w
  144.6 0.0 copy-start.9
  144.6 0.0 copy-start.5
  144.6 2.5 %collective-permute-start.8 = (bf16[2048,1024]{1,0:T(8,128)(2,1)}, bf16[2048,1024]{1,0:T(8,128)(2,1)}, u32[]{:S(2)}, u32[]{:S(2)}) collective-permute-start(bf16[2048,1024]{1,0:T(8,128)(2,1)} %tie.1.w_own), channel_id=1, source_target_pairs={{0,16},{16,0},{1,17},{17,1},{2,18},{18,2},{3,19},{19,3},{4,20},{20... | collective-permute-start | bytes 12582920 | tf_op jit(solution)/shard_map/ppermute | solution.py:311
  147.1 0.0 copy-done.10
  147.1 1.0 collective-permute-start.10
  148.1 0.0 copy-done.9
  148.1 0.9 collective-permute-start.11
  148.9 0.0 copy-done.5
  148.9 0.6 collective-permute-start.9
  149.5 7.7 %collective-permute-done.10.n2 = s16[272,1024]{1,0:T(8,128)(2,1)S(1)} collective-permute-done((s16[272,1024]{1,0:T(8,128)(2,1)S(1)}, s16[272,1024]{1,0:T(8,128)(2,1)S(1)}, u32[]{:S(2)}, u32[]{:S(2)}) %collective-permute-start.10) | collective-permute-done | bytes 557088 | tf_op jit(solution)/shard_map/ppermute | solution.py:312
  157.3 4.3 %collective-permute-done.11.n3 = s16[272,1024]{1,0:T(8,128)(2,1)S(1)} collective-permute-done((s16[272,1024]{1,0:T(8,128)(2,1)S(1)}, s16[272,1024]{1,0:T(8,128)(2,1)S(1)}, u32[]{:S(2)}, u32[]{:S(2)}) %collective-permute-start.11) | collective-permute-done | bytes 557088 | tf_op jit(solution)/shard_map/ppermute | solution.py:312
  161.6 1.6 collective-permute-done.9.n1
  163.2 0.0 copy-done.6
  163.2 0.0 copy-done.7
  163.2 0.9 copy-done.8
  164.1 4.8 %rotate.1 = s16[256,1152]{1,0:T(8,128)(2,1)} custom-call(s32[1]{0:T(128)} %bitcast.core, f32[256,1024]{1,0:T(8,128)} %get-tuple-element.21.own, s32[256,1024]{1,0:T(8,128)} %signs.3, s16[272,1024]{1,0:T(8,128)(2,1)} %copy-done.8, s16[272,1024]{1,0:T(8,128)(2,1)} %copy-done.6, s16[272,1024]{1,0:T(8,128)(2,1)} %copy-done.7, ...), custom_call_target="tpu_custom_call" | custom-call | flops 268435456 | bytes 4194304 | tf_op jit(solution)/shard_map/rotate/pallas_call | solution.py:452
  168.9 8.2 %all-to-all-start = ((s16[8,32,1152]{2,1,0:T(8,128)(2,1)}), s16[8,32,1152]{2,1,0:T(8,128)(2,1)S(1)}, u32[]{:S(2)}, u32[]{:S(2)}) async-start(s16[8,32,1152]{2,1,0:T(8,128)(2,1)} %bitcast.21), calls=%async_computation | async-start | bytes 1179648 | tf_op jit(solution)/shard_map/all_to_all | solution.py:473
  177.7 15.9 %all-to-all-done = s16[8,32,1152]{2,1,0:T(8,128)(2,1)S(1)} async-done(((s16[8,32,1152]{2,1,0:T(8,128)(2,1)}), s16[8,32,1152]{2,1,0:T(8,128)(2,1)S(1)}, u32[]{:S(2)}, u32[]{:S(2)}) %all-to-all-start) | async-done | bytes 589856 | tf_op jit(solution)/shard_map/all_to_all | solution.py:473
  193.6 0.8 copy-done.4
  194.4 2.7 %levels.1 = s16[16,1152]{1,0:T(8,128)(2,1)} custom-call(s32[1]{0:T(128)} %bitcast.20.count, s16[256,1152]{1,0:T(8,128)(2,1)} %bitcast.22, bf16[128,128]{1,0:T(8,128)(2,1)} %constant.188.clone.inner, bf16[16,16]{1,0:T(8,128)(2,1)} %constant.190.clone.rows), custom_call_target="tpu_custom_call" | custom-call | flops 67108864 | bytes 1048576 | tf_op jit(solution)/shard_map/levels/pallas_call | solution.py:475
  197.1 21.0 %all_gather.7.q = s16[256,1152]{1,0:T(8,128)(2,1)} all-gather(s16[16,1152]{1,0:T(8,128)(2,1)} %levels.1), channel_id=1, replica_groups=mesh['z'=8,'core'=2,'x'=4,'y'=4] {'z','core'}, dimensions={0}, use_global_device_ids=true | all-gather | bytes 626688 | tf_op jit(solution)/shard_map/all_gather | solution.py:484
  218.2 2.6 %finish.1 = f32[256,1024]{1,0:T(8,128)} custom-call(s16[256,1152]{1,0:T(8,128)(2,1)} %all_gather.7.q, s32[256,1024]{1,0:T(8,128)} %signs.3), custom_call_target="tpu_custom_call" | custom-call | flops 1048576 | bytes 3145728 | tf_op jit(solution)/shard_map/finish/pallas_call | solution.py:485
  220.8 0.0 collective-permute-done.8.w_oth
  220.8 16.9 %input_grad.1 = bf16[512,4096]{1,0:T(8,128)(2,1)} custom-call(s32[1]{0:T(128)} %bitcast.core, bf16[512,1024]{1,0:T(8,128)(2,1)} %c.1, bf16[2048,1024]{1,0:T(8,128)(2,1)} %tie.1.w_own, bf16[2048,1024]{1,0:T(8,128)(2,1)} %collective-permute-done.8.w_oth), custom_call_target="tpu_custom_call" | custom-call | flops 4294967296 | bytes 13631488 | tf_op jit(solution)/shard_map/input_grad/pallas_call | solution.py:495
  (6 shorter events, 0.0 us)
Async XLA Ops:
  7.2 1.0 copy-start
  7.2 137.4 %all-gather.2.cloned.1.call-start = ((), (), s32[]{:S(2)}) async-start(), calls=%async_computation.1 | async-start | bytes 4456448 | tf_op jit(solution)/shard_map/all_gather | solution.py:333
  73.7 8.8 %collective-permute-start = (bf16[512,2048]{1,0:T(8,128)(2,1)}, bf16[512,2048]{1,0:T(8,128)(2,1)S(1)}, u32[]{:S(2)}, u32[]{:S(2)}) collective-permute-start(bf16[512,2048]{1,0:T(8,128)(2,1)} %pick.1), channel_id=1, source_target_pairs={{0,16},{16,0},{1,17},{17,1},{2,18},{18,2},{3,19},{19,3},{4,20},{20... | collective-permute-start | bytes 6291464 | tf_op jit(solution)/shard_map/ppermute | solution.py:311
  77.1 5.5 %collective-permute-start.1 = (bf16[512,1024]{1,0:T(8,128)(2,1)}, bf16[512,1024]{1,0:T(8,128)(2,1)}, u32[]{:S(2)}, u32[]{:S(2)}) collective-permute-start(bf16[512,1024]{1,0:T(8,128)(2,1)} %c.1), channel_id=1, source_target_pairs={{0,16},{16,0},{1,17},{17,1},{2,18},{18,2},{3,19},{19,3},{4,20},{20... | collective-permute-start | bytes 3145736 | tf_op jit(solution)/shard_map/ppermute | solution.py:311
  82.6 1.4 copy-start.1
  91.4 18.6 %collective-permute-start.6 = (s16[528,1024]{1,0:T(8,128)(2,1)}, s16[528,1024]{1,0:T(8,128)(2,1)}, u32[]{:S(2)}, u32[]{:S(2)}) collective-permute-start(s16[528,1024]{1,0:T(8,128)(2,1)} %get-tuple-element.19), channel_id=1, source_target_pairs={{0,12},{1,13},{2,14},{3,15},{4,0},{5,1},{6,2},{7,3},{8,4},{9,5},{1... | collective-permute-start | bytes 3244040 | tf_op jit(solution)/shard_map/ppermute | solution.py:312
  92.4 24.7 %collective-permute-start.2 = (s16[528,1024]{1,0:T(8,128)(2,1)}, s16[528,1024]{1,0:T(8,128)(2,1)}, u32[]{:S(2)}, u32[]{:S(2)}) collective-permute-start(s16[528,1024]{1,0:T(8,128)(2,1)} %get-tuple-element.15), channel_id=1, source_target_pairs={{0,4},{1,5},{2,6},{3,7},{4,8},{5,9},{6,10},{7,11},{8,12},{9,13},{1... | collective-permute-start | bytes 3244040 | tf_op jit(solution)/shard_map/ppermute | solution.py:312
  100.9 27.6 %collective-permute-start.5 = (s16[528,1024]{1,0:T(8,128)(2,1)}, s16[528,1024]{1,0:T(8,128)(2,1)S(1)}, u32[]{:S(2)}, u32[]{:S(2)}) collective-permute-start(s16[528,1024]{1,0:T(8,128)(2,1)} %get-tuple-element.17), channel_id=1, source_target_pairs={{0,12},{1,13},{2,14},{3,15},{4,0},{5,1},{6,2},{7,3},{8,4},{9,5},{1... | collective-permute-start | bytes 3244040 | tf_op jit(solution)/shard_map/ppermute | solution.py:312
  109.9 18.6 %collective-permute-start.4 = (s16[528,1024]{1,0:T(8,128)(2,1)}, s16[528,1024]{1,0:T(8,128)(2,1)S(1)}, u32[]{:S(2)}, u32[]{:S(2)}) collective-permute-start(s16[528,1024]{1,0:T(8,128)(2,1)} %get-tuple-element.16), channel_id=1, source_target_pairs={{0,4},{1,5},{2,6},{3,7},{4,8},{5,9},{6,10},{7,11},{8,12},{9,13},{1... | collective-permute-start | bytes 3244040 | tf_op jit(solution)/shard_map/ppermute | solution.py:312
  114.5 15.1 %collective-permute-start.7 = (s16[528,1024]{1,0:T(8,128)(2,1)}, s16[528,1024]{1,0:T(8,128)(2,1)}, u32[]{:S(2)}, u32[]{:S(2)}) collective-permute-start(s16[528,1024]{1,0:T(8,128)(2,1)} %relay.3), channel_id=1, source_target_pairs={{0,12},{1,13},{2,14},{3,15},{4,0},{5,1},{6,2},{7,3},{8,4},{9,5},{1... | collective-permute-start | bytes 3244040 | tf_op jit(solution)/shard_map/ppermute | solution.py:312
  121.7 15.8 %collective-permute-start.3 = (s16[528,1024]{1,0:T(8,128)(2,1)}, s16[528,1024]{1,0:T(8,128)(2,1)}, u32[]{:S(2)}, u32[]{:S(2)}) collective-permute-start(s16[528,1024]{1,0:T(8,128)(2,1)} %relay.2), channel_id=1, source_target_pairs={{0,4},{1,5},{2,6},{3,7},{4,8},{5,9},{6,10},{7,11},{8,12},{9,13},{1... | collective-permute-start | bytes 3244040 | tf_op jit(solution)/shard_map/ppermute | solution.py:312
  128.6 8.9 %copy-start.2 = (s16[528,1024]{1,0:T(8,128)(2,1)}, s16[528,1024]{1,0:T(8,128)(2,1)S(1)}, u32[]{:S(2)}) copy-start(s16[528,1024]{1,0:T(8,128)(2,1)S(1)} %collective-permute-done.5.da.da_ex) | copy-start | bytes 3244036
  128.6 8.9 %copy-start.3 = (s16[528,1024]{1,0:T(8,128)(2,1)}, s16[528,1024]{1,0:T(8,128)(2,1)S(1)}, u32[]{:S(2)}) copy-start(s16[528,1024]{1,0:T(8,128)(2,1)S(1)} %collective-permute-done.4.ub.ub_ex) | copy-start | bytes 3244036
  144.6 2.5 %copy-start.10 = (s16[272,1024]{1,0:T(8,128)(2,1)S(1)}, s16[272,1024]{1,0:T(8,128)(2,1)}, u32[]{:S(2)}) copy-start(s16[272,1024]{1,0:T(8,128)(2,1)} %get-tuple-element.22) | copy-start | bytes 1671172
  144.6 3.5 %copy-start.9 = (s16[272,1024]{1,0:T(8,128)(2,1)S(1)}, s16[272,1024]{1,0:T(8,128)(2,1)}, u32[]{:S(2)}) copy-start(s16[272,1024]{1,0:T(8,128)(2,1)} %get-tuple-element.23) | copy-start | bytes 1671172
  144.6 4.4 %copy-start.5 = (s16[272,1024]{1,0:T(8,128)(2,1)S(1)}, s16[272,1024]{1,0:T(8,128)(2,1)}, u32[]{:S(2)}) copy-start(s16[272,1024]{1,0:T(8,128)(2,1)} %get-tuple-element.20.after) | copy-start | bytes 1671172
  144.6 76.1 %collective-permute-start.8 = (bf16[2048,1024]{1,0:T(8,128)(2,1)}, bf16[2048,1024]{1,0:T(8,128)(2,1)}, u32[]{:S(2)}, u32[]{:S(2)}) collective-permute-start(bf16[2048,1024]{1,0:T(8,128)(2,1)} %tie.1.w_own), channel_id=1, source_target_pairs={{0,16},{16,0},{1,17},{17,1},{2,18},{18,2},{3,19},{19,3},{4,20},{20... | collective-permute-start | bytes 12582920 | tf_op jit(solution)/shard_map/ppermute | solution.py:311
  147.1 10.2 %collective-permute-start.10 = (s16[272,1024]{1,0:T(8,128)(2,1)S(1)}, s16[272,1024]{1,0:T(8,128)(2,1)S(1)}, u32[]{:S(2)}, u32[]{:S(2)}) collective-permute-start(s16[272,1024]{1,0:T(8,128)(2,1)S(1)} %copy-done.10), channel_id=1, source_target_pairs={{0,2},{1,3},{2,0},{3,1},{4,6},{5,7},{6,4},{7,5},{8,10},{9,11},{10,... | collective-permute-start | bytes 1671176 | tf_op jit(solution)/shard_map/ppermute | solution.py:312
  148.1 13.5 %collective-permute-start.11 = (s16[272,1024]{1,0:T(8,128)(2,1)S(1)}, s16[272,1024]{1,0:T(8,128)(2,1)S(1)}, u32[]{:S(2)}, u32[]{:S(2)}) collective-permute-start(s16[272,1024]{1,0:T(8,128)(2,1)S(1)} %copy-done.9), channel_id=1, source_target_pairs={{0,3},{1,0},{2,1},{3,2},{4,7},{5,4},{6,5},{7,6},{8,11},{9,8},{10,9... | collective-permute-start | bytes 1671176 | tf_op jit(solution)/shard_map/ppermute | solution.py:312
  148.9 14.3 %collective-permute-start.9 = (s16[272,1024]{1,0:T(8,128)(2,1)S(1)}, s16[272,1024]{1,0:T(8,128)(2,1)S(1)}, u32[]{:S(2)}, u32[]{:S(2)}) collective-permute-start(s16[272,1024]{1,0:T(8,128)(2,1)S(1)} %copy-done.5), channel_id=1, source_target_pairs={{0,1},{1,2},{2,3},{3,0},{4,5},{5,6},{6,7},{7,4},{8,9},{9,10},{10,1... | collective-permute-start | bytes 1671176 | tf_op jit(solution)/shard_map/ppermute | solution.py:312
  157.3 5.9 %copy-start.6 = (s16[272,1024]{1,0:T(8,128)(2,1)}, s16[272,1024]{1,0:T(8,128)(2,1)S(1)}, u32[]{:S(2)}) copy-start(s16[272,1024]{1,0:T(8,128)(2,1)S(1)} %collective-permute-done.10.n2) | copy-start | bytes 1671172
  161.6 1.6 copy-start.7
  163.2 0.9 copy-start.8
  168.9 24.8 %all-to-all-start = ((s16[8,32,1152]{2,1,0:T(8,128)(2,1)}), s16[8,32,1152]{2,1,0:T(8,128)(2,1)S(1)}, u32[]{:S(2)}, u32[]{:S(2)}) async-start(s16[8,32,1152]{2,1,0:T(8,128)(2,1)} %bitcast.21), calls=%async_computation | async-start | bytes 1179648 | tf_op jit(solution)/shard_map/all_to_all | solution.py:473
  193.6 0.8 copy-start.4
Sparse Core Ops, SparseCore 0:
  10.4 60.3 all-gather.1

commit v3 on v1

v3 whole, which is shorter than its diff:
```python
import jax
import jax.numpy as jnp
import numpy as np
from jax import lax
from jax.experimental import pallas as pl
from jax.experimental.pallas import tpu as pltpu
from jax.sharding import Mesh, PartitionSpec as P

NZ, NC, NX, NY = 8, 2, 4, 4
AXES = ("z", "core", "x", "y")
KV = 1024
TOK = 512
F32, BF16, I16, I32 = jnp.float32, jnp.bfloat16, jnp.int16, jnp.int32
VMEM = 56 * 1024 * 1024
SMALL = 24 * 1024 * 1024


def hadamard(size):
    positions = np.arange(size)
    common = positions[:, None] & positions[None, :]
    parity = np.zeros((size, size), np.int64)
    for bit in range(16):
        parity += (common >> bit) & 1
    return (1 - 2 * (parity & 1)).astype(np.float32)


def power(e):
    return jnp.exp2(e * 0.125)


def step_of(top, low):
    return jnp.ceil(jnp.log2(jnp.maximum(top, low)) * 8.0)


def encode(v, ce):
    u = v if ce is None else v * power(-ce)
    e = step_of(jnp.max(jnp.abs(u), axis=1, keepdims=True), 1e-30) - 119.0
    q = jnp.floor(u * power(-e) + 0.5)
    return q.astype(I32).astype(I16), e


def to_float(q):
    return q.astype(I32).astype(F32)


def eye():
    return lax.broadcasted_iota(I32, (128, 128), 0) == lax.broadcasted_iota(I32, (128, 128), 1)


def to_lanes(col):
    return jnp.sum(jnp.where(eye(), col, 0.0), axis=0, keepdims=True)


def to_rows(row):
    return jnp.sum(jnp.where(eye(), row, 0.0), axis=1, keepdims=True)


def write(msg, v, ce):
    count = v.shape[0]
    q, e = encode(v, ce)
    msg[0:count, :] = q
    parts = [to_lanes(e[k : k + 128]) for k in range(0, count, 128)]
    line = jnp.concatenate(parts + [jnp.zeros((1, KV - count), F32)], 1)
    row = lax.broadcasted_iota(I32, (16, KV), 0)
    extra = jnp.where(row == 0, line, jnp.where(row == 1, ce, 0.0))
    msg[count : count + 16, :] = extra.astype(I32).astype(I16)


def steps_in(msg):
    count = msg.shape[0] - 16
    return to_float(msg[count : count + 16, :])


def read(msg):
    count = msg.shape[0] - 16
    extra = steps_in(msg)
    e = jnp.concatenate([to_rows(extra[0:1, k : k + 128]) for k in range(0, count, 128)], 0)
    return to_float(msg[0:count, :]) * power(e) * power(extra[1:2, :])


def product(tiles, c):
    a = jnp.concatenate([t[...] for t in tiles], 1)
    return lax.dot_general(a, c[...], (((0,), (0,)), ((), ())), preferred_element_type=F32)


def column_steps(c):
    top = jnp.max(jnp.abs(c.astype(F32)), axis=0, keepdims=True)
    return jnp.clip(step_of(top, 1e-30), -800.0, 800.0)


def half(v, number):
    return jnp.concatenate([v[k + 64 * number : k + 64 * number + 64] for k in range(0, v.shape[0], 128)], 0)


def far_kernel(idx, t0, t1, t2, t3, c, up_x, down_x, up_y, down_y, ce):
    ce[...] = jnp.broadcast_to(column_steps(c[...]), (8, KV))
    p = product((t0, t1, t2, t3), c)
    for axis, (up, down) in enumerate(((up_x, down_x), (up_y, down_y))):

        @pl.when(pl.program_id(0) == axis)
        def _(up=up, down=down):
            write(up, half(p, 0), ce[0:1, :])
            write(down, half(p, 1), ce[0:1, :])


def near_kernel(idx, t0, t1, t2, t3, c, ce, up_x, down_x, up_y, down_y, keep):
    p = product((t0, t1, t2, t3), c)
    for step, msg in enumerate((up_x, down_x, up_y, down_y)):

        @pl.when(pl.program_id(0) == step)
        def _(step=step, msg=msg):
            kept = step % 2
            keep[...] = half(p, kept)
            write(msg, half(p, 1 - kept), ce[0:1, :])


def own_kernel(idx, t0, t1, t2, t3, c, keep):
    keep[...] = product((t0, t1, t2, t3), c)


def relay_kernel(keep, ce, *refs):
    for step in range(4):

        @pl.when(pl.program_id(0) == step)
        def _(got=refs[step], msg=refs[4 + step]):
            write(msg, keep[...] + read(got), jnp.maximum(ce[0:1, :], steps_in(got)[1:2, :]))


def cross_kernel(keep, ce, *refs):
    for axis in range(2):

        @pl.when(pl.program_id(0) == axis)
        def _(got=refs[4 * axis : 4 * axis + 4], out=refs[8 + 4 * axis : 12 + 4 * axis]):
            up2, down2, up3, down3 = got
            ce_all = ce[0:1, :]
            for msg in got:
                ce_all = jnp.maximum(ce_all, steps_in(msg)[1:2, :])
            first, last = read(up3) + read(down2), read(up2) + read(down3)
            for t in range(4):
                rows = slice(t * 64, t * 64 + 64)
                total = keep[t * 128 : t * 128 + 128, :] + jnp.concatenate([first[rows], last[rows]], 0)
                if t == 0:
                    out[0][...] = total
                else:
                    write(out[t], total, ce_all)


def split_dot(x, m):
    hi = x.astype(BF16)
    rest = x - hi.astype(F32)
    mid = rest.astype(BF16)
    lo = (rest - mid.astype(F32)).astype(BF16)
    dot = lambda a: jnp.dot(a, m, preferred_element_type=F32)
    return dot(hi) + (dot(mid) + dot(lo))


def split_dot_left(m, x):
    hi = x.astype(BF16)
    rest = x - hi.astype(F32)
    mid = rest.astype(BF16)
    lo = (rest - mid.astype(F32)).astype(BF16)
    dot = lambda a: jnp.dot(m, a, preferred_element_type=F32)
    return dot(hi) + (dot(mid) + dot(lo))


def rotate(v, inner, rows):
    tiles = [v[:, k * 128 : (k + 1) * 128] for k in range(8)]
    for bit in (1, 2, 4):
        tiles = [tiles[k ^ bit] - tiles[k] if k & bit else tiles[k] + tiles[k ^ bit] for k in range(8)]
    mixed = jnp.concatenate([split_dot(t, inner) for t in tiles], 1)
    return split_dot_left(rows, mixed) * (1.0 / 64.0)


def rotate_kernel(own_x, own_y, x1, x2, x3, y1, y2, y3, signs, inner, rows, out):
    for k, (own, msgs) in enumerate(((own_x, (x1, x2, x3)), (own_y, (y1, y2, y3)))):
        here = slice(k * 128, k * 128 + 128)
        total = own[...]
        for msg in msgs:
            total = total + read(msg)
        q, e = encode(rotate(total * signs[here, :].astype(F32), inner[...], rows[...]), None)
        out[here, 0:KV] = q
        out[here, KV : KV + 128] = jnp.broadcast_to(e, (128, 128)).astype(I32).astype(I16)


def levels_kernel(count, x, inner, rows, out):
    level = count[0].astype(F32)

    def group(g):
        q = x[g * 16 : g * 16 + 16, :]
        e = to_float(q[:, KV : KV + 128])[:, 0:1]
        return to_float(q[:, 0:KV]) * power(e)

    groups = [group(g) for g in range(NZ * NC)]
    top = jnp.abs(groups[0])
    for v in groups[1:]:
        top = jnp.maximum(top, jnp.abs(v))
    top = jnp.max(top, axis=1, keepdims=True)
    block = lax.shift_right_logical(lax.broadcasted_iota(I32, (16, 1), 0), 2)
    peak = jnp.zeros((16, 1), F32)
    for b in range(4):
        peak = jnp.where(block == b, jnp.max(jnp.where(block == b, top, 0.0), axis=0, keepdims=True), peak)
    peak = peak + 1e-06
    scale = level / peak
    total = jnp.floor(groups[0] * scale + 0.5)
    for v in groups[1:]:
        total = total + jnp.floor(v * scale + 0.5)
    q, e = encode(rotate(total * (peak / level), inner[...], rows[...]), None)
    out[:, 0:KV] = q
    out[:, KV : KV + 128] = jnp.broadcast_to(e, (16, 128)).astype(I32).astype(I16)


def finish_kernel(q, signs, out):
    e = to_float(q[:, KV : KV + 128])[:, 0:1]
    out[...] = signs[...].astype(F32) * (to_float(q[:, 0:KV]) * power(e))


def input_grad_kernel(core, c, w_own, w_oth, out, w):
    for k in range(4):
        rows = slice(k * 128, k * 128 + 128)
        w[pl.ds(pl.multiple_of(k * 256 + core[0] * 128, 128), 128), :] = w_own[rows, :]
        w[pl.ds(pl.multiple_of(k * 256 + 128 - core[0] * 128, 128), 128), :] = w_oth[rows, :]
    out[...] = lax.dot_general(c[...], w[...], (((1,), (1,)), ((), ())), preferred_element_type=F32).astype(BF16)


def tie_kernel(w, after, out):
    del w, after, out


def half_kernel(core, w, after, out):
    out[...] = w[...]


def params(limit=VMEM):
    return pltpu.CompilerParams(vmem_limit_bytes=limit)


def cost(flops, moved):
    return pl.CostEstimate(flops=int(flops), bytes_accessed=int(moved), transcendentals=0)


def whole(shape):
    return pl.BlockSpec(shape, lambda *_: (0,) * len(shape))


def shift(size, s):
    return [(k, (k + s) % size) for k in range(size)]


def shards(activations, cotangent, value_weights, sign_flips, level_count):
    core = lax.axis_index("core").astype(I32)
    x, y = lax.axis_index("x").astype(I32), lax.axis_index("y").astype(I32)
    sds = jax.ShapeDtypeStruct
    anywhere = pl.BlockSpec(memory_space=pl.ANY)
    in_vmem = pl.BlockSpec(memory_space=pltpu.VMEM)

    def send(v, axis, s):
        return lax.ppermute(v, "xy"[axis], shift((NX, NY)[axis], s))

    ids = []
    for axis in range(2):
        for dp in range(4):
            for dq in range(4):
                tx = (x + (dq if axis else dp)) % NX
                ty = (y + (dp if axis else dq)) % NY
                ids.append(2 * (tx * NY + ty) + axis)
    idx = jnp.stack(ids).astype(I32)

    def operands(where):
        tiles = [pl.BlockSpec((TOK, 128), lambda k, ids, t=t: (0, ids[where(k) + t])) for t in range(4)]
        return tiles + [whole((TOK, KV))]

    inputs = (activations,) * 4 + (cotangent,)
    message = pltpu.HBM((272, KV), I16)
    mm = 2 * 1024 * 1024 * 512

    up1x, down1x, up1y, down1y, ce = pl.pallas_call(
        far_kernel,
        out_shape=(message,) * 4 + (sds((8, KV), F32),),
        grid_spec=pltpu.PrefetchScalarGridSpec(
            num_scalar_prefetch=1,
            grid=(2,),
            in_specs=operands(lambda k: 16 * k + 8),
            out_specs=(whole((272, KV)),) * 4 + (whole((8, KV)),),
        ),
        compiler_params=params(),
        cost_estimate=cost(mm, 6 << 20),
        name="far",
    )(idx, *inputs)
    got1 = [send(up1x, 0, 1), send(down1x, 0, -1), send(up1y, 1, 1), send(down1y, 1, -1)]

    up2x, down2x, up2y, down2y, keep_near = pl.pallas_call(
        near_kernel,
        out_shape=(message,) * 4 + (sds((1024, KV), F32),),
        grid_spec=pltpu.PrefetchScalarGridSpec(
            num_scalar_prefetch=1,
            grid=(4,),
            in_specs=operands(lambda k: 16 * (k // 2) + 4 + 8 * (k % 2)) + [whole((8, KV))],
            out_specs=(whole((272, KV)),) * 4 + (pl.BlockSpec((256, KV), lambda k, ids: (k, 0)),),
        ),
        compiler_params=params(SMALL),
        cost_estimate=cost(2 * mm, 11 << 20),
        name="near",
    )(idx, *inputs, ce)
    got2 = [send(up2x, 0, 1), send(down2x, 0, -1), send(up2y, 1, 1), send(down2y, 1, -1)]

    keep = pl.pallas_call(
        own_kernel,
        out_shape=sds((1024, KV), F32),
        grid_spec=pltpu.PrefetchScalarGridSpec(
            num_scalar_prefetch=1,
            grid=(2,),
            in_specs=operands(lambda k: 16 * k),
            out_specs=pl.BlockSpec((512, KV), lambda k, ids: (k, 0)),
        ),
        compiler_params=params(SMALL),
        cost_estimate=cost(mm, 8 << 20),
        name="own",
    )(idx, *inputs)

    up3x, down3x, up3y, down3y = pl.pallas_call(
        relay_kernel,
        out_shape=(message,) * 4,
        grid=(4,),
        in_specs=[pl.BlockSpec((256, KV), lambda k: (k, 0)), whole((8, KV))] + [whole((272, KV))] * 4,
        out_specs=(whole((272, KV)),) * 4,
        compiler_params=params(SMALL),
        cost_estimate=cost(1 << 20, 8 << 20),
        name="relay",
    )(keep_near, ce, *got1)
    got3 = [send(up3x, 0, 1), send(down3x, 0, -1), send(up3y, 1, 1), send(down3y, 1, -1)]

    parts = pl.pallas_call(
        cross_kernel,
        out_shape=((pltpu.HBM((128, KV), F32),) + (pltpu.HBM((144, KV), I16),) * 3) * 2,
        grid=(2,),
        in_specs=[pl.BlockSpec((512, KV), lambda k: (k, 0)), whole((8, KV))] + [whole((272, KV))] * 8,
        out_specs=((whole((128, KV)),) + (whole((144, KV)),) * 3) * 2,
        compiler_params=params(SMALL),
        cost_estimate=cost(1 << 20, 12 << 20),
        name="cross",
    )(keep, ce, got2[0], got2[1], got3[0], got3[1], got2[2], got2[3], got3[2], got3[3])
    own_x, x1, x2, x3, own_y, y1, y2, y3 = parts
    last = [send(x1, 1, 1), send(x2, 1, 2), send(x3, 1, -1), send(y1, 0, 1), send(y2, 0, 2), send(y3, 0, -1)]

    half_w = pl.pallas_call(
        half_kernel,
        out_shape=pltpu.HBM((128, KV), BF16),
        grid_spec=pltpu.PrefetchScalarGridSpec(
            num_scalar_prefetch=1,
            grid=(1,),
            in_specs=[pl.BlockSpec((128, KV), lambda k, c: (c[0], 0)), anywhere],
            out_specs=whole((128, KV)),
        ),
        compiler_params=params(SMALL),
        name="half",
    )(core.reshape(1), value_weights, keep)
    w_own = lax.all_gather(half_w, ("x", "y"), axis=0, tiled=True)

    inner = jnp.asarray(hadamard(128), BF16)
    quad = hadamard(4)
    spun = pl.pallas_call(
        rotate_kernel,
        out_shape=sds((256, KV + 128), I16),
        in_specs=[in_vmem] * 11,
        out_specs=in_vmem,
        compiler_params=params(SMALL),
        cost_estimate=cost(1 << 28, 4 << 20),
        name="rotate",
    )(own_x, own_y, *last, sign_flips, inner, jnp.asarray(np.kron(np.eye(32), quad), BF16))
    groups = lax.all_to_all(spun, ("z", "core"), 0, 0, tiled=True)

    back = pl.pallas_call(
        levels_kernel,
        out_shape=sds((16, KV + 128), I16),
        in_specs=[pl.BlockSpec(memory_space=pltpu.SMEM)] + [in_vmem] * 3,
        out_specs=in_vmem,
        compiler_params=params(SMALL),
        cost_estimate=cost(1 << 26, 1 << 20),
        name="levels",
    )(level_count.reshape(1), groups, inner, jnp.asarray(np.kron(np.eye(4), quad), BF16))
    w_own = pl.pallas_call(
        tie_kernel,
        out_shape=sds((2048, KV), BF16),
        in_specs=[anywhere] * 2,
        out_specs=anywhere,
        input_output_aliases={0: 0},
        name="tie",
    )(w_own, back)
    w_oth = lax.ppermute(w_own, "core", shift(NC, 1))
    gathered = lax.all_gather(back, ("z", "core"), axis=0, tiled=True)
    weight_grad = pl.pallas_call(
        finish_kernel,
        out_shape=sds((256, KV), F32),
        in_specs=[in_vmem] * 2,
        out_specs=in_vmem,
        compiler_params=params(SMALL),
        cost_estimate=cost(1 << 20, 3 << 20),
        name="finish",
    )(gathered, sign_flips)
    input_grad = pl.pallas_call(
        input_grad_kernel,
        out_shape=pltpu.HBM((TOK, 4096), BF16),
        grid_spec=pltpu.PrefetchScalarGridSpec(
            num_scalar_prefetch=1,
            grid=(4,),
            in_specs=[
                whole((TOK, KV)),
                pl.BlockSpec((512, KV), lambda k, c: (k, 0)),
                pl.BlockSpec((512, KV), lambda k, c: (k, 0)),
            ],
            out_specs=pl.BlockSpec((TOK, 1024), lambda k, c: (0, k)),
            scratch_shapes=[pltpu.VMEM((1024, KV), BF16)],
        ),
        compiler_params=params(SMALL),
        cost_estimate=cost(4 * mm, 13 << 20),
        name="input_grad",
    )(core.reshape(1), cotangent, w_own, w_oth)

    return (input_grad, weight_grad)


def solution(mesh):
    torus = Mesh(mesh.devices.reshape(NZ, NC, NX, NY), AXES)
    rows = P(AXES, None)
    part = P(("x", "y"), None)
    return jax.shard_map(
        shards,
        mesh=torus,
        in_specs=(rows, rows, part, part, P()),
        out_specs=(rows, part),
        check_vma=False,
    )
```

time: 267 us -> 181 us (0.68)
  waiting for transfers between devices: 212 us -> 60.1 us
  Pallas kernels: 0 us -> 37.7 us
  starting transfers between devices: 8.14 us -> 40.1 us
  matrix products: 23.5 us -> 0 us
  blocking collectives: 0 us -> 16.1 us
  local copies, waits for them, and re-layouts: 4.35 us -> 12 us
  other arithmetic: 4.3 us -> 0 us
    reduce_scatter x1 -> x0, waiting for transfers between devices: 118 us -> none  [shards(): lax.psum_scatter(lax.dot_general(activations, cotangent, (((0,), (0,)), (...]
    all_gather x2 -> x1, waiting for transfers between devices: 65.1 us -> 0.01 us  [shards(): w_own = lax.all_gather(half_w, ('x', 'y'), axis=0, tiled=True)]
    ppermute x0 -> x19, waiting for transfers between devices: none -> 42 us  [the longest x18 42 us: send(): return lax.ppermute(v, 'xy'[axis], shift((NX, NY)[axis], s))]
    pallas_call x0 -> x11, Pallas kernels: none -> 37.7 us  [the longest x1 7.48 us: shards(): pl.pallas_call(near_kernel, out_shape=(message,) * 4 + (sds((1024, KV), F...]
    ppermute x0 -> x19, starting transfers between devices: none -> 28.1 us  [the longest x18 28.1 us: send(): return lax.ppermute(v, 'xy'[axis], shift((NX, NY)[axis], s))]
    dot_general x6 -> x0, matrix products: 23.5 us -> none  [the longest x1 10.4 us: shards(): lax.dot_general(activations, cotangent, (((0,), (0,)), ((), ())), preferr...]
    all_gather x0 -> x1, blocking collectives: none -> 16.1 us  [shards(): gathered = lax.all_gather(back, ('z', 'core'), axis=0, tiled=True)]
    unnamed x4 -> x38, local copies, waits for them, and re-layouts: 1.18 us -> 11.9 us
  transfers between devices with their start and end apart: 4 -> 21, of which waited for: 4 -> 9; matrix products, arithmetic and copies ran while one was open for 7% -> 0% of each run, Pallas kernels for 0% -> 15%
where the time goes in v3:
time: 181 us
  waiting for transfers between devices  60.1 us (33%)
  starting transfers between devices  40.1 us (22%)
  Pallas kernels  37.7 us (21%)
  blocking collectives  16.1 us (9%)
  between operations  14.9 us (8%)
  local copies, waits for them, and re-layouts  12 us (7%)
    ppermute x18, waiting for transfers between devices, send(): return lax.ppermute(v, 'xy'[axis], shift((NX, NY)[axis], s))  42 us
    ppermute x18, starting transfers between devices, send(): return lax.ppermute(v, 'xy'[axis], shift((NX, NY)[axis], s))  28.1 us
    all_to_all x1, waiting for transfers between devices, shards(): groups = lax.all_to_all(spun, ('z', 'core'), 0, 0, tiled=True)  18 us
    all_gather x1, blocking collectives, shards(): gathered = lax.all_gather(back, ('z', 'core'), axis=0, tiled=True)  16.1 us
    all_to_all x1, starting transfers between devices, shards(): groups = lax.all_to_all(spun, ('z', 'core'), 0, 0, tiled=True)  11.9 us
    unnamed x38, local copies, waits for them, and re-layouts  11.9 us
    pallas_call x1, Pallas kernels, shards(): pl.pallas_call(near_kernel, out_shape=(message,) * 4 + (sds((1024, KV), F...  7.48 us
    pallas_call x1, Pallas kernels, shards(): pl.pallas_call(far_kernel, out_shape=(message,) * 4 + (sds((8, KV), F32),...  6.97 us
  transfers between devices with their start and end apart: 21, of which 9 were waited for; matrix products, arithmetic and copies ran while one was open for 0% of the time, Pallas kernels for 15%

profile of v3, /device:TPU:1, one launch (start us, length us, event | category | flops | bytes accessed | tf_op | source)
XLA Modules:
  0.0 180.8 jit_solution(8524636692681305302)
XLA Ops:
  7.2 0.0 all-gather.2.cloned.1.call-start
  7.3 0.1 stack.131.idx
  7.4 0.0 copy-start
  7.4 2.2 %copy-done = bf16[512,4096]{1,0:T(8,128)(2,1)S(1)} copy-done((bf16[512,4096]{1,0:T(8,128)(2,1)S(1)}, bf16[512,4096]{1,0:T(8,128)(2,1)}, u32[]{:S(2)}) %copy-start) | copy-done | bytes 4194328
  9.6 1.2 copy-done.4
  10.8 2.4 %own.1.after.keep = f32[1024,1024]{1,0:T(8,128)S(1)} custom-call(s32[32]{0:T(128)S(1)} %stack.131.idx, bf16[512,4096]{1,0:T(8,128)(2,1)S(1)} %copy-done, bf16[512,4096]{1,0:T(8,128)(2,1)S(1)} %copy-done, bf16[512,4096]{1,0:T(8,128)(2,1)S(1)} %copy-done, bf16[512,4096]{1,0:T(8,128)(2,1)S(1)} %copy-done, bf16[512,1024]{1,0:T(8,128)(2,1)S(1)} %copy-done.4), custom_call_target="tpu_custom_call" | custom-call | flops 1073741824 | bytes 8388608 | tf_op jit(solution)/shard_map/own/pallas_call | solution.py:306
  13.3 0.8 half.1
  14.0 2.0 %copy-done.2 = f32[1024,1024]{1,0:T(8,128)} copy-done((f32[1024,1024]{1,0:T(8,128)}, f32[1024,1024]{1,0:T(8,128)S(1)}, u32[]{:S(2)}) %copy-start.2) | copy-done | bytes 4194328
  16.1 0.0 all-gather.2.cloned.1.call-update
  16.1 0.0 copy-start.1
  16.1 0.0 copy-start.5
  16.1 7.0 %far.1 = (s16[272,1024]{1,0:T(8,128)(2,1)}, s16[272,1024]{1,0:T(8,128)(2,1)}, s16[272,1024]{1,0:T(8,128)(2,1)}, s16[272,1024]{1,0:T(8,128)(2,1)}, f32[8,1024]{1,0:T(8,128)}) custom-call(s32[32]{0:T(128)} %copy-done.16, bf16[512,4096]{1,0:T(8,128)(2,1)} %t3.5, bf16[512,4096]{1,0:T(8,128)(2,1)} %t3.5, bf16[512,4096]{1,0:T(8,128)(2,1)} %t3.5, ...), custom_call_target="tpu_custom_call" | custom-call | flops 1073741824 | bytes 6291456 | tf_op jit(solution)/shard_map/far/pallas_call | solution.py:276
  23.1 2.0 %collective-permute-start.2 = (s16[272,1024]{1,0:T(8,128)(2,1)}, s16[272,1024]{1,0:T(8,128)(2,1)S(1)}, u32[]{:S(2)}, u32[]{:S(2)}) collective-permute-start(s16[272,1024]{1,0:T(8,128)(2,1)} %get-tuple-element.28), channel_id=1, source_target_pairs={{0,4},{4,8},{8,12},{12,0},{1,5},{5,9},{9,13},{13,1},{2,6},{6,10},{... | collective-permute-start | bytes 1671176 | tf_op jit(solution)/shard_map/ppermute | solution.py:257
  25.1 1.4 collective-permute-start.3
  26.5 1.4 collective-permute-start.4
  27.9 1.4 collective-permute-start.5
  29.3 0.8 copy-done.13
  30.1 7.5 %near.1 = (s16[272,1024]{1,0:T(8,128)(2,1)}, s16[272,1024]{1,0:T(8,128)(2,1)}, s16[272,1024]{1,0:T(8,128)(2,1)}, s16[272,1024]{1,0:T(8,128)(2,1)}, f32[1024,1024]{1,0:T(8,128)S(1)}) custom-call(s32[32]{0:T(128)S(1)} %copy-done.17, bf16[512,4096]{1,0:T(8,128)(2,1)S(1)} %copy-done.1, bf16[512,4096]{1,0:T(8,128)(2,1)S(1)} %copy-done.1, ...), custom_call_target="tpu_custom_call" | custom-call | flops 2147483648 | bytes 11534336 | tf_op jit(solution)/shard_map/near/pallas_call | solution.py:291
  37.6 0.0 collective-permute-start
  37.6 0.3 collective-permute-done.2.refs_0_
  37.9 4.1 %collective-permute-start.1 = (s16[272,1024]{1,0:T(8,128)(2,1)}, s16[272,1024]{1,0:T(8,128)(2,1)S(1)}, u32[]{:S(2)}, u32[]{:S(2)}) collective-permute-start(s16[272,1024]{1,0:T(8,128)(2,1)} %get-tuple-element.26), channel_id=1, source_target_pairs={{0,12},{4,0},{8,4},{12,8},{1,13},{5,1},{9,5},{13,9},{2,14},{6,2},{... | collective-permute-start | bytes 1671176 | tf_op jit(solution)/shard_map/ppermute | solution.py:257
  42.0 0.0 collective-permute-done.3.refs_1_
  42.0 1.9 %collective-permute-start.8 = (s16[272,1024]{1,0:T(8,128)(2,1)}, s16[272,1024]{1,0:T(8,128)(2,1)S(1)}, u32[]{:S(2)}, u32[]{:S(2)}) collective-permute-start(s16[272,1024]{1,0:T(8,128)(2,1)} %get-tuple-element.34), channel_id=1, source_target_pairs={{0,1},{1,2},{2,3},{3,0},{4,5},{5,6},{6,7},{7,4},{8,9},{9,10},{10,1... | collective-permute-start | bytes 1671176 | tf_op jit(solution)/shard_map/ppermute | solution.py:257
  43.9 0.0 collective-permute-done.4.refs_2_
  43.9 2.2 %collective-permute-start.9 = (s16[272,1024]{1,0:T(8,128)(2,1)}, s16[272,1024]{1,0:T(8,128)(2,1)S(1)}, u32[]{:S(2)}, u32[]{:S(2)}) collective-permute-start(s16[272,1024]{1,0:T(8,128)(2,1)} %get-tuple-element.35), channel_id=1, source_target_pairs={{0,3},{1,0},{2,1},{3,2},{4,7},{5,4},{6,5},{7,6},{8,11},{9,8},{10,9... | collective-permute-start | bytes 1671176 | tf_op jit(solution)/shard_map/ppermute | solution.py:257
  46.1 0.0 collective-permute-done.5.refs_3_
  46.1 4.0 %relay.1 = (s16[272,1024]{1,0:T(8,128)(2,1)}, s16[272,1024]{1,0:T(8,128)(2,1)}, s16[272,1024]{1,0:T(8,128)(2,1)}, s16[272,1024]{1,0:T(8,128)(2,1)}) custom-call(f32[1024,1024]{1,0:T(8,128)S(1)} %get-tuple-element.27.keep, f32[8,1024]{1,0:T(8,128)S(1)} %copy-done.13, s16[272,1024]{1,0:T(8,128)(2,1)S(1)} %collective-permute-done.2.refs_0_, ...), custom_call_target="tpu_custom_call" | custom-call | flops 1048576 | bytes 8388608 | tf_op jit(solution)/shard_map/relay/pallas_call | solution.py:320
  50.1 0.0 collective-permute-start.10
  50.1 3.9 %collective-permute-done.refs_0_ = s16[272,1024]{1,0:T(8,128)(2,1)S(1)} collective-permute-done((s16[272,1024]{1,0:T(8,128)(2,1)}, s16[272,1024]{1,0:T(8,128)(2,1)S(1)}, u32[]{:S(2)}, u32[]{:S(2)}) %collective-permute-start) | collective-permute-done | bytes 557088 | tf_op jit(solution)/shard_map/ppermute | solution.py:257
  54.0 3.7 %collective-permute-start.11 = (s16[272,1024]{1,0:T(8,128)(2,1)}, s16[272,1024]{1,0:T(8,128)(2,1)S(1)}, u32[]{:S(2)}, u32[]{:S(2)}) collective-permute-start(s16[272,1024]{1,0:T(8,128)(2,1)} %get-tuple-element.37), channel_id=1, source_target_pairs={{0,3},{1,0},{2,1},{3,2},{4,7},{5,4},{6,5},{7,6},{8,11},{9,8},{10,9... | collective-permute-start | bytes 1671176 | tf_op jit(solution)/shard_map/ppermute | solution.py:257
  57.7 0.0 collective-permute-done.1.refs_1_
  57.7 0.0 collective-permute-start.6
  57.7 0.0 collective-permute-done.8.refs_4_
  57.7 0.0 copy-start.6
  57.7 0.0 copy-start.14
  57.8 0.0 copy-start.15
  57.8 2.7 %collective-permute-start.7 = (s16[272,1024]{1,0:T(8,128)(2,1)}, s16[272,1024]{1,0:T(8,128)(2,1)S(1)}, u32[]{:S(2)}, u32[]{:S(2)}) collective-permute-start(s16[272,1024]{1,0:T(8,128)(2,1)} %get-tuple-element.33), channel_id=1, source_target_pairs={{0,12},{4,0},{8,4},{12,8},{1,13},{5,1},{9,5},{13,9},{2,14},{6,2},{... | collective-permute-start | bytes 1671176 | tf_op jit(solution)/shard_map/ppermute | solution.py:257
  60.5 12.9 %collective-permute-done.10.refs_6_ = s16[272,1024]{1,0:T(8,128)(2,1)S(1)} collective-permute-done((s16[272,1024]{1,0:T(8,128)(2,1)}, s16[272,1024]{1,0:T(8,128)(2,1)S(1)}, u32[]{:S(2)}, u32[]{:S(2)}) %collective-permute-start.10) | collective-permute-done | bytes 557088 | tf_op jit(solution)/shard_map/ppermute | solution.py:257
  73.4 8.6 %collective-permute-done.11.refs_7_ = s16[272,1024]{1,0:T(8,128)(2,1)S(1)} collective-permute-done((s16[272,1024]{1,0:T(8,128)(2,1)}, s16[272,1024]{1,0:T(8,128)(2,1)S(1)}, u32[]{:S(2)}, u32[]{:S(2)}) %collective-permute-start.11) | collective-permute-done | bytes 557088 | tf_op jit(solution)/shard_map/ppermute | solution.py:257
  82.0 2.8 %collective-permute-done.6.refs_2_ = s16[272,1024]{1,0:T(8,128)(2,1)S(1)} collective-permute-done((s16[272,1024]{1,0:T(8,128)(2,1)}, s16[272,1024]{1,0:T(8,128)(2,1)S(1)}, u32[]{:S(2)}, u32[]{:S(2)}) %collective-permute-start.6) | collective-permute-done | bytes 557088 | tf_op jit(solution)/shard_map/ppermute | solution.py:257
  84.8 0.0 collective-permute-done.7.refs_3_
  84.8 4.2 %cross.1 = (f32[128,1024]{1,0:T(8,128)}, s16[144,1024]{1,0:T(8,128)(2,1)}, s16[144,1024]{1,0:T(8,128)(2,1)}, s16[144,1024]{1,0:T(8,128)(2,1)}, f32[128,1024]{1,0...) custom-call(f32[1024,1024]{1,0:T(8,128)S(1)} %copy-done.3, ...), custom_call_target="tpu_custom_call" | custom-call | flops 1048576 | bytes 12582912 | tf_op jit(solution)/shard_map/cross/pallas_call | solution.py:332
  89.0 0.0 collective-permute-start.12
  89.0 1.8 %collective-permute-start.13 = (s16[144,1024]{1,0:T(8,128)(2,1)}, s16[144,1024]{1,0:T(8,128)(2,1)S(1)}, u32[]{:S(2)}, u32[]{:S(2)}) collective-permute-start(s16[144,1024]{1,0:T(8,128)(2,1)} %get-tuple-element.41), channel_id=1, source_target_pairs={{0,2},{1,3},{2,0},{3,1},{4,6},{5,7},{6,4},{7,5},{8,10},{9,11},{10,... | collective-permute-start | bytes 884744 | tf_op jit(solution)/shard_map/ppermute | solution.py:257
  90.9 0.9 collective-permute-start.14
  91.7 2.5 %collective-permute-start.16 = (s16[144,1024]{1,0:T(8,128)(2,1)}, s16[144,1024]{1,0:T(8,128)(2,1)S(1)}, u32[]{:S(2)}, u32[]{:S(2)}) collective-permute-start(s16[144,1024]{1,0:T(8,128)(2,1)} %get-tuple-element.44), channel_id=1, source_target_pairs={{0,8},{4,12},{8,0},{12,4},{1,9},{5,13},{9,1},{13,5},{2,10},{6,14},... | collective-permute-start | bytes 884744 | tf_op jit(solution)/shard_map/ppermute | solution.py:257
  94.3 5.7 %collective-permute-done.12.x1 = s16[144,1024]{1,0:T(8,128)(2,1)S(1)} collective-permute-done((s16[144,1024]{1,0:T(8,128)(2,1)}, s16[144,1024]{1,0:T(8,128)(2,1)S(1)}, u32[]{:S(2)}, u32[]{:S(2)}) %collective-permute-start.12) | collective-permute-done | bytes 294944 | tf_op jit(solution)/shard_map/ppermute | solution.py:257
  99.9 2.0 %collective-permute-start.17 = (s16[144,1024]{1,0:T(8,128)(2,1)}, s16[144,1024]{1,0:T(8,128)(2,1)S(1)}, u32[]{:S(2)}, u32[]{:S(2)}) collective-permute-start(s16[144,1024]{1,0:T(8,128)(2,1)} %get-tuple-element.45), channel_id=1, source_target_pairs={{0,12},{4,0},{8,4},{12,8},{1,13},{5,1},{9,5},{13,9},{2,14},{6,2},{... | collective-permute-start | bytes 884744 | tf_op jit(solution)/shard_map/ppermute | solution.py:257
  102.0 0.2 collective-permute-done.15.y1
  102.2 7.7 %collective-permute-done.17.y3 = s16[144,1024]{1,0:T(8,128)(2,1)S(1)} collective-permute-done((s16[144,1024]{1,0:T(8,128)(2,1)}, s16[144,1024]{1,0:T(8,128)(2,1)S(1)}, u32[]{:S(2)}, u32[]{:S(2)}) %collective-permute-start.17) | collective-permute-done | bytes 294944 | tf_op jit(solution)/shard_map/ppermute | solution.py:257
  109.8 1.0 copy-done.9
  110.9 1.0 copy-done.10
  111.9 2.9 %rotate.1 = s16[256,1152]{1,0:T(8,128)(2,1)} custom-call(f32[128,1024]{1,0:T(8,128)S(1)} %copy-done.9, f32[128,1024]{1,0:T(8,128)S(1)} %copy-done.10, s16[144,1024]{1,0:T(8,128)(2,1)S(1)} %collective-permute-done.12.x1, s16[144,1024]{1,0:T(8,128)(2,1)S(1)} %collective-permute-done.13.x2, s16[144,1024]{1,0:T(8,128)(2,1)S(1)} %collective-permute-done.14.x3, ...), custom_call_target="tpu_custom_call" | custom-call | flops 268435456 | bytes 4194304 | tf_op jit(solution)/shard_map/rotate/pallas_call | solution.py:361
  114.8 11.9 %all-to-all-start = ((s16[16,16,1152]{2,1,0:T(8,128)(2,1)}), s16[16,16,1152]{2,1,0:T(8,128)(2,1)S(1)}, u32[]{:S(2)}, u32[]{:S(2)}) async-start(s16[16,16,1152]{2,1,0:T(8,128)(2,1)} %bitcast.34), calls=%async_computation | async-start | bytes 1179648 | tf_op jit(solution)/shard_map/all_to_all | solution.py:370
  127.4 18.0 %all-to-all-done = s16[16,16,1152]{2,1,0:T(8,128)(2,1)S(1)} async-done(((s16[16,16,1152]{2,1,0:T(8,128)(2,1)}), s16[16,16,1152]{2,1,0:T(8,128)(2,1)S(1)}, u32[]{:S(2)}, u32[]{:S(2)}) %all-to-all-start) | async-done | bytes 589856 | tf_op jit(solution)/shard_map/all_to_all | solution.py:370
  145.4 1.0 levels.1.after
  146.4 0.0 copy-start.11
  146.4 0.6 copy-done.11
  147.0 0.0 collective-permute-start.18
  147.0 0.8 copy-done.12
  147.8 16.1 %all_gather.7.q = s16[256,1152]{1,0:T(8,128)(2,1)S(1)} all-gather(s16[16,1152]{1,0:T(8,128)(2,1)S(1)} %copy-done.12), channel_id=1, replica_groups=mesh['z'=8,'core'=2,'x'=4,'y'=4] {'z','core'}, dimensions={0}, use_global_device_ids=true | all-gather | bytes 626688 | tf_op jit(solution)/shard_map/all_gather | solution.py:390
  163.9 1.2 finish.1
  165.1 2.2 %copy-done.7 = bf16[2048,1024]{1,0:T(8,128)(2,1)S(1)} copy-done((bf16[2048,1024]{1,0:T(8,128)(2,1)S(1)}, bf16[2048,1024]{1,0:T(8,128)(2,1)}, u32[]{:S(2)}) %copy-start.7) | copy-done | bytes 4194328
  167.2 6.7 %input_grad.1 = bf16[512,4096]{1,0:T(8,128)(2,1)} custom-call(s32[1]{0:T(128)} %bitcast.core, bf16[512,1024]{1,0:T(8,128)(2,1)S(1)} %copy-done.5, bf16[2048,1024]{1,0:T(8,128)(2,1)S(1)} %copy-done.7, bf16[2048,1024]{1,0:T(8,128)(2,1)S(1)} %collective-permute-done.18.w_oth), custom_call_target="tpu_custom_call" | custom-call | flops 4294967296 | bytes 13631488 | tf_op jit(solution)/shard_map/input_grad/pallas_call | solution.py:400
  (30 shorter events, 0.1 us)
Async XLA Ops:
  7.2 139.9 %all-gather.2.cloned.1.call-start = ((), (), s32[]{:S(2)}) async-start(), calls=%async_computation.1 | async-start | bytes 4456448 | tf_op jit(solution)/shard_map/all_gather | solution.py:357
  7.4 2.2 %copy-start = (bf16[512,4096]{1,0:T(8,128)(2,1)S(1)}, bf16[512,4096]{1,0:T(8,128)(2,1)}, u32[]{:S(2)}) copy-start(bf16[512,4096]{1,0:T(8,128)(2,1)} %t3.5) | copy-start | bytes 12582916
  9.6 1.2 copy-start.4
  10.8 2.4 %copy-start.16 = (s32[32]{0:T(128)}, s32[32]{0:T(128)S(1)}, u32[]{:S(2)}) copy-start(s32[32]{0:T(128)S(1)} %stack.131.idx) | copy-start | bytes 388
  10.8 2.4 %copy-start.8 = (bf16[256,1024]{1,0:T(8,128)(2,1)S(1)}, bf16[256,1024]{1,0:T(8,128)(2,1)}, u32[]{:S(2)}) copy-start(bf16[256,1024]{1,0:T(8,128)(2,1)} %w.1) | copy-start | bytes 1572868
  14.0 2.0 %copy-start.2 = (f32[1024,1024]{1,0:T(8,128)}, f32[1024,1024]{1,0:T(8,128)S(1)}, u32[]{:S(2)}) copy-start(f32[1024,1024]{1,0:T(8,128)S(1)} %own.1.after.keep) | copy-start | bytes 12582916
  16.1 13.3 %copy-start.1 = (bf16[512,4096]{1,0:T(8,128)(2,1)S(1)}, bf16[512,4096]{1,0:T(8,128)(2,1)}, u32[]{:S(2)}) copy-start(bf16[512,4096]{1,0:T(8,128)(2,1)} %t3.5) | copy-start | bytes 12582916
  16.1 13.2 %copy-start.5 = (bf16[512,1024]{1,0:T(8,128)(2,1)S(1)}, bf16[512,1024]{1,0:T(8,128)(2,1)}, u32[]{:S(2)}) copy-start(bf16[512,1024]{1,0:T(8,128)(2,1)} %c.7) | copy-start | bytes 3145732
  16.1 13.2 %copy-start.17 = (s32[32]{0:T(128)S(1)}, s32[32]{0:T(128)}, u32[]{:S(2)}) copy-start(s32[32]{0:T(128)} %copy-done.16) | copy-start | bytes 388
  23.1 14.8 %collective-permute-start.2 = (s16[272,1024]{1,0:T(8,128)(2,1)}, s16[272,1024]{1,0:T(8,128)(2,1)S(1)}, u32[]{:S(2)}, u32[]{:S(2)}) collective-permute-start(s16[272,1024]{1,0:T(8,128)(2,1)} %get-tuple-element.28), channel_id=1, source_target_pairs={{0,4},{4,8},{8,12},{12,0},{1,5},{5,9},{9,13},{13,1},{2,6},{6,10},{... | collective-permute-start | bytes 1671176 | tf_op jit(solution)/shard_map/ppermute | solution.py:257
  25.1 16.8 %collective-permute-start.3 = (s16[272,1024]{1,0:T(8,128)(2,1)}, s16[272,1024]{1,0:T(8,128)(2,1)S(1)}, u32[]{:S(2)}, u32[]{:S(2)}) collective-permute-start(s16[272,1024]{1,0:T(8,128)(2,1)} %get-tuple-element.29), channel_id=1, source_target_pairs={{0,12},{4,0},{8,4},{12,8},{1,13},{5,1},{9,5},{13,9},{2,14},{6,2},{... | collective-permute-start | bytes 1671176 | tf_op jit(solution)/shard_map/ppermute | solution.py:257
  26.5 17.4 %collective-permute-start.4 = (s16[272,1024]{1,0:T(8,128)(2,1)}, s16[272,1024]{1,0:T(8,128)(2,1)S(1)}, u32[]{:S(2)}, u32[]{:S(2)}) collective-permute-start(s16[272,1024]{1,0:T(8,128)(2,1)} %get-tuple-element.30), channel_id=1, source_target_pairs={{0,1},{1,2},{2,3},{3,0},{4,5},{5,6},{6,7},{7,4},{8,9},{9,10},{10,1... | collective-permute-start | bytes 1671176 | tf_op jit(solution)/shard_map/ppermute | solution.py:257
  27.9 18.2 %collective-permute-start.5 = (s16[272,1024]{1,0:T(8,128)(2,1)}, s16[272,1024]{1,0:T(8,128)(2,1)S(1)}, u32[]{:S(2)}, u32[]{:S(2)}) collective-permute-start(s16[272,1024]{1,0:T(8,128)(2,1)} %get-tuple-element.31), channel_id=1, source_target_pairs={{0,3},{1,0},{2,1},{3,2},{4,7},{5,4},{6,5},{7,6},{8,11},{9,8},{10,9... | collective-permute-start | bytes 1671176 | tf_op jit(solution)/shard_map/ppermute | solution.py:257
  29.3 0.8 copy-start.13
  37.6 47.2 %copy-start.3 = (f32[1024,1024]{1,0:T(8,128)S(1)}, f32[1024,1024]{1,0:T(8,128)}, u32[]{:S(2)}) copy-start(f32[1024,1024]{1,0:T(8,128)} %copy-done.2) | copy-start | bytes 12582916
  37.6 16.5 %collective-permute-start = (s16[272,1024]{1,0:T(8,128)(2,1)}, s16[272,1024]{1,0:T(8,128)(2,1)S(1)}, u32[]{:S(2)}, u32[]{:S(2)}) collective-permute-start(s16[272,1024]{1,0:T(8,128)(2,1)} %get-tuple-element.25), channel_id=1, source_target_pairs={{0,4},{4,8},{8,12},{12,0},{1,5},{5,9},{9,13},{13,1},{2,6},{6,10},{... | collective-permute-start | bytes 1671176 | tf_op jit(solution)/shard_map/ppermute | solution.py:257
  37.9 19.9 %collective-permute-start.1 = (s16[272,1024]{1,0:T(8,128)(2,1)}, s16[272,1024]{1,0:T(8,128)(2,1)S(1)}, u32[]{:S(2)}, u32[]{:S(2)}) collective-permute-start(s16[272,1024]{1,0:T(8,128)(2,1)} %get-tuple-element.26), channel_id=1, source_target_pairs={{0,12},{4,0},{8,4},{12,8},{1,13},{5,1},{9,5},{13,9},{2,14},{6,2},{... | collective-permute-start | bytes 1671176 | tf_op jit(solution)/shard_map/ppermute | solution.py:257
  42.0 15.8 %collective-permute-start.8 = (s16[272,1024]{1,0:T(8,128)(2,1)}, s16[272,1024]{1,0:T(8,128)(2,1)S(1)}, u32[]{:S(2)}, u32[]{:S(2)}) collective-permute-start(s16[272,1024]{1,0:T(8,128)(2,1)} %get-tuple-element.34), channel_id=1, source_target_pairs={{0,1},{1,2},{2,3},{3,0},{4,5},{5,6},{6,7},{7,4},{8,9},{9,10},{10,1... | collective-permute-start | bytes 1671176 | tf_op jit(solution)/shard_map/ppermute | solution.py:257
  43.9 16.6 %collective-permute-start.9 = (s16[272,1024]{1,0:T(8,128)(2,1)}, s16[272,1024]{1,0:T(8,128)(2,1)S(1)}, u32[]{:S(2)}, u32[]{:S(2)}) collective-permute-start(s16[272,1024]{1,0:T(8,128)(2,1)} %get-tuple-element.35), channel_id=1, source_target_pairs={{0,3},{1,0},{2,1},{3,2},{4,7},{5,4},{6,5},{7,6},{8,11},{9,8},{10,9... | collective-permute-start | bytes 1671176 | tf_op jit(solution)/shard_map/ppermute | solution.py:257
  50.1 23.3 %collective-permute-start.10 = (s16[272,1024]{1,0:T(8,128)(2,1)}, s16[272,1024]{1,0:T(8,128)(2,1)S(1)}, u32[]{:S(2)}, u32[]{:S(2)}) collective-permute-start(s16[272,1024]{1,0:T(8,128)(2,1)} %get-tuple-element.36), channel_id=1, source_target_pairs={{0,1},{1,2},{2,3},{3,0},{4,5},{5,6},{6,7},{7,4},{8,9},{9,10},{10,1... | collective-permute-start | bytes 1671176 | tf_op jit(solution)/shard_map/ppermute | solution.py:257
  54.0 28.0 %collective-permute-start.11 = (s16[272,1024]{1,0:T(8,128)(2,1)}, s16[272,1024]{1,0:T(8,128)(2,1)S(1)}, u32[]{:S(2)}, u32[]{:S(2)}) collective-permute-start(s16[272,1024]{1,0:T(8,128)(2,1)} %get-tuple-element.37), channel_id=1, source_target_pairs={{0,3},{1,0},{2,1},{3,2},{4,7},{5,4},{6,5},{7,6},{8,11},{9,8},{10,9... | collective-permute-start | bytes 1671176 | tf_op jit(solution)/shard_map/ppermute | solution.py:257
  57.7 27.1 %collective-permute-start.6 = (s16[272,1024]{1,0:T(8,128)(2,1)}, s16[272,1024]{1,0:T(8,128)(2,1)S(1)}, u32[]{:S(2)}, u32[]{:S(2)}) collective-permute-start(s16[272,1024]{1,0:T(8,128)(2,1)} %get-tuple-element.32), channel_id=1, source_target_pairs={{0,4},{4,8},{8,12},{12,0},{1,5},{5,9},{9,13},{13,1},{2,6},{6,10},{... | collective-permute-start | bytes 1671176 | tf_op jit(solution)/shard_map/ppermute | solution.py:257
  57.7 52.1 %copy-start.6 = (s32[256,1024]{1,0:T(8,128)S(1)}, s32[256,1024]{1,0:T(8,128)}, u32[]{:S(2)}) copy-start(s32[256,1024]{1,0:T(8,128)} %signs.3) | copy-start | bytes 3145732
  57.7 52.1 %copy-start.14 = (bf16[128,128]{1,0:T(8,128)(2,1)S(1)}, bf16[128,128]{1,0:T(8,128)(2,1)}, u32[]{:S(2)}) copy-start(bf16[128,128]{1,0:T(8,128)(2,1)} %constant.177.clone.inner) | copy-start | bytes 98308
  57.8 52.1 %copy-start.15 = (bf16[128,128]{1,0:T(8,128)(2,1)S(1)}, bf16[128,128]{1,0:T(8,128)(2,1)}, u32[]{:S(2)}) copy-start(bf16[128,128]{1,0:T(8,128)(2,1)} %constant.178.clone.rows) | copy-start | bytes 98308
  57.8 27.0 %collective-permute-start.7 = (s16[272,1024]{1,0:T(8,128)(2,1)}, s16[272,1024]{1,0:T(8,128)(2,1)S(1)}, u32[]{:S(2)}, u32[]{:S(2)}) collective-permute-start(s16[272,1024]{1,0:T(8,128)(2,1)} %get-tuple-element.33), channel_id=1, source_target_pairs={{0,12},{4,0},{8,4},{12,8},{1,13},{5,1},{9,5},{13,9},{2,14},{6,2},{... | collective-permute-start | bytes 1671176 | tf_op jit(solution)/shard_map/ppermute | solution.py:257
  89.0 56.4 %copy-start.18 = (bf16[16,16]{1,0:T(8,128)(2,1)S(1)}, bf16[16,16]{1,0:T(8,128)(2,1)}, u32[]{:S(2)}) copy-start(bf16[16,16]{1,0:T(8,128)(2,1)} %constant.179.clone.rows) | copy-start | bytes 1540
  89.0 10.9 %collective-permute-start.12 = (s16[144,1024]{1,0:T(8,128)(2,1)}, s16[144,1024]{1,0:T(8,128)(2,1)S(1)}, u32[]{:S(2)}, u32[]{:S(2)}) collective-permute-start(s16[144,1024]{1,0:T(8,128)(2,1)} %get-tuple-element.40), channel_id=1, source_target_pairs={{0,1},{1,2},{2,3},{3,0},{4,5},{5,6},{6,7},{7,4},{8,9},{9,10},{10,1... | collective-permute-start | bytes 884744 | tf_op jit(solution)/shard_map/ppermute | solution.py:257
  89.0 12.9 %collective-permute-start.13 = (s16[144,1024]{1,0:T(8,128)(2,1)}, s16[144,1024]{1,0:T(8,128)(2,1)S(1)}, u32[]{:S(2)}, u32[]{:S(2)}) collective-permute-start(s16[144,1024]{1,0:T(8,128)(2,1)} %get-tuple-element.41), channel_id=1, source_target_pairs={{0,2},{1,3},{2,0},{3,1},{4,6},{5,7},{6,4},{7,5},{8,10},{9,11},{10,... | collective-permute-start | bytes 884744 | tf_op jit(solution)/shard_map/ppermute | solution.py:257
  90.9 11.1 %collective-permute-start.14 = (s16[144,1024]{1,0:T(8,128)(2,1)}, s16[144,1024]{1,0:T(8,128)(2,1)S(1)}, u32[]{:S(2)}, u32[]{:S(2)}) collective-permute-start(s16[144,1024]{1,0:T(8,128)(2,1)} %get-tuple-element.42), channel_id=1, source_target_pairs={{0,3},{1,0},{2,1},{3,2},{4,7},{5,4},{6,5},{7,6},{8,11},{9,8},{10,9... | collective-permute-start | bytes 884744 | tf_op jit(solution)/shard_map/ppermute | solution.py:257
  91.7 10.4 %collective-permute-start.15 = (s16[144,1024]{1,0:T(8,128)(2,1)}, s16[144,1024]{1,0:T(8,128)(2,1)S(1)}, u32[]{:S(2)}, u32[]{:S(2)}) collective-permute-start(s16[144,1024]{1,0:T(8,128)(2,1)} %get-tuple-element.43), channel_id=1, source_target_pairs={{0,4},{4,8},{8,12},{12,0},{1,5},{5,9},{9,13},{13,1},{2,6},{6,10},{... | collective-permute-start | bytes 884744 | tf_op jit(solution)/shard_map/ppermute | solution.py:257
  91.7 10.4 %collective-permute-start.16 = (s16[144,1024]{1,0:T(8,128)(2,1)}, s16[144,1024]{1,0:T(8,128)(2,1)S(1)}, u32[]{:S(2)}, u32[]{:S(2)}) collective-permute-start(s16[144,1024]{1,0:T(8,128)(2,1)} %get-tuple-element.44), channel_id=1, source_target_pairs={{0,8},{4,12},{8,0},{12,4},{1,9},{5,13},{9,1},{13,5},{2,10},{6,14},... | collective-permute-start | bytes 884744 | tf_op jit(solution)/shard_map/ppermute | solution.py:257
  99.9 9.9 %collective-permute-start.17 = (s16[144,1024]{1,0:T(8,128)(2,1)}, s16[144,1024]{1,0:T(8,128)(2,1)S(1)}, u32[]{:S(2)}, u32[]{:S(2)}) collective-permute-start(s16[144,1024]{1,0:T(8,128)(2,1)} %get-tuple-element.45), channel_id=1, source_target_pairs={{0,12},{4,0},{8,4},{12,8},{1,13},{5,1},{9,5},{13,9},{2,14},{6,2},{... | collective-permute-start | bytes 884744 | tf_op jit(solution)/shard_map/ppermute | solution.py:257
  109.8 1.0 copy-start.9
  110.9 1.0 copy-start.10
  114.8 30.6 %all-to-all-start = ((s16[16,16,1152]{2,1,0:T(8,128)(2,1)}), s16[16,16,1152]{2,1,0:T(8,128)(2,1)S(1)}, u32[]{:S(2)}, u32[]{:S(2)}) async-start(s16[16,16,1152]{2,1,0:T(8,128)(2,1)} %bitcast.34), calls=%async_computation | async-start | bytes 1179648 | tf_op jit(solution)/shard_map/all_to_all | solution.py:370
  146.4 0.6 copy-start.11
  147.0 0.8 copy-start.12
  147.0 18.0 %collective-permute-start.18 = (bf16[2048,1024]{1,0:T(8,128)(2,1)}, bf16[2048,1024]{1,0:T(8,128)(2,1)S(1)}, u32[]{:S(2)}, u32[]{:S(2)}) collective-permute-start(bf16[2048,1024]{1,0:T(8,128)(2,1)} %tie.1.w_own), channel_id=1, source_target_pairs={{0,16},{16,0},{1,17},{17,1},{2,18},{18,2},{3,19},{19,3},{4,20},{20... | collective-permute-start | bytes 12582920 | tf_op jit(solution)/shard_map/ppermute | solution.py:389
  165.1 2.2 %copy-start.7 = (bf16[2048,1024]{1,0:T(8,128)(2,1)S(1)}, bf16[2048,1024]{1,0:T(8,128)(2,1)}, u32[]{:S(2)}) copy-start(bf16[2048,1024]{1,0:T(8,128)(2,1)} %tie.1.w_own) | copy-start | bytes 12582916
Sparse Core Ops, SparseCore 0:
  16.2 74.5 all-gather.1

commit v4 on v3

--- a/solution.py
+++ b/solution.py
@@ -182,7 +182,7 @@
         out[here, KV : KV + 128] = jnp.broadcast_to(e, (128, 128)).astype(I32).astype(I16)
 
 
-def levels_kernel(count, x, inner, rows, out):
+def levels_kernel(count, x, inner, rows, after, out):
     level = count[0].astype(F32)
 
     def group(g):
@@ -214,11 +214,12 @@
     out[...] = signs[...].astype(F32) * (to_float(q[:, 0:KV]) * power(e))
 
 
-def input_grad_kernel(core, c, w_own, w_oth, out, w):
-    for k in range(4):
-        rows = slice(k * 128, k * 128 + 128)
-        w[pl.ds(pl.multiple_of(k * 256 + core[0] * 128, 128), 128), :] = w_own[rows, :]
-        w[pl.ds(pl.multiple_of(k * 256 + 128 - core[0] * 128, 128), 128), :] = w_oth[rows, :]
+def input_grad_kernel(at, c, w_own, w_oth, out, w):
+    for j in range(4):
+        chip = ((at[1] + 4 - j) % 4) * 256
+        for z in range(NZ):
+            w[pl.ds(pl.multiple_of(chip + z * 32 + at[2] * 16, 16), 16), :] = w_own[z, j, 0]
+            w[pl.ds(pl.multiple_of(chip + z * 32 + 16 - at[2] * 16, 16), 16), :] = w_oth[z, j, 0]
     out[...] = lax.dot_general(c[...], w[...], (((1,), (1,)), ((), ())), preferred_element_type=F32).astype(BF16)
 
 
@@ -226,8 +227,15 @@
     del w, after, out
 
 
-def half_kernel(core, w, after, out):
-    out[...] = w[...]
+def tie(v, after):
+    return pl.pallas_call(
+        tie_kernel,
+        out_shape=jax.ShapeDtypeStruct(v.shape, v.dtype),
+        in_specs=[pl.BlockSpec(memory_space=pl.ANY)] * 2,
+        out_specs=pl.BlockSpec(memory_space=pl.ANY),
+        input_output_aliases={0: 0},
+        name="tie",
+    )(v, after)
 
 
 def params(limit=VMEM):
@@ -251,6 +259,7 @@
     x, y = lax.axis_index("x").astype(I32), lax.axis_index("y").astype(I32)
     sds = jax.ShapeDtypeStruct
     anywhere = pl.BlockSpec(memory_space=pl.ANY)
+    in_hbm = lambda v: pltpu.with_memory_space_constraint(v, pltpu.HBM)
     in_vmem = pl.BlockSpec(memory_space=pltpu.VMEM)
 
     def send(v, axis, s):
@@ -264,6 +273,14 @@
                 ty = (y + (dp if axis else dq)) % NY
                 ids.append(2 * (tx * NY + ty) + axis)
     idx = jnp.stack(ids).astype(I32)
+
+    z = lax.axis_index("z").astype(I32)
+
+    def spread(piece, axis):
+        return [lax.ppermute(piece, axis, shift(4, s)) for s in (1, 2, 3)]
+
+    piece = lax.dynamic_slice_in_dim(value_weights, (2 * z + core) * 16, 16, 0)
+    round1 = spread(piece, "x")
 
     def operands(where):
         tiles = [pl.BlockSpec((TOK, 128), lambda k, ids, t=t: (0, ids[where(k) + t])) for t in range(4)]
@@ -288,6 +305,10 @@
     )(idx, *inputs)
     got1 = [send(up1x, 0, 1), send(down1x, 0, -1), send(up1y, 1, 1), send(down1y, 1, -1)]
 
+    piece = jnp.concatenate([piece, tie(round1[0], up1x)] + round1[1:], 0)
+    piece = jnp.concatenate([piece] + spread(piece, "y"), 0)
+    w_own = lax.all_gather(piece, "z", axis=0, tiled=True)
+
     up2x, down2x, up2y, down2y, keep_near = pl.pallas_call(
         near_kernel,
         out_shape=(message,) * 4 + (sds((1024, KV), F32),),
@@ -297,7 +318,7 @@
             in_specs=operands(lambda k: 16 * (k // 2) + 4 + 8 * (k % 2)) + [whole((8, KV))],
             out_specs=(whole((272, KV)),) * 4 + (pl.BlockSpec((256, KV), lambda k, ids: (k, 0)),),
         ),
-        compiler_params=params(SMALL),
+        compiler_params=params(),
         cost_estimate=cost(2 * mm, 11 << 20),
         name="near",
     )(idx, *inputs, ce)
@@ -342,20 +363,6 @@
     own_x, x1, x2, x3, own_y, y1, y2, y3 = parts
     last = [send(x1, 1, 1), send(x2, 1, 2), send(x3, 1, -1), send(y1, 0, 1), send(y2, 0, 2), send(y3, 0, -1)]
 
-    half_w = pl.pallas_call(
-        half_kernel,
-        out_shape=pltpu.HBM((128, KV), BF16),
-        grid_spec=pltpu.PrefetchScalarGridSpec(
-            num_scalar_prefetch=1,
-            grid=(1,),
-            in_specs=[pl.BlockSpec((128, KV), lambda k, c: (c[0], 0)), anywhere],
-            out_specs=whole((128, KV)),
-        ),
-        compiler_params=params(SMALL),
-        name="half",
-    )(core.reshape(1), value_weights, keep)
-    w_own = lax.all_gather(half_w, ("x", "y"), axis=0, tiled=True)
-
     inner = jnp.asarray(hadamard(128), BF16)
     quad = hadamard(4)
     spun = pl.pallas_call(
@@ -366,27 +373,37 @@
         compiler_params=params(SMALL),
         cost_estimate=cost(1 << 28, 4 << 20),
         name="rotate",
-    )(own_x, own_y, *last, sign_flips, inner, jnp.asarray(np.kron(np.eye(32), quad), BF16))
+    )(in_hbm(own_x), in_hbm(own_y), *last, sign_flips, inner, jnp.asarray(np.kron(np.eye(32), quad), BF16))
     groups = lax.all_to_all(spun, ("z", "core"), 0, 0, tiled=True)
+
+    w_own = tie(w_own, spun)
+    w_oth = lax.ppermute(w_own, "core", shift(NC, 1))
+    place = jnp.stack([x, y, core]).astype(I32)
+    w_block = pl.BlockSpec((NZ, 4, 1, 16, KV), lambda k, at: (0, 0, k, 0, 0))
+    input_grad = pl.pallas_call(
+        input_grad_kernel,
+        out_shape=pltpu.HBM((TOK, 4096), BF16),
+        grid_spec=pltpu.PrefetchScalarGridSpec(
+            num_scalar_prefetch=1,
+            grid=(4,),
+            in_specs=[whole((TOK, KV)), w_block, w_block],
+            out_specs=pl.BlockSpec((TOK, 1024), lambda k, at: (0, (at[0] + 4 - k) % 4)),
+            scratch_shapes=[pltpu.VMEM((1024, KV), BF16)],
+        ),
+        compiler_params=params(SMALL),
+        cost_estimate=cost(4 * mm, 13 << 20),
+        name="input_grad",
+    )(place, cotangent, w_own.reshape(NZ, 4, 4, 16, KV), w_oth.reshape(NZ, 4, 4, 16, KV))
 
     back = pl.pallas_call(
         levels_kernel,
         out_shape=sds((16, KV + 128), I16),
-        in_specs=[pl.BlockSpec(memory_space=pltpu.SMEM)] + [in_vmem] * 3,
+        in_specs=[pl.BlockSpec(memory_space=pltpu.SMEM)] + [in_vmem] * 3 + [anywhere],
         out_specs=in_vmem,
         compiler_params=params(SMALL),
         cost_estimate=cost(1 << 26, 1 << 20),
         name="levels",
-    )(level_count.reshape(1), groups, inner, jnp.asarray(np.kron(np.eye(4), quad), BF16))
-    w_own = pl.pallas_call(
-        tie_kernel,
-        out_shape=sds((2048, KV), BF16),
-        in_specs=[anywhere] * 2,
-        out_specs=anywhere,
-        input_output_aliases={0: 0},
-        name="tie",
-    )(w_own, back)
-    w_oth = lax.ppermute(w_own, "core", shift(NC, 1))
+    )(level_count.reshape(1), groups, inner, jnp.asarray(np.kron(np.eye(4), quad), BF16), in_hbm(input_grad))
     gathered = lax.all_gather(back, ("z", "core"), axis=0, tiled=True)
     weight_grad = pl.pallas_call(
         finish_kernel,
@@ -397,25 +414,6 @@
         cost_estimate=cost(1 << 20, 3 << 20),
         name="finish",
     )(gathered, sign_flips)
-    input_grad = pl.pallas_call(
-        input_grad_kernel,
-        out_shape=pltpu.HBM((TOK, 4096), BF16),
-        grid_spec=pltpu.PrefetchScalarGridSpec(
-            num_scalar_prefetch=1,
-            grid=(4,),
-            in_specs=[
-                whole((TOK, KV)),
-                pl.BlockSpec((512, KV), lambda k, c: (k, 0)),
-                pl.BlockSpec((512, KV), lambda k, c: (k, 0)),
-            ],
-            out_specs=pl.BlockSpec((TOK, 1024), lambda k, c: (0, k)),
-            scratch_shapes=[pltpu.VMEM((1024, KV), BF16)],
-        ),
-        compiler_params=params(SMALL),
-        cost_estimate=cost(4 * mm, 13 << 20),
-        name="input_grad",
-    )(core.reshape(1), cotangent, w_own, w_oth)
-
     return (input_grad, weight_grad)
 
 

time: 181 us -> 161 us (0.89)
  waiting for transfers between devices: 60.1 us -> 30.4 us
  starting transfers between devices: 40.1 us -> 48.5 us
  local copies, waits for them, and re-layouts: 12 us -> 8.19 us
  Pallas kernels: 37.7 us -> 41.4 us
    ppermute x18, waiting for transfers between devices: 42 us -> 20.3 us  [send(): return lax.ppermute(v, 'xy'[axis], shift((NX, NY)[axis], s))]
    all_to_all x1, waiting for transfers between devices: 18 us -> 6.89 us  [shards(): groups = lax.all_to_all(spun, ('z', 'core'), 0, 0, tiled=True)]
    ppermute x0 -> x6, starting transfers between devices: none -> 10.7 us  [spread(): return [lax.ppermute(piece, axis, shift(4, s)) for s in (1, 2, 3)]]
    ppermute x1, starting transfers between devices: 0.01 us -> 5.53 us  [shards(): w_oth = lax.ppermute(w_own, 'core', shift(NC, 1))]
    ppermute x18, starting transfers between devices: 28.1 us -> 23.6 us  [send(): return lax.ppermute(v, 'xy'[axis], shift((NX, NY)[axis], s))]
    unnamed x38 -> x30, local copies, waits for them, and re-layouts: 11.9 us -> 7.48 us
    all_to_all x1, starting transfers between devices: 11.9 us -> 8.59 us  [shards(): groups = lax.all_to_all(spun, ('z', 'core'), 0, 0, tiled=True)]
    ppermute x0 -> x6, waiting for transfers between devices: none -> 3.22 us  [spread(): return [lax.ppermute(piece, axis, shift(4, s)) for s in (1, 2, 3)]]
  transfers between devices with their start and end apart: 21 -> 27, of which waited for: 9 -> 10; matrix products, arithmetic and copies ran while one was open for 0% -> 1% of each run, Pallas kernels for 15% -> 24%
where the time goes in v4:
time: 161 us; the launch traced here: 160 us
  starting transfers between devices  48.5 us (30%)
  Pallas kernels  41.4 us (26%)
  waiting for transfers between devices  30.4 us (19%)
  blocking collectives  16.1 us (10%)
  between operations  14.9 us (9%)
  local copies, waits for them, and re-layouts  8.19 us (5%)
    ppermute x18, starting transfers between devices, send(): return lax.ppermute(v, 'xy'[axis], shift((NX, NY)[axis], s))  23.6 us
    ppermute x18, waiting for transfers between devices, send(): return lax.ppermute(v, 'xy'[axis], shift((NX, NY)[axis], s))  20.3 us
    all_gather x1, blocking collectives, shards(): gathered = lax.all_gather(back, ('z', 'core'), axis=0, tiled=True)  16.1 us
    ppermute x6, starting transfers between devices, spread(): return [lax.ppermute(piece, axis, shift(4, s)) for s in (1, 2, 3)]  10.7 us
    pallas_call x1, Pallas kernels, shards(): pl.pallas_call(near_kernel, out_shape=(message,) * 4 + (sds((1024, KV), F...  9.23 us
    pallas_call x1, Pallas kernels, shards(): pl.pallas_call(input_grad_kernel, out_shape=pltpu.HBM((TOK, 4096), BF16),...  8.84 us
    all_to_all x1, starting transfers between devices, shards(): groups = lax.all_to_all(spun, ('z', 'core'), 0, 0, tiled=True)  8.59 us
    unnamed x30, local copies, waits for them, and re-layouts  7.48 us
  transfers between devices with their start and end apart: 27, of which 10 were waited for; matrix products, arithmetic and copies ran while one was open for 1% of the time, Pallas kernels for 24%

profile of v4, /device:TPU:1, one launch (start us, length us, event | category | flops | bytes accessed | tf_op | source)
XLA Modules:
  0.0 160.3 jit_solution(6410695709859740441)
XLA Ops:
  7.2 0.0 all-gather.2.cloned.1.call-start
  7.2 0.8 constant_dynamic-update-slice_fusion.6
  8.0 2.0 %collective-permute-start = (bf16[16,1024]{1,0:T(8,128)(2,1)S(1)}, bf16[16,1024]{1,0:T(8,128)(2,1)S(1)}, u32[]{:S(2)}, u32[]{:S(2)}) collective-permute-start(bf16[16,1024]{1,0:T(8,128)(2,1)S(1)} %get-tuple-element.47), channel_id=1, source_target_pairs={{0,4},{4,8},{8,12},{12,0},{1,5},{5,9},{9,13},{13,1},{2,6},{6,10},{... | collective-permute-start | bytes 98312 | tf_op jit(solution)/shard_map/ppermute | solution.py:280
  10.0 2.5 %collective-permute-start.1 = (bf16[16,1024]{1,0:T(8,128)(2,1)S(1)}, bf16[16,1024]{1,0:T(8,128)(2,1)S(1)}, u32[]{:S(2)}, u32[]{:S(2)}) collective-permute-start(bf16[16,1024]{1,0:T(8,128)(2,1)S(1)} %get-tuple-element.47), channel_id=1, source_target_pairs={{0,8},{4,12},{8,0},{12,4},{1,9},{5,13},{9,1},{13,5},{2,10},{6,14},... | collective-permute-start | bytes 98312 | tf_op jit(solution)/shard_map/ppermute | solution.py:280
  12.5 1.2 collective-permute-start.2
  13.6 0.7 stack.147.idx
  14.3 6.4 %far.1 = (s16[272,1024]{1,0:T(8,128)(2,1)}, s16[272,1024]{1,0:T(8,128)(2,1)}, s16[272,1024]{1,0:T(8,128)(2,1)}, s16[272,1024]{1,0:T(8,128)(2,1)}, f32[8,1024]{1,0:T(8,128)}) custom-call(s32[32]{0:T(128)} %stack.147.idx, bf16[512,4096]{1,0:T(8,128)(2,1)} %t3.5, bf16[512,4096]{1,0:T(8,128)(2,1)} %t3.5, bf16[512,4096]{1,0:T(8,128)(2,1)} %t3.5, ...), custom_call_target="tpu_custom_call" | custom-call | flops 1073741824 | bytes 6291456 | tf_op jit(solution)/shard_map/far/pallas_call | solution.py:293
  20.8 0.0 collective-permute-done.w
  20.8 0.0 copy-start.11
  20.8 0.6 copy-done.11
  21.4 0.0 collective-permute-done.1
  21.4 0.0 collective-permute-done.2
  21.4 0.8 pad_maximum_fusion
  22.2 1.4 collective-permute-start.3
  23.5 2.6 %collective-permute-start.4 = (bf16[64,1024]{1,0:T(8,128)(2,1)S(1)}, bf16[64,1024]{1,0:T(8,128)(2,1)S(1)}, u32[]{:S(2)}, u32[]{:S(2)}) collective-permute-start(bf16[64,1024]{1,0:T(8,128)(2,1)S(1)} %pad_maximum_fusion), channel_id=1, source_target_pairs={{0,2},{1,3},{2,0},{3,1},{4,6},{5,7},{6,4},{7,5},{8,10},{9,11},{10,... | collective-permute-start | bytes 393224 | tf_op jit(solution)/shard_map/ppermute | solution.py:280
  26.2 1.1 collective-permute-start.5
  27.2 0.8 constant_dynamic-update-slice_fusion.5
  28.0 0.0 collective-permute-done.3
  28.0 2.6 %collective-permute-done.4 = bf16[64,1024]{1,0:T(8,128)(2,1)S(1)} collective-permute-done((bf16[64,1024]{1,0:T(8,128)(2,1)S(1)}, bf16[64,1024]{1,0:T(8,128)(2,1)S(1)}, u32[]{:S(2)}, u32[]{:S(2)}) %collective-permute-start.4) | collective-permute-done | bytes 131104 | tf_op jit(solution)/shard_map/ppermute | solution.py:280
  30.7 0.6 collective-permute-done.5
  31.3 0.9 copy-done.10
  32.2 0.0 all-gather.2.cloned.1.call-update
  32.2 0.5 collective-permute-start.10
  32.7 2.2 %collective-permute-start.11 = (s16[272,1024]{1,0:T(8,128)(2,1)}, s16[272,1024]{1,0:T(8,128)(2,1)S(1)}, u32[]{:S(2)}, u32[]{:S(2)}) collective-permute-start(s16[272,1024]{1,0:T(8,128)(2,1)} %get-tuple-element.31), channel_id=1, source_target_pairs={{0,3},{1,0},{2,1},{3,2},{4,7},{5,4},{6,5},{7,6},{8,11},{9,8},{10,9... | collective-permute-start | bytes 1671176 | tf_op jit(solution)/shard_map/ppermute | solution.py:266
  34.9 0.3 collective-permute-start.8
  35.2 2.4 %collective-permute-start.9 = (s16[272,1024]{1,0:T(8,128)(2,1)}, s16[272,1024]{1,0:T(8,128)(2,1)S(1)}, u32[]{:S(2)}, u32[]{:S(2)}) collective-permute-start(s16[272,1024]{1,0:T(8,128)(2,1)} %get-tuple-element.29), channel_id=1, source_target_pairs={{0,12},{4,0},{8,4},{12,8},{1,13},{5,1},{9,5},{13,9},{2,14},{6,2},{... | collective-permute-start | bytes 1671176 | tf_op jit(solution)/shard_map/ppermute | solution.py:266
  37.6 9.2 %near.1 = (s16[272,1024]{1,0:T(8,128)(2,1)}, s16[272,1024]{1,0:T(8,128)(2,1)}, s16[272,1024]{1,0:T(8,128)(2,1)}, s16[272,1024]{1,0:T(8,128)(2,1)}, f32[1024,1024]{1,0:T(8,128)}) custom-call(s32[32]{0:T(128)} %stack.147.idx, bf16[512,4096]{1,0:T(8,128)(2,1)} %t3.5, bf16[512,4096]{1,0:T(8,128)(2,1)} %t3.5, bf16[512,4096]{1,0:T(8,128)(2,1)} %t3.5, ...), custom_call_target="tpu_custom_call" | custom-call | flops 2147483648 | bytes 11534336 | tf_op jit(solution)/shard_map/near/pallas_call | solution.py:312
  46.8 0.0 copy-start.1
  46.9 0.3 collective-permute-start.14
  47.1 2.7 %collective-permute-start.15 = (s16[272,1024]{1,0:T(8,128)(2,1)}, s16[272,1024]{1,0:T(8,128)(2,1)S(1)}, u32[]{:S(2)}, u32[]{:S(2)}) collective-permute-start(s16[272,1024]{1,0:T(8,128)(2,1)} %get-tuple-element.35), channel_id=1, source_target_pairs={{0,3},{1,0},{2,1},{3,2},{4,7},{5,4},{6,5},{7,6},{8,11},{9,8},{10,9... | collective-permute-start | bytes 1671176 | tf_op jit(solution)/shard_map/ppermute | solution.py:266
  49.8 0.0 collective-permute-done.11.refs_3_
  49.8 0.0 collective-permute-start.6
  49.8 2.7 %collective-permute-start.7 = (s16[272,1024]{1,0:T(8,128)(2,1)}, s16[272,1024]{1,0:T(8,128)(2,1)S(1)}, u32[]{:S(2)}, u32[]{:S(2)}) collective-permute-start(s16[272,1024]{1,0:T(8,128)(2,1)} %get-tuple-element.27), channel_id=1, source_target_pairs={{0,12},{4,0},{8,4},{12,8},{1,13},{5,1},{9,5},{13,9},{2,14},{6,2},{... | collective-permute-start | bytes 1671176 | tf_op jit(solution)/shard_map/ppermute | solution.py:266
  52.5 2.2 %copy-done.3 = f32[1024,1024]{1,0:T(8,128)S(1)} copy-done((f32[1024,1024]{1,0:T(8,128)S(1)}, f32[1024,1024]{1,0:T(8,128)}, u32[]{:S(2)}) %copy-start.3) | copy-done | bytes 4194328
  54.7 3.9 %relay.1 = (s16[272,1024]{1,0:T(8,128)(2,1)}, s16[272,1024]{1,0:T(8,128)(2,1)}, s16[272,1024]{1,0:T(8,128)(2,1)}, s16[272,1024]{1,0:T(8,128)(2,1)}) custom-call(f32[1024,1024]{1,0:T(8,128)S(1)} %copy-done.3, f32[8,1024]{1,0:T(8,128)S(1)} %copy-done.5, s16[272,1024]{1,0:T(8,128)(2,1)S(1)} %collective-permute-done.8.refs_0_, ...), custom_call_target="tpu_custom_call" | custom-call | flops 1048576 | bytes 8388608 | tf_op jit(solution)/shard_map/relay/pallas_call | solution.py:341
  58.6 0.8 collective-permute-done.14.refs_4_
  59.4 1.9 %collective-permute-start.13 = (s16[272,1024]{1,0:T(8,128)(2,1)}, s16[272,1024]{1,0:T(8,128)(2,1)S(1)}, u32[]{:S(2)}, u32[]{:S(2)}) collective-permute-start(s16[272,1024]{1,0:T(8,128)(2,1)} %get-tuple-element.33), channel_id=1, source_target_pairs={{0,12},{4,0},{8,4},{12,8},{1,13},{5,1},{9,5},{13,9},{2,14},{6,2},{... | collective-permute-start | bytes 1671176 | tf_op jit(solution)/shard_map/ppermute | solution.py:266
  61.3 0.2 collective-permute-done.6.refs_0_
  61.5 2.5 %collective-permute-start.17 = (s16[272,1024]{1,0:T(8,128)(2,1)}, s16[272,1024]{1,0:T(8,128)(2,1)S(1)}, u32[]{:S(2)}, u32[]{:S(2)}) collective-permute-start(s16[272,1024]{1,0:T(8,128)(2,1)} %get-tuple-element.37), channel_id=1, source_target_pairs={{0,3},{1,0},{2,1},{3,2},{4,7},{5,4},{6,5},{7,6},{8,11},{9,8},{10,9... | collective-permute-start | bytes 1671176 | tf_op jit(solution)/shard_map/ppermute | solution.py:266
  64.0 2.4 %own.1.keep = f32[1024,1024]{1,0:T(8,128)S(1)} custom-call(s32[32]{0:T(128)S(1)} %copy-done.8, bf16[512,4096]{1,0:T(8,128)(2,1)S(1)} %copy-done, bf16[512,4096]{1,0:T(8,128)(2,1)S(1)} %copy-done, bf16[512,4096]{1,0:T(8,128)(2,1)S(1)} %copy-done, bf16[512,4096]{1,0:T(8,128)(2,1)S(1)} %copy-done, bf16[512,1024]{1,0:T(8,128)(2,1)S(1)} %copy-done.1), custom_call_target="tpu_custom_call" | custom-call | flops 1073741824 | bytes 8388608 | tf_op jit(solution)/shard_map/own/pallas_call | solution.py:327
  66.4 0.0 copy-start.4
  66.4 0.0 copy-start.6
  66.5 0.0 copy-start.7
  66.5 8.4 %collective-permute-done.12.refs_2_ = s16[272,1024]{1,0:T(8,128)(2,1)S(1)} collective-permute-done((s16[272,1024]{1,0:T(8,128)(2,1)}, s16[272,1024]{1,0:T(8,128)(2,1)S(1)}, u32[]{:S(2)}, u32[]{:S(2)}) %collective-permute-start.12) | collective-permute-done | bytes 557088 | tf_op jit(solution)/shard_map/ppermute | solution.py:266
  74.9 4.3 %cross.1 = (f32[128,1024]{1,0:T(8,128)}, s16[144,1024]{1,0:T(8,128)(2,1)}, s16[144,1024]{1,0:T(8,128)(2,1)}, s16[144,1024]{1,0:T(8,128)(2,1)}, f32[128,1024]{1,0...) custom-call(f32[1024,1024]{1,0:T(8,128)S(1)} %own.1.keep, ...), custom_call_target="tpu_custom_call" | custom-call | flops 1048576 | bytes 12582912 | tf_op jit(solution)/shard_map/cross/pallas_call | solution.py:353
  79.2 0.0 collective-permute-start.18
  79.2 1.3 collective-permute-start.19
  80.4 1.4 collective-permute-start.20
  81.8 3.8 %collective-permute-start.22 = (s16[144,1024]{1,0:T(8,128)(2,1)}, s16[144,1024]{1,0:T(8,128)(2,1)S(1)}, u32[]{:S(2)}, u32[]{:S(2)}) collective-permute-start(s16[144,1024]{1,0:T(8,128)(2,1)} %get-tuple-element.44), channel_id=1, source_target_pairs={{0,8},{4,12},{8,0},{12,4},{1,9},{5,13},{9,1},{13,5},{2,10},{6,14},... | collective-permute-start | bytes 884744 | tf_op jit(solution)/shard_map/ppermute | solution.py:266
  85.7 5.2 %collective-permute-done.18.x1 = s16[144,1024]{1,0:T(8,128)(2,1)S(1)} collective-permute-done((s16[144,1024]{1,0:T(8,128)(2,1)}, s16[144,1024]{1,0:T(8,128)(2,1)S(1)}, u32[]{:S(2)}, u32[]{:S(2)}) %collective-permute-start.18) | collective-permute-done | bytes 294944 | tf_op jit(solution)/shard_map/ppermute | solution.py:266
  90.9 1.7 %collective-permute-start.23 = (s16[144,1024]{1,0:T(8,128)(2,1)}, s16[144,1024]{1,0:T(8,128)(2,1)S(1)}, u32[]{:S(2)}, u32[]{:S(2)}) collective-permute-start(s16[144,1024]{1,0:T(8,128)(2,1)} %get-tuple-element.45), channel_id=1, source_target_pairs={{0,12},{4,0},{8,4},{12,8},{1,13},{5,1},{9,5},{13,9},{2,14},{6,2},{... | collective-permute-start | bytes 884744 | tf_op jit(solution)/shard_map/ppermute | solution.py:266
  92.5 0.9 collective-permute-done.20.x3
  93.4 1.7 %collective-permute-done.22.y2 = s16[144,1024]{1,0:T(8,128)(2,1)S(1)} collective-permute-done((s16[144,1024]{1,0:T(8,128)(2,1)}, s16[144,1024]{1,0:T(8,128)(2,1)S(1)}, u32[]{:S(2)}, u32[]{:S(2)}) %collective-permute-start.22) | collective-permute-done | bytes 294944 | tf_op jit(solution)/shard_map/ppermute | solution.py:266
  95.1 3.2 %collective-permute-done.23.y3 = s16[144,1024]{1,0:T(8,128)(2,1)S(1)} collective-permute-done((s16[144,1024]{1,0:T(8,128)(2,1)}, s16[144,1024]{1,0:T(8,128)(2,1)S(1)}, u32[]{:S(2)}, u32[]{:S(2)}) %collective-permute-start.23) | collective-permute-done | bytes 294944 | tf_op jit(solution)/shard_map/ppermute | solution.py:266
  98.3 4.1 %rotate.1.after = s16[256,1152]{1,0:T(8,128)(2,1)} custom-call(f32[128,1024]{1,0:T(8,128)} %get-tuple-element.38.own_x, f32[128,1024]{1,0:T(8,128)} %get-tuple-element.39.own_y, s16[144,1024]{1,0:T(8,128)(2,1)S(1)} %collective-permute-done.18.x1, s16[144,1024]{1,0:T(8,128)(2,1)S(1)} %collective-permute-done.19.x2, ...), custom_call_target="tpu_custom_call" | custom-call | flops 268435456 | bytes 4194304 | tf_op jit(solution)/shard_map/rotate/pallas_call | solution.py:368
  102.4 5.5 %collective-permute-start.24 = (bf16[2048,1024]{1,0:T(8,128)(2,1)}, bf16[2048,1024]{1,0:T(8,128)(2,1)}, u32[]{:S(2)}, u32[]{:S(2)}) collective-permute-start(bf16[2048,1024]{1,0:T(8,128)(2,1)} %tie.3), channel_id=1, source_target_pairs={{0,16},{16,0},{1,17},{17,1},{2,18},{18,2},{3,19},{19,3},{4,20},{20... | collective-permute-start | bytes 12582920 | tf_op jit(solution)/shard_map/ppermute | solution.py:380
  108.0 8.6 %all-to-all-start = ((s16[16,16,1152]{2,1,0:T(8,128)(2,1)}), s16[16,16,1152]{2,1,0:T(8,128)(2,1)S(1)}, u32[]{:S(2)}, u32[]{:S(2)}) async-start(s16[16,16,1152]{2,1,0:T(8,128)(2,1)} %bitcast.38), calls=%async_computation | async-start | bytes 1179648 | tf_op jit(solution)/shard_map/all_to_all | solution.py:377
  117.2 0.1 pad_add_fusion.at
  117.3 2.2 %copy-done.2 = bf16[2048,1024]{1,0:T(8,128)(2,1)S(1)} copy-done((bf16[2048,1024]{1,0:T(8,128)(2,1)S(1)}, bf16[2048,1024]{1,0:T(8,128)(2,1)}, u32[]{:S(2)}) %copy-start.2) | copy-done | bytes 4194328
  119.5 8.8 %input_grad.1.after = bf16[512,4096]{1,0:T(8,128)(2,1)} custom-call(s32[3]{0:T(128)S(1)} %pad_add_fusion.at, bf16[512,1024]{1,0:T(8,128)(2,1)S(1)} %copy-done.1, bf16[8,4,4,16,1024]{4,3,2,1,0:T(8,128)(2,1)S(1)} %bitcast.41, bf16[8,4,4,16,1024]{4,3,2,1,0:T(8,128)(2,1)} %bitcast.36.w_oth), custom_call_target="tpu_custom_call" | custom-call | flops 4294967296 | bytes 13631488 | tf_op jit(solution)/shard_map/input_grad/pallas_call | solution.py:383
  128.3 6.9 %all-to-all-done = s16[16,16,1152]{2,1,0:T(8,128)(2,1)S(1)} async-done(((s16[16,16,1152]{2,1,0:T(8,128)(2,1)}), s16[16,16,1152]{2,1,0:T(8,128)(2,1)S(1)}, u32[]{:S(2)}, u32[]{:S(2)}) %all-to-all-start) | async-done | bytes 589856 | tf_op jit(solution)/shard_map/all_to_all | solution.py:377
  135.2 1.0 levels.1
  136.2 16.1 %all_gather.7.q = s16[256,1152]{1,0:T(8,128)(2,1)S(1)} all-gather(s16[16,1152]{1,0:T(8,128)(2,1)S(1)} %levels.1), channel_id=1, replica_groups=mesh['z'=8,'core'=2,'x'=4,'y'=4] {'z','core'}, dimensions={0}, use_global_device_ids=true | all-gather | bytes 626688 | tf_op jit(solution)/shard_map/all_gather | solution.py:407
  152.3 1.2 finish.1
  (37 shorter events, 0.1 us)
Async XLA Ops:
  7.2 95.3 %all-gather.2.cloned.1.call-start = ((), (), s32[]{:S(2)}) async-start(), calls=%async_computation.1 | async-start | bytes 4718592 | tf_op jit(solution)/shard_map/all_gather | solution.py:310
  8.0 12.8 %collective-permute-start = (bf16[16,1024]{1,0:T(8,128)(2,1)S(1)}, bf16[16,1024]{1,0:T(8,128)(2,1)S(1)}, u32[]{:S(2)}, u32[]{:S(2)}) collective-permute-start(bf16[16,1024]{1,0:T(8,128)(2,1)S(1)} %get-tuple-element.47), channel_id=1, source_target_pairs={{0,4},{4,8},{8,12},{12,0},{1,5},{5,9},{9,13},{13,1},{2,6},{6,10},{... | collective-permute-start | bytes 98312 | tf_op jit(solution)/shard_map/ppermute | solution.py:280
  10.0 11.4 %collective-permute-start.1 = (bf16[16,1024]{1,0:T(8,128)(2,1)S(1)}, bf16[16,1024]{1,0:T(8,128)(2,1)S(1)}, u32[]{:S(2)}, u32[]{:S(2)}) collective-permute-start(bf16[16,1024]{1,0:T(8,128)(2,1)S(1)} %get-tuple-element.47), channel_id=1, source_target_pairs={{0,8},{4,12},{8,0},{12,4},{1,9},{5,13},{9,1},{13,5},{2,10},{6,14},... | collective-permute-start | bytes 98312 | tf_op jit(solution)/shard_map/ppermute | solution.py:280
  12.5 8.9 %collective-permute-start.2 = (bf16[16,1024]{1,0:T(8,128)(2,1)S(1)}, bf16[16,1024]{1,0:T(8,128)(2,1)S(1)}, u32[]{:S(2)}, u32[]{:S(2)}) collective-permute-start(bf16[16,1024]{1,0:T(8,128)(2,1)S(1)} %get-tuple-element.47), channel_id=1, source_target_pairs={{0,12},{4,0},{8,4},{12,8},{1,13},{5,1},{9,5},{13,9},{2,14},{6,2},{... | collective-permute-start | bytes 98312 | tf_op jit(solution)/shard_map/ppermute | solution.py:280
  20.8 0.6 copy-start.11
  22.2 5.8 %collective-permute-start.3 = (bf16[64,1024]{1,0:T(8,128)(2,1)S(1)}, bf16[64,1024]{1,0:T(8,128)(2,1)S(1)}, u32[]{:S(2)}, u32[]{:S(2)}) collective-permute-start(bf16[64,1024]{1,0:T(8,128)(2,1)S(1)} %pad_maximum_fusion), channel_id=1, source_target_pairs={{0,1},{1,2},{2,3},{3,0},{4,5},{5,6},{6,7},{7,4},{8,9},{9,10},{10,1... | collective-permute-start | bytes 393224 | tf_op jit(solution)/shard_map/ppermute | solution.py:280
  23.5 7.1 %collective-permute-start.4 = (bf16[64,1024]{1,0:T(8,128)(2,1)S(1)}, bf16[64,1024]{1,0:T(8,128)(2,1)S(1)}, u32[]{:S(2)}, u32[]{:S(2)}) collective-permute-start(bf16[64,1024]{1,0:T(8,128)(2,1)S(1)} %pad_maximum_fusion), channel_id=1, source_target_pairs={{0,2},{1,3},{2,0},{3,1},{4,6},{5,7},{6,4},{7,5},{8,10},{9,11},{10,... | collective-permute-start | bytes 393224 | tf_op jit(solution)/shard_map/ppermute | solution.py:280
  26.2 5.1 %collective-permute-start.5 = (bf16[64,1024]{1,0:T(8,128)(2,1)S(1)}, bf16[64,1024]{1,0:T(8,128)(2,1)S(1)}, u32[]{:S(2)}, u32[]{:S(2)}) collective-permute-start(bf16[64,1024]{1,0:T(8,128)(2,1)S(1)} %pad_maximum_fusion), channel_id=1, source_target_pairs={{0,3},{1,0},{2,1},{3,2},{4,7},{5,4},{6,5},{7,6},{8,11},{9,8},{10,9... | collective-permute-start | bytes 393224 | tf_op jit(solution)/shard_map/ppermute | solution.py:280
  31.3 0.9 copy-start.10
  32.2 15.0 %collective-permute-start.10 = (s16[272,1024]{1,0:T(8,128)(2,1)}, s16[272,1024]{1,0:T(8,128)(2,1)S(1)}, u32[]{:S(2)}, u32[]{:S(2)}) collective-permute-start(s16[272,1024]{1,0:T(8,128)(2,1)} %get-tuple-element.30), channel_id=1, source_target_pairs={{0,1},{1,2},{2,3},{3,0},{4,5},{5,6},{6,7},{7,4},{8,9},{9,10},{10,1... | collective-permute-start | bytes 1671176 | tf_op jit(solution)/shard_map/ppermute | solution.py:266
  32.7 17.1 %collective-permute-start.11 = (s16[272,1024]{1,0:T(8,128)(2,1)}, s16[272,1024]{1,0:T(8,128)(2,1)S(1)}, u32[]{:S(2)}, u32[]{:S(2)}) collective-permute-start(s16[272,1024]{1,0:T(8,128)(2,1)} %get-tuple-element.31), channel_id=1, source_target_pairs={{0,3},{1,0},{2,1},{3,2},{4,7},{5,4},{6,5},{7,6},{8,11},{9,8},{10,9... | collective-permute-start | bytes 1671176 | tf_op jit(solution)/shard_map/ppermute | solution.py:266
  34.9 14.9 %collective-permute-start.8 = (s16[272,1024]{1,0:T(8,128)(2,1)}, s16[272,1024]{1,0:T(8,128)(2,1)S(1)}, u32[]{:S(2)}, u32[]{:S(2)}) collective-permute-start(s16[272,1024]{1,0:T(8,128)(2,1)} %get-tuple-element.24.after), channel_id=1, source_target_pairs={{0,4},{4,8},{8,12},{12,0},{1,5},{5,9},{9,13},{13,1},{2,6},{6,10},{... | collective-permute-start | bytes 1671176 | tf_op jit(solution)/shard_map/ppermute | solution.py:266
  35.2 17.2 %collective-permute-start.9 = (s16[272,1024]{1,0:T(8,128)(2,1)}, s16[272,1024]{1,0:T(8,128)(2,1)S(1)}, u32[]{:S(2)}, u32[]{:S(2)}) collective-permute-start(s16[272,1024]{1,0:T(8,128)(2,1)} %get-tuple-element.29), channel_id=1, source_target_pairs={{0,12},{4,0},{8,4},{12,8},{1,13},{5,1},{9,5},{13,9},{2,14},{6,2},{... | collective-permute-start | bytes 1671176 | tf_op jit(solution)/shard_map/ppermute | solution.py:266
  37.6 14.9 %copy-start.5 = (f32[8,1024]{1,0:T(8,128)S(1)}, f32[8,1024]{1,0:T(8,128)}, u32[]{:S(2)}) copy-start(f32[8,1024]{1,0:T(8,128)} %get-tuple-element.25.ce) | copy-start | bytes 98308
  37.6 26.4 %copy-start.8 = (s32[32]{0:T(128)S(1)}, s32[32]{0:T(128)}, u32[]{:S(2)}) copy-start(s32[32]{0:T(128)} %stack.147.idx) | copy-start | bytes 388
  46.8 17.2 %copy-start = (bf16[512,4096]{1,0:T(8,128)(2,1)S(1)}, bf16[512,4096]{1,0:T(8,128)(2,1)}, u32[]{:S(2)}) copy-start(bf16[512,4096]{1,0:T(8,128)(2,1)} %t3.5) | copy-start | bytes 12582916
  46.8 17.2 %copy-start.1 = (bf16[512,1024]{1,0:T(8,128)(2,1)S(1)}, bf16[512,1024]{1,0:T(8,128)(2,1)}, u32[]{:S(2)}) copy-start(bf16[512,1024]{1,0:T(8,128)(2,1)} %c.7) | copy-start | bytes 3145732
  46.9 12.6 %collective-permute-start.14 = (s16[272,1024]{1,0:T(8,128)(2,1)}, s16[272,1024]{1,0:T(8,128)(2,1)S(1)}, u32[]{:S(2)}, u32[]{:S(2)}) collective-permute-start(s16[272,1024]{1,0:T(8,128)(2,1)} %get-tuple-element.34), channel_id=1, source_target_pairs={{0,1},{1,2},{2,3},{3,0},{4,5},{5,6},{6,7},{7,4},{8,9},{9,10},{10,1... | collective-permute-start | bytes 1671176 | tf_op jit(solution)/shard_map/ppermute | solution.py:266
  47.1 14.2 %collective-permute-start.15 = (s16[272,1024]{1,0:T(8,128)(2,1)}, s16[272,1024]{1,0:T(8,128)(2,1)S(1)}, u32[]{:S(2)}, u32[]{:S(2)}) collective-permute-start(s16[272,1024]{1,0:T(8,128)(2,1)} %get-tuple-element.35), channel_id=1, source_target_pairs={{0,3},{1,0},{2,1},{3,2},{4,7},{5,4},{6,5},{7,6},{8,11},{9,8},{10,9... | collective-permute-start | bytes 1671176 | tf_op jit(solution)/shard_map/ppermute | solution.py:266
  49.8 11.7 %collective-permute-start.6 = (s16[272,1024]{1,0:T(8,128)(2,1)}, s16[272,1024]{1,0:T(8,128)(2,1)S(1)}, u32[]{:S(2)}, u32[]{:S(2)}) collective-permute-start(s16[272,1024]{1,0:T(8,128)(2,1)} %get-tuple-element.26), channel_id=1, source_target_pairs={{0,4},{4,8},{8,12},{12,0},{1,5},{5,9},{9,13},{13,1},{2,6},{6,10},{... | collective-permute-start | bytes 1671176 | tf_op jit(solution)/shard_map/ppermute | solution.py:266
  49.8 16.7 %collective-permute-start.7 = (s16[272,1024]{1,0:T(8,128)(2,1)}, s16[272,1024]{1,0:T(8,128)(2,1)S(1)}, u32[]{:S(2)}, u32[]{:S(2)}) collective-permute-start(s16[272,1024]{1,0:T(8,128)(2,1)} %get-tuple-element.27), channel_id=1, source_target_pairs={{0,12},{4,0},{8,4},{12,8},{1,13},{5,1},{9,5},{13,9},{2,14},{6,2},{... | collective-permute-start | bytes 1671176 | tf_op jit(solution)/shard_map/ppermute | solution.py:266
  52.5 2.2 %copy-start.3 = (f32[1024,1024]{1,0:T(8,128)S(1)}, f32[1024,1024]{1,0:T(8,128)}, u32[]{:S(2)}) copy-start(f32[1024,1024]{1,0:T(8,128)} %get-tuple-element.28.keep) | copy-start | bytes 12582916
  58.6 16.2 %collective-permute-start.12 = (s16[272,1024]{1,0:T(8,128)(2,1)}, s16[272,1024]{1,0:T(8,128)(2,1)S(1)}, u32[]{:S(2)}, u32[]{:S(2)}) collective-permute-start(s16[272,1024]{1,0:T(8,128)(2,1)} %get-tuple-element.32), channel_id=1, source_target_pairs={{0,4},{4,8},{8,12},{12,0},{1,5},{5,9},{9,13},{13,1},{2,6},{6,10},{... | collective-permute-start | bytes 1671176 | tf_op jit(solution)/shard_map/ppermute | solution.py:266
  59.4 15.5 %collective-permute-start.13 = (s16[272,1024]{1,0:T(8,128)(2,1)}, s16[272,1024]{1,0:T(8,128)(2,1)S(1)}, u32[]{:S(2)}, u32[]{:S(2)}) collective-permute-start(s16[272,1024]{1,0:T(8,128)(2,1)} %get-tuple-element.33), channel_id=1, source_target_pairs={{0,12},{4,0},{8,4},{12,8},{1,13},{5,1},{9,5},{13,9},{2,14},{6,2},{... | collective-permute-start | bytes 1671176 | tf_op jit(solution)/shard_map/ppermute | solution.py:266
  61.3 13.6 %collective-permute-start.16 = (s16[272,1024]{1,0:T(8,128)(2,1)}, s16[272,1024]{1,0:T(8,128)(2,1)S(1)}, u32[]{:S(2)}, u32[]{:S(2)}) collective-permute-start(s16[272,1024]{1,0:T(8,128)(2,1)} %get-tuple-element.36), channel_id=1, source_target_pairs={{0,1},{1,2},{2,3},{3,0},{4,5},{5,6},{6,7},{7,4},{8,9},{9,10},{10,1... | collective-permute-start | bytes 1671176 | tf_op jit(solution)/shard_map/ppermute | solution.py:266
  61.5 13.4 %collective-permute-start.17 = (s16[272,1024]{1,0:T(8,128)(2,1)}, s16[272,1024]{1,0:T(8,128)(2,1)S(1)}, u32[]{:S(2)}, u32[]{:S(2)}) collective-permute-start(s16[272,1024]{1,0:T(8,128)(2,1)} %get-tuple-element.37), channel_id=1, source_target_pairs={{0,3},{1,0},{2,1},{3,2},{4,7},{5,4},{6,5},{7,6},{8,11},{9,8},{10,9... | collective-permute-start | bytes 1671176 | tf_op jit(solution)/shard_map/ppermute | solution.py:266
  66.4 31.9 %copy-start.4 = (s32[256,1024]{1,0:T(8,128)S(1)}, s32[256,1024]{1,0:T(8,128)}, u32[]{:S(2)}) copy-start(s32[256,1024]{1,0:T(8,128)} %signs.3) | copy-start | bytes 3145732
  66.4 31.8 %copy-start.6 = (bf16[128,128]{1,0:T(8,128)(2,1)S(1)}, bf16[128,128]{1,0:T(8,128)(2,1)}, u32[]{:S(2)}) copy-start(bf16[128,128]{1,0:T(8,128)(2,1)} %constant.188.clone.inner) | copy-start | bytes 98308
  66.5 31.8 %copy-start.7 = (bf16[128,128]{1,0:T(8,128)(2,1)S(1)}, bf16[128,128]{1,0:T(8,128)(2,1)}, u32[]{:S(2)}) copy-start(bf16[128,128]{1,0:T(8,128)(2,1)} %constant.189.clone.rows) | copy-start | bytes 98308
  79.2 11.7 %collective-permute-start.18 = (s16[144,1024]{1,0:T(8,128)(2,1)}, s16[144,1024]{1,0:T(8,128)(2,1)S(1)}, u32[]{:S(2)}, u32[]{:S(2)}) collective-permute-start(s16[144,1024]{1,0:T(8,128)(2,1)} %get-tuple-element.40), channel_id=1, source_target_pairs={{0,1},{1,2},{2,3},{3,0},{4,5},{5,6},{6,7},{7,4},{8,9},{9,10},{10,1... | collective-permute-start | bytes 884744 | tf_op jit(solution)/shard_map/ppermute | solution.py:266
  79.2 13.4 %collective-permute-start.19 = (s16[144,1024]{1,0:T(8,128)(2,1)}, s16[144,1024]{1,0:T(8,128)(2,1)S(1)}, u32[]{:S(2)}, u32[]{:S(2)}) collective-permute-start(s16[144,1024]{1,0:T(8,128)(2,1)} %get-tuple-element.41), channel_id=1, source_target_pairs={{0,2},{1,3},{2,0},{3,1},{4,6},{5,7},{6,4},{7,5},{8,10},{9,11},{10,... | collective-permute-start | bytes 884744 | tf_op jit(solution)/shard_map/ppermute | solution.py:266
  80.4 13.0 %collective-permute-start.20 = (s16[144,1024]{1,0:T(8,128)(2,1)}, s16[144,1024]{1,0:T(8,128)(2,1)S(1)}, u32[]{:S(2)}, u32[]{:S(2)}) collective-permute-start(s16[144,1024]{1,0:T(8,128)(2,1)} %get-tuple-element.42), channel_id=1, source_target_pairs={{0,3},{1,0},{2,1},{3,2},{4,7},{5,4},{6,5},{7,6},{8,11},{9,8},{10,9... | collective-permute-start | bytes 884744 | tf_op jit(solution)/shard_map/ppermute | solution.py:266
  81.8 11.6 %collective-permute-start.21 = (s16[144,1024]{1,0:T(8,128)(2,1)}, s16[144,1024]{1,0:T(8,128)(2,1)S(1)}, u32[]{:S(2)}, u32[]{:S(2)}) collective-permute-start(s16[144,1024]{1,0:T(8,128)(2,1)} %get-tuple-element.43), channel_id=1, source_target_pairs={{0,4},{4,8},{8,12},{12,0},{1,5},{5,9},{9,13},{13,1},{2,6},{6,10},{... | collective-permute-start | bytes 884744 | tf_op jit(solution)/shard_map/ppermute | solution.py:266
  81.8 13.2 %collective-permute-start.22 = (s16[144,1024]{1,0:T(8,128)(2,1)}, s16[144,1024]{1,0:T(8,128)(2,1)S(1)}, u32[]{:S(2)}, u32[]{:S(2)}) collective-permute-start(s16[144,1024]{1,0:T(8,128)(2,1)} %get-tuple-element.44), channel_id=1, source_target_pairs={{0,8},{4,12},{8,0},{12,4},{1,9},{5,13},{9,1},{13,5},{2,10},{6,14},... | collective-permute-start | bytes 884744 | tf_op jit(solution)/shard_map/ppermute | solution.py:266
  90.9 7.4 %collective-permute-start.23 = (s16[144,1024]{1,0:T(8,128)(2,1)}, s16[144,1024]{1,0:T(8,128)(2,1)S(1)}, u32[]{:S(2)}, u32[]{:S(2)}) collective-permute-start(s16[144,1024]{1,0:T(8,128)(2,1)} %get-tuple-element.45), channel_id=1, source_target_pairs={{0,12},{4,0},{8,4},{12,8},{1,13},{5,1},{9,5},{13,9},{2,14},{6,2},{... | collective-permute-start | bytes 884744 | tf_op jit(solution)/shard_map/ppermute | solution.py:266
  102.4 14.9 %collective-permute-start.24 = (bf16[2048,1024]{1,0:T(8,128)(2,1)}, bf16[2048,1024]{1,0:T(8,128)(2,1)}, u32[]{:S(2)}, u32[]{:S(2)}) collective-permute-start(bf16[2048,1024]{1,0:T(8,128)(2,1)} %tie.3), channel_id=1, source_target_pairs={{0,16},{16,0},{1,17},{17,1},{2,18},{18,2},{3,19},{19,3},{4,20},{20... | collective-permute-start | bytes 12582920 | tf_op jit(solution)/shard_map/ppermute | solution.py:380
  108.0 27.2 %all-to-all-start = ((s16[16,16,1152]{2,1,0:T(8,128)(2,1)}), s16[16,16,1152]{2,1,0:T(8,128)(2,1)S(1)}, u32[]{:S(2)}, u32[]{:S(2)}) async-start(s16[16,16,1152]{2,1,0:T(8,128)(2,1)} %bitcast.38), calls=%async_computation | async-start | bytes 1179648 | tf_op jit(solution)/shard_map/all_to_all | solution.py:377
  117.3 2.2 %copy-start.2 = (bf16[2048,1024]{1,0:T(8,128)(2,1)S(1)}, bf16[2048,1024]{1,0:T(8,128)(2,1)}, u32[]{:S(2)}) copy-start(bf16[2048,1024]{1,0:T(8,128)(2,1)} %tie.3) | copy-start | bytes 12582916
  119.5 15.7 %copy-start.9 = (bf16[16,16]{1,0:T(8,128)(2,1)S(1)}, bf16[16,16]{1,0:T(8,128)(2,1)}, u32[]{:S(2)}) copy-start(bf16[16,16]{1,0:T(8,128)(2,1)} %constant.190.clone.rows) | copy-start | bytes 1540
Sparse Core Ops, SparseCore 0:
  32.3 56.2 all-gather.1

commit v5 on v4

--- a/solution.py
+++ b/solution.py
@@ -92,15 +92,12 @@
     return jnp.concatenate([v[k + 64 * number : k + 64 * number + 64] for k in range(0, v.shape[0], 128)], 0)
 
 
-def far_kernel(idx, t0, t1, t2, t3, c, up_x, down_x, up_y, down_y, ce):
+def far_kernel(idx, t0, t1, t2, t3, c, *refs):
+    up, down, ce = refs[-3:]
     ce[...] = jnp.broadcast_to(column_steps(c[...]), (8, KV))
     p = product((t0, t1, t2, t3), c)
-    for axis, (up, down) in enumerate(((up_x, down_x), (up_y, down_y))):
-
-        @pl.when(pl.program_id(0) == axis)
-        def _(up=up, down=down):
-            write(up, half(p, 0), ce[0:1, :])
-            write(down, half(p, 1), ce[0:1, :])
+    write(up, half(p, 0), ce[0:1, :])
+    write(down, half(p, 1), ce[0:1, :])
 
 
 def near_kernel(idx, t0, t1, t2, t3, c, ce, up_x, down_x, up_y, down_y, keep):
@@ -286,28 +283,32 @@
         tiles = [pl.BlockSpec((TOK, 128), lambda k, ids, t=t: (0, ids[where(k) + t])) for t in range(4)]
         return tiles + [whole((TOK, KV))]
 
-    inputs = (activations,) * 4 + (cotangent,)
+    inputs = (in_hbm(activations),) * 4 + (in_hbm(cotangent),)
     message = pltpu.HBM((272, KV), I16)
     mm = 2 * 1024 * 1024 * 512
 
-    up1x, down1x, up1y, down1y, ce = pl.pallas_call(
-        far_kernel,
-        out_shape=(message,) * 4 + (sds((8, KV), F32),),
-        grid_spec=pltpu.PrefetchScalarGridSpec(
-            num_scalar_prefetch=1,
-            grid=(2,),
-            in_specs=operands(lambda k: 16 * k + 8),
-            out_specs=(whole((272, KV)),) * 4 + (whole((8, KV)),),
-        ),
-        compiler_params=params(),
-        cost_estimate=cost(mm, 6 << 20),
-        name="far",
-    )(idx, *inputs)
+    def far(axis, *after):
+        return pl.pallas_call(
+            far_kernel,
+            out_shape=(message, message, sds((8, KV), F32)),
+            grid_spec=pltpu.PrefetchScalarGridSpec(
+                num_scalar_prefetch=1,
+                grid=(1,),
+                in_specs=operands(lambda k: 16 * axis + 8) + [anywhere] * len(after),
+                out_specs=(whole((272, KV)), whole((272, KV)), whole((8, KV))),
+            ),
+            compiler_params=params(SMALL),
+            cost_estimate=cost(mm // 2, 3 << 20),
+            name="far",
+        )(idx, *inputs, *after)
+
+    up1x, down1x, ce = far(0)
+    piece = jnp.concatenate([piece, tie(round1[0], up1x)] + round1[1:], 0)
+    round2 = spread(piece, "y")
+    up1y, down1y, _ = far(1, piece)
+    piece = jnp.concatenate([piece, tie(round2[0], up1y)] + round2[1:], 0)
+    w_own = lax.all_gather(piece, "z", axis=0, tiled=True)
     got1 = [send(up1x, 0, 1), send(down1x, 0, -1), send(up1y, 1, 1), send(down1y, 1, -1)]
-
-    piece = jnp.concatenate([piece, tie(round1[0], up1x)] + round1[1:], 0)
-    piece = jnp.concatenate([piece] + spread(piece, "y"), 0)
-    w_own = lax.all_gather(piece, "z", axis=0, tiled=True)
 
     up2x, down2x, up2y, down2y, keep_near = pl.pallas_call(
         near_kernel,
@@ -318,7 +319,7 @@
             in_specs=operands(lambda k: 16 * (k // 2) + 4 + 8 * (k % 2)) + [whole((8, KV))],
             out_specs=(whole((272, KV)),) * 4 + (pl.BlockSpec((256, KV), lambda k, ids: (k, 0)),),
         ),
-        compiler_params=params(),
+        compiler_params=params(SMALL),
         cost_estimate=cost(2 * mm, 11 << 20),
         name="near",
     )(idx, *inputs, ce)

time: 161 us -> 160 us (level)
  waiting for transfers between devices: 30.4 us -> 25.4 us
  Pallas kernels: 41.4 us -> 44.1 us
  starting transfers between devices: 48.5 us -> 51 us
    ppermute x18, starting transfers between devices: 23.6 us -> 29.1 us  [send(): return lax.ppermute(v, 'xy'[axis], shift((NX, NY)[axis], s))]
    ppermute x6, waiting for transfers between devices: 3.22 us -> 0.02 us  [spread(): return [lax.ppermute(piece, axis, shift(4, s)) for s in (1, 2, 3)]]
    ppermute x1, starting transfers between devices: 5.53 us -> 3.07 us  [shards(): w_oth = lax.ppermute(w_own, 'core', shift(NC, 1))]
    pallas_call x1 -> x2, Pallas kernels: 6.45 us -> 8.65 us  [far(): pl.pallas_call(far_kernel, out_shape=(message, message, sds((8, KV), F32)...]
    ppermute x18, waiting for transfers between devices: 20.3 us -> 18.4 us  [send(): return lax.ppermute(v, 'xy'[axis], shift((NX, NY)[axis], s))]
    unnamed x30 -> x28, local copies, waits for them, and re-layouts: 7.48 us -> 6.8 us
  transfers between devices with their start and end apart: 27 -> 27, of which waited for: 10 -> 7; matrix products, arithmetic and copies ran while one was open for 1% -> 1% of each run, Pallas kernels for 24% -> 26%
where the time goes in v5:
time: 160 us; the launch traced here: 159 us
  starting transfers between devices  51 us (32%)
  Pallas kernels  44.1 us (28%)
  waiting for transfers between devices  25.4 us (16%)
  blocking collectives  16.1 us (10%)
  between operations  14.9 us (9%)
  local copies, waits for them, and re-layouts  6.92 us (4%)
    ppermute x18, starting transfers between devices, send(): return lax.ppermute(v, 'xy'[axis], shift((NX, NY)[axis], s))  29.1 us
    ppermute x18, waiting for transfers between devices, send(): return lax.ppermute(v, 'xy'[axis], shift((NX, NY)[axis], s))  18.4 us
    all_gather x1, blocking collectives, shards(): gathered = lax.all_gather(back, ('z', 'core'), axis=0, tiled=True)  16.1 us
    ppermute x6, starting transfers between devices, spread(): return [lax.ppermute(piece, axis, shift(4, s)) for s in (1, 2, 3)]  10.7 us
    pallas_call x1, Pallas kernels, shards(): pl.pallas_call(input_grad_kernel, out_shape=pltpu.HBM((TOK, 4096), BF16),...  8.85 us
    pallas_call x2, Pallas kernels, far(): pl.pallas_call(far_kernel, out_shape=(message, message, sds((8, KV), F32)...  8.65 us
    pallas_call x1, Pallas kernels, shards(): pl.pallas_call(near_kernel, out_shape=(message,) * 4 + (sds((1024, KV), F...  8.44 us
    all_to_all x1, starting transfers between devices, shards(): groups = lax.all_to_all(spun, ('z', 'core'), 0, 0, tiled=True)  8.1 us
  transfers between devices with their start and end apart: 27, of which 7 were waited for; matrix products, arithmetic and copies ran while one was open for 1% of the time, Pallas kernels for 26%

profile of v5, /device:TPU:1, one launch (start us, length us, event | category | flops | bytes accessed | tf_op | source)
XLA Modules:
  0.0 159.2 jit_solution(2644475979401142693)
XLA Ops:
  7.2 0.0 all-gather.2.cloned.1.call-start
  7.2 0.8 constant_dynamic-update-slice_fusion.6
  8.0 2.0 %collective-permute-start = (bf16[16,1024]{1,0:T(8,128)(2,1)S(1)}, bf16[16,1024]{1,0:T(8,128)(2,1)S(1)}, u32[]{:S(2)}, u32[]{:S(2)}) collective-permute-start(bf16[16,1024]{1,0:T(8,128)(2,1)S(1)} %get-tuple-element.47), channel_id=1, source_target_pairs={{0,4},{4,8},{8,12},{12,0},{1,5},{5,9},{9,13},{13,1},{2,6},{6,10},{... | collective-permute-start | bytes 98312 | tf_op jit(solution)/shard_map/ppermute | solution.py:277
  10.0 2.5 %collective-permute-start.1 = (bf16[16,1024]{1,0:T(8,128)(2,1)S(1)}, bf16[16,1024]{1,0:T(8,128)(2,1)S(1)}, u32[]{:S(2)}, u32[]{:S(2)}) collective-permute-start(bf16[16,1024]{1,0:T(8,128)(2,1)S(1)} %get-tuple-element.47), channel_id=1, source_target_pairs={{0,8},{4,12},{8,0},{12,4},{1,9},{5,13},{9,1},{13,5},{2,10},{6,14},... | collective-permute-start | bytes 98312 | tf_op jit(solution)/shard_map/ppermute | solution.py:277
  12.5 1.2 collective-permute-start.2
  13.6 0.1 stack.147.idx
  13.7 4.3 %far.2 = (s16[272,1024]{1,0:T(8,128)(2,1)}, s16[272,1024]{1,0:T(8,128)(2,1)}, f32[8,1024]{1,0:T(8,128)S(1)}) custom-call(s32[32]{0:T(128)S(1)} %stack.147.idx, bf16[512,4096]{1,0:T(8,128)(2,1)} %t3.7, bf16[512,4096]{1,0:T(8,128)(2,1)} %t3.7, bf16[512,4096]{1,0:T(8,128)(2,1)} %t3.7, bf16[512,4096]{1,0:T(8,128)(2,1)} %t3.7, bf16[512,1024]{1,0:T(8,128)(2,1)} %c.9), custom_call_target="tpu_custom_call" | custom-call | flops 536870912 | bytes 3145728 | tf_op jit(solution)/shard_map/far/pallas_call | solution.py:291
  18.0 0.6 copy-done.9
  18.6 0.0 collective-permute-done.1
  18.6 0.0 collective-permute-done.2
  18.6 0.8 pad_maximum_fusion.refs_0_
  19.4 1.4 collective-permute-start.3
  20.8 2.6 %collective-permute-start.4 = (bf16[64,1024]{1,0:T(8,128)(2,1)S(1)}, bf16[64,1024]{1,0:T(8,128)(2,1)S(1)}, u32[]{:S(2)}, u32[]{:S(2)}) collective-permute-start(bf16[64,1024]{1,0:T(8,128)(2,1)S(1)} %pad_maximum_fusion.refs_0_), channel_id=1, source_target_pairs={{0,2},{1,3},{2,0},{3,1},{4,6},{5,7},{6,4},{7,5},{8,10},{9,11},{10,... | collective-permute-start | bytes 393224 | tf_op jit(solution)/shard_map/ppermute | solution.py:277
  23.4 1.1 collective-permute-start.5
  24.5 0.8 constant_dynamic-update-slice_fusion.5
  25.2 0.0 copy-start.7
  25.3 0.0 copy-start.10
  25.3 4.4 %far.3 = (s16[272,1024]{1,0:T(8,128)(2,1)}, s16[272,1024]{1,0:T(8,128)(2,1)}, f32[8,1024]{1,0:T(8,128)}) custom-call(s32[32]{0:T(128)S(1)} %stack.147.idx, bf16[512,4096]{1,0:T(8,128)(2,1)} %t3.7, bf16[512,4096]{1,0:T(8,128)(2,1)} %t3.7, bf16[512,4096]{1,0:T(8,128)(2,1)} %t3.7, bf16[512,4096]{1,0:T(8,128)(2,1)} %t3.7, bf16[512,1024]{1,0:T(8,128)(2,1)} %c.9, ...), custom_call_target="tpu_custom_call" | custom-call | flops 536870912 | bytes 3145728 | tf_op jit(solution)/shard_map/far/pallas_call | solution.py:291
  29.6 0.0 collective-permute-done.3.w
  29.6 0.6 copy-done.8
  30.3 0.9 constant_dynamic-update-slice_fusion.2
  31.2 0.0 collective-permute-done.4
  31.3 0.9 copy-done.6
  32.1 0.0 all-gather.2.cloned.1.call-update
  32.2 0.4 collective-permute-start.8
  32.6 2.4 %collective-permute-start.9 = (s16[272,1024]{1,0:T(8,128)(2,1)S(1)}, s16[272,1024]{1,0:T(8,128)(2,1)S(1)}, u32[]{:S(2)}, u32[]{:S(2)}) collective-permute-start(s16[272,1024]{1,0:T(8,128)(2,1)S(1)} %copy-done.10), channel_id=1, source_target_pairs={{0,12},{4,0},{8,4},{12,8},{1,13},{5,1},{9,5},{13,9},{2,14},{6,2},{... | collective-permute-start | bytes 1671176 | tf_op jit(solution)/shard_map/ppermute | solution.py:263
  34.9 0.4 collective-permute-start.10
  35.3 2.3 %collective-permute-start.11 = (s16[272,1024]{1,0:T(8,128)(2,1)}, s16[272,1024]{1,0:T(8,128)(2,1)S(1)}, u32[]{:S(2)}, u32[]{:S(2)}) collective-permute-start(s16[272,1024]{1,0:T(8,128)(2,1)} %get-tuple-element.31), channel_id=1, source_target_pairs={{0,3},{1,0},{2,1},{3,2},{4,7},{5,4},{6,5},{7,6},{8,11},{9,8},{10,9... | collective-permute-start | bytes 1671176 | tf_op jit(solution)/shard_map/ppermute | solution.py:263
  37.6 8.4 %near.1 = (s16[272,1024]{1,0:T(8,128)(2,1)}, s16[272,1024]{1,0:T(8,128)(2,1)}, s16[272,1024]{1,0:T(8,128)(2,1)}, s16[272,1024]{1,0:T(8,128)(2,1)}, f32[1024,1024]{1,0:T(8,128)S(1)}) custom-call(s32[32]{0:T(128)S(1)} %stack.147.idx, bf16[512,4096]{1,0:T(8,128)(2,1)} %t3.7, bf16[512,4096]{1,0:T(8,128)(2,1)} %t3.7, bf16[512,4096]{1,0:T(8,128)(2,1)} %t3.7, ...), custom_call_target="tpu_custom_call" | custom-call | flops 2147483648 | bytes 11534336 | tf_op jit(solution)/shard_map/near/pallas_call | solution.py:313
  46.0 0.0 collective-permute-start.14
  46.0 0.0 collective-permute-done.8.refs_0_
  46.1 2.7 %collective-permute-start.15 = (s16[272,1024]{1,0:T(8,128)(2,1)}, s16[272,1024]{1,0:T(8,128)(2,1)S(1)}, u32[]{:S(2)}, u32[]{:S(2)}) collective-permute-start(s16[272,1024]{1,0:T(8,128)(2,1)} %get-tuple-element.35), channel_id=1, source_target_pairs={{0,3},{1,0},{2,1},{3,2},{4,7},{5,4},{6,5},{7,6},{8,11},{9,8},{10,9... | collective-permute-start | bytes 1671176 | tf_op jit(solution)/shard_map/ppermute | solution.py:263
  48.7 0.0 collective-permute-start.6
  48.7 0.0 collective-permute-done.10.refs_2_
  48.7 2.7 %collective-permute-start.7 = (s16[272,1024]{1,0:T(8,128)(2,1)}, s16[272,1024]{1,0:T(8,128)(2,1)S(1)}, u32[]{:S(2)}, u32[]{:S(2)}) collective-permute-start(s16[272,1024]{1,0:T(8,128)(2,1)} %get-tuple-element.28), channel_id=1, source_target_pairs={{0,12},{4,0},{8,4},{12,8},{1,13},{5,1},{9,5},{13,9},{2,14},{6,2},{... | collective-permute-start | bytes 1671176 | tf_op jit(solution)/shard_map/ppermute | solution.py:263
  51.4 3.9 %relay.1 = (s16[272,1024]{1,0:T(8,128)(2,1)}, s16[272,1024]{1,0:T(8,128)(2,1)}, s16[272,1024]{1,0:T(8,128)(2,1)}, s16[272,1024]{1,0:T(8,128)(2,1)}) custom-call(f32[1024,1024]{1,0:T(8,128)S(1)} %get-tuple-element.29.keep, f32[8,1024]{1,0:T(8,128)S(1)} %get-tuple-element.26.ce, s16[272,1024]{1,0:T(8,128)(2,1)S(1)} %collective-permute-done.8.refs_0_, ...), custom_call_target="tpu_custom_call" | custom-call | flops 1048576 | bytes 8388608 | tf_op jit(solution)/shard_map/relay/pallas_call | solution.py:342
  55.3 4.5 %collective-permute-done.14.refs_4_ = s16[272,1024]{1,0:T(8,128)(2,1)S(1)} collective-permute-done((s16[272,1024]{1,0:T(8,128)(2,1)}, s16[272,1024]{1,0:T(8,128)(2,1)S(1)}, u32[]{:S(2)}, u32[]{:S(2)}) %collective-permute-start.14) | collective-permute-done | bytes 557088 | tf_op jit(solution)/shard_map/ppermute | solution.py:263
  59.9 0.3 collective-permute-start.13
  60.2 0.2 collective-permute-done.6.refs_0_
  60.3 2.5 %collective-permute-start.17 = (s16[272,1024]{1,0:T(8,128)(2,1)}, s16[272,1024]{1,0:T(8,128)(2,1)S(1)}, u32[]{:S(2)}, u32[]{:S(2)}) collective-permute-start(s16[272,1024]{1,0:T(8,128)(2,1)} %get-tuple-element.37), channel_id=1, source_target_pairs={{0,3},{1,0},{2,1},{3,2},{4,7},{5,4},{6,5},{7,6},{8,11},{9,8},{10,9... | collective-permute-start | bytes 1671176 | tf_op jit(solution)/shard_map/ppermute | solution.py:263
  62.8 3.7 %own.1.keep = f32[1024,1024]{1,0:T(8,128)S(1)} custom-call(s32[32]{0:T(128)S(1)} %stack.147.idx, bf16[512,4096]{1,0:T(8,128)(2,1)} %t3.7, bf16[512,4096]{1,0:T(8,128)(2,1)} %t3.7, bf16[512,4096]{1,0:T(8,128)(2,1)} %t3.7, bf16[512,4096]{1,0:T(8,128)(2,1)} %t3.7, bf16[512,1024]{1,0:T(8,128)(2,1)} %c.9), custom_call_target="tpu_custom_call" | custom-call | flops 1073741824 | bytes 8388608 | tf_op jit(solution)/shard_map/own/pallas_call | solution.py:328
  66.5 0.0 copy-start.2
  66.6 0.0 copy-start.3
  66.6 0.0 copy-start.4
  66.6 5.7 %collective-permute-done.12.refs_2_ = s16[272,1024]{1,0:T(8,128)(2,1)S(1)} collective-permute-done((s16[272,1024]{1,0:T(8,128)(2,1)}, s16[272,1024]{1,0:T(8,128)(2,1)S(1)}, u32[]{:S(2)}, u32[]{:S(2)}) %collective-permute-start.12) | collective-permute-done | bytes 557088 | tf_op jit(solution)/shard_map/ppermute | solution.py:263
  72.3 0.7 collective-permute-done.13.refs_3_
  73.0 4.3 %cross.1 = (f32[128,1024]{1,0:T(8,128)}, s16[144,1024]{1,0:T(8,128)(2,1)}, s16[144,1024]{1,0:T(8,128)(2,1)}, s16[144,1024]{1,0:T(8,128)(2,1)}, f32[128,1024]{1,0...) custom-call(f32[1024,1024]{1,0:T(8,128)S(1)} %own.1.keep, ...), custom_call_target="tpu_custom_call" | custom-call | flops 1048576 | bytes 12582912 | tf_op jit(solution)/shard_map/cross/pallas_call | solution.py:354
  77.2 1.6 %collective-permute-start.19 = (s16[144,1024]{1,0:T(8,128)(2,1)}, s16[144,1024]{1,0:T(8,128)(2,1)S(1)}, u32[]{:S(2)}, u32[]{:S(2)}) collective-permute-start(s16[144,1024]{1,0:T(8,128)(2,1)} %get-tuple-element.41), channel_id=1, source_target_pairs={{0,2},{1,3},{2,0},{3,1},{4,6},{5,7},{6,4},{7,5},{8,10},{9,11},{10,... | collective-permute-start | bytes 884744 | tf_op jit(solution)/shard_map/ppermute | solution.py:263
  78.9 1.0 collective-permute-start.20
  79.9 1.1 collective-permute-start.21
  81.0 3.5 %collective-permute-start.22 = (s16[144,1024]{1,0:T(8,128)(2,1)}, s16[144,1024]{1,0:T(8,128)(2,1)S(1)}, u32[]{:S(2)}, u32[]{:S(2)}) collective-permute-start(s16[144,1024]{1,0:T(8,128)(2,1)} %get-tuple-element.44), channel_id=1, source_target_pairs={{0,8},{4,12},{8,0},{12,4},{1,9},{5,13},{9,1},{13,5},{2,10},{6,14},... | collective-permute-start | bytes 884744 | tf_op jit(solution)/shard_map/ppermute | solution.py:263
  84.5 2.9 %collective-permute-done.18.x1 = s16[144,1024]{1,0:T(8,128)(2,1)S(1)} collective-permute-done((s16[144,1024]{1,0:T(8,128)(2,1)}, s16[144,1024]{1,0:T(8,128)(2,1)S(1)}, u32[]{:S(2)}, u32[]{:S(2)}) %collective-permute-start.18) | collective-permute-done | bytes 294944 | tf_op jit(solution)/shard_map/ppermute | solution.py:263
  87.4 8.3 %collective-permute-start.23 = (s16[144,1024]{1,0:T(8,128)(2,1)}, s16[144,1024]{1,0:T(8,128)(2,1)S(1)}, u32[]{:S(2)}, u32[]{:S(2)}) collective-permute-start(s16[144,1024]{1,0:T(8,128)(2,1)} %get-tuple-element.45), channel_id=1, source_target_pairs={{0,12},{4,0},{8,4},{12,8},{1,13},{5,1},{9,5},{13,9},{2,14},{6,2},{... | collective-permute-start | bytes 884744 | tf_op jit(solution)/shard_map/ppermute | solution.py:263
  95.7 4.4 %collective-permute-done.23.y3 = s16[144,1024]{1,0:T(8,128)(2,1)S(1)} collective-permute-done((s16[144,1024]{1,0:T(8,128)(2,1)}, s16[144,1024]{1,0:T(8,128)(2,1)S(1)}, u32[]{:S(2)}, u32[]{:S(2)}) %collective-permute-start.23) | collective-permute-done | bytes 294944 | tf_op jit(solution)/shard_map/ppermute | solution.py:263
  100.1 4.1 %rotate.1.after = s16[256,1152]{1,0:T(8,128)(2,1)} custom-call(f32[128,1024]{1,0:T(8,128)} %get-tuple-element.38.own_x, f32[128,1024]{1,0:T(8,128)} %get-tuple-element.39.own_y, s16[144,1024]{1,0:T(8,128)(2,1)S(1)} %collective-permute-done.18.x1, s16[144,1024]{1,0:T(8,128)(2,1)S(1)} %collective-permute-done.19.x2, ...), custom_call_target="tpu_custom_call" | custom-call | flops 268435456 | bytes 4194304 | tf_op jit(solution)/shard_map/rotate/pallas_call | solution.py:369
  104.3 3.1 %collective-permute-start.24 = (bf16[2048,1024]{1,0:T(8,128)(2,1)}, bf16[2048,1024]{1,0:T(8,128)(2,1)}, u32[]{:S(2)}, u32[]{:S(2)}) collective-permute-start(bf16[2048,1024]{1,0:T(8,128)(2,1)} %tie.5), channel_id=1, source_target_pairs={{0,16},{16,0},{1,17},{17,1},{2,18},{18,2},{3,19},{19,3},{4,20},{20... | collective-permute-start | bytes 12582920 | tf_op jit(solution)/shard_map/ppermute | solution.py:381
  107.3 8.1 %all-to-all-start = ((s16[16,16,1152]{2,1,0:T(8,128)(2,1)}), s16[16,16,1152]{2,1,0:T(8,128)(2,1)S(1)}, u32[]{:S(2)}, u32[]{:S(2)}) async-start(s16[16,16,1152]{2,1,0:T(8,128)(2,1)} %bitcast.38), calls=%async_computation | async-start | bytes 1179648 | tf_op jit(solution)/shard_map/all_to_all | solution.py:378
  116.1 0.1 pad_add_fusion.at
  116.2 2.2 %copy-done.1 = bf16[2048,1024]{1,0:T(8,128)(2,1)S(1)} copy-done((bf16[2048,1024]{1,0:T(8,128)(2,1)S(1)}, bf16[2048,1024]{1,0:T(8,128)(2,1)}, u32[]{:S(2)}) %copy-start.1) | copy-done | bytes 4194328
  118.4 8.8 %input_grad.1.after = bf16[512,4096]{1,0:T(8,128)(2,1)} custom-call(s32[3]{0:T(128)S(1)} %pad_add_fusion.at, bf16[512,1024]{1,0:T(8,128)(2,1)S(1)} %copy-done, bf16[8,4,4,16,1024]{4,3,2,1,0:T(8,128)(2,1)S(1)} %bitcast.41, bf16[8,4,4,16,1024]{4,3,2,1,0:T(8,128)(2,1)} %bitcast.36.w_oth), custom_call_target="tpu_custom_call" | custom-call | flops 4294967296 | bytes 13631488 | tf_op jit(solution)/shard_map/input_grad/pallas_call | solution.py:384
  127.2 6.9 %all-to-all-done = s16[16,16,1152]{2,1,0:T(8,128)(2,1)S(1)} async-done(((s16[16,16,1152]{2,1,0:T(8,128)(2,1)}), s16[16,16,1152]{2,1,0:T(8,128)(2,1)S(1)}, u32[]{:S(2)}, u32[]{:S(2)}) %all-to-all-start) | async-done | bytes 589856 | tf_op jit(solution)/shard_map/all_to_all | solution.py:378
  134.1 1.0 levels.1
  135.1 16.1 %all_gather.7.q = s16[256,1152]{1,0:T(8,128)(2,1)S(1)} all-gather(s16[16,1152]{1,0:T(8,128)(2,1)S(1)} %levels.1), channel_id=1, replica_groups=mesh['z'=8,'core'=2,'x'=4,'y'=4] {'z','core'}, dimensions={0}, use_global_device_ids=true | all-gather | bytes 626688 | tf_op jit(solution)/shard_map/all_gather | solution.py:408
  151.2 1.2 finish.1
  (37 shorter events, 0.1 us)
Async XLA Ops:
  7.2 97.1 %all-gather.2.cloned.1.call-start = ((), (), s32[]{:S(2)}) async-start(), calls=%async_computation.1 | async-start | bytes 4718592 | tf_op jit(solution)/shard_map/all_gather | solution.py:310
  8.0 10.0 %collective-permute-start = (bf16[16,1024]{1,0:T(8,128)(2,1)S(1)}, bf16[16,1024]{1,0:T(8,128)(2,1)S(1)}, u32[]{:S(2)}, u32[]{:S(2)}) collective-permute-start(bf16[16,1024]{1,0:T(8,128)(2,1)S(1)} %get-tuple-element.47), channel_id=1, source_target_pairs={{0,4},{4,8},{8,12},{12,0},{1,5},{5,9},{9,13},{13,1},{2,6},{6,10},{... | collective-permute-start | bytes 98312 | tf_op jit(solution)/shard_map/ppermute | solution.py:277
  10.0 8.6 %collective-permute-start.1 = (bf16[16,1024]{1,0:T(8,128)(2,1)S(1)}, bf16[16,1024]{1,0:T(8,128)(2,1)S(1)}, u32[]{:S(2)}, u32[]{:S(2)}) collective-permute-start(bf16[16,1024]{1,0:T(8,128)(2,1)S(1)} %get-tuple-element.47), channel_id=1, source_target_pairs={{0,8},{4,12},{8,0},{12,4},{1,9},{5,13},{9,1},{13,5},{2,10},{6,14},... | collective-permute-start | bytes 98312 | tf_op jit(solution)/shard_map/ppermute | solution.py:277
  12.5 6.2 %collective-permute-start.2 = (bf16[16,1024]{1,0:T(8,128)(2,1)S(1)}, bf16[16,1024]{1,0:T(8,128)(2,1)S(1)}, u32[]{:S(2)}, u32[]{:S(2)}) collective-permute-start(bf16[16,1024]{1,0:T(8,128)(2,1)S(1)} %get-tuple-element.47), channel_id=1, source_target_pairs={{0,12},{4,0},{8,4},{12,8},{1,13},{5,1},{9,5},{13,9},{2,14},{6,2},{... | collective-permute-start | bytes 98312 | tf_op jit(solution)/shard_map/ppermute | solution.py:277
  18.0 0.6 copy-start.9
  19.4 10.2 %collective-permute-start.3 = (bf16[64,1024]{1,0:T(8,128)(2,1)S(1)}, bf16[64,1024]{1,0:T(8,128)(2,1)S(1)}, u32[]{:S(2)}, u32[]{:S(2)}) collective-permute-start(bf16[64,1024]{1,0:T(8,128)(2,1)S(1)} %pad_maximum_fusion.refs_0_), channel_id=1, source_target_pairs={{0,1},{1,2},{2,3},{3,0},{4,5},{5,6},{6,7},{7,4},{8,9},{9,10},{10,1... | collective-permute-start | bytes 393224 | tf_op jit(solution)/shard_map/ppermute | solution.py:277
  20.8 10.4 %collective-permute-start.4 = (bf16[64,1024]{1,0:T(8,128)(2,1)S(1)}, bf16[64,1024]{1,0:T(8,128)(2,1)S(1)}, u32[]{:S(2)}, u32[]{:S(2)}) collective-permute-start(bf16[64,1024]{1,0:T(8,128)(2,1)S(1)} %pad_maximum_fusion.refs_0_), channel_id=1, source_target_pairs={{0,2},{1,3},{2,0},{3,1},{4,6},{5,7},{6,4},{7,5},{8,10},{9,11},{10,... | collective-permute-start | bytes 393224 | tf_op jit(solution)/shard_map/ppermute | solution.py:277
  23.4 7.8 %collective-permute-start.5 = (bf16[64,1024]{1,0:T(8,128)(2,1)S(1)}, bf16[64,1024]{1,0:T(8,128)(2,1)S(1)}, u32[]{:S(2)}, u32[]{:S(2)}) collective-permute-start(bf16[64,1024]{1,0:T(8,128)(2,1)S(1)} %pad_maximum_fusion.refs_0_), channel_id=1, source_target_pairs={{0,3},{1,0},{2,1},{3,2},{4,7},{5,4},{6,5},{7,6},{8,11},{9,8},{10,9... | collective-permute-start | bytes 393224 | tf_op jit(solution)/shard_map/ppermute | solution.py:277
  25.2 6.9 %copy-start.7 = (s16[272,1024]{1,0:T(8,128)(2,1)S(1)}, s16[272,1024]{1,0:T(8,128)(2,1)}, u32[]{:S(2)}) copy-start(s16[272,1024]{1,0:T(8,128)(2,1)} %get-tuple-element.24.after) | copy-start | bytes 1671172
  25.3 7.3 %copy-start.10 = (s16[272,1024]{1,0:T(8,128)(2,1)S(1)}, s16[272,1024]{1,0:T(8,128)(2,1)}, u32[]{:S(2)}) copy-start(s16[272,1024]{1,0:T(8,128)(2,1)} %get-tuple-element.30) | copy-start | bytes 1671172
  29.6 0.7 copy-start.8
  31.3 0.9 copy-start.6
  32.2 13.9 %collective-permute-start.8 = (s16[272,1024]{1,0:T(8,128)(2,1)S(1)}, s16[272,1024]{1,0:T(8,128)(2,1)S(1)}, u32[]{:S(2)}, u32[]{:S(2)}) collective-permute-start(s16[272,1024]{1,0:T(8,128)(2,1)S(1)} %copy-done.7), channel_id=1, source_target_pairs={{0,4},{4,8},{8,12},{12,0},{1,5},{5,9},{9,13},{13,1},{2,6},{6,10},{... | collective-permute-start | bytes 1671176 | tf_op jit(solution)/shard_map/ppermute | solution.py:263
  32.6 16.2 %collective-permute-start.9 = (s16[272,1024]{1,0:T(8,128)(2,1)S(1)}, s16[272,1024]{1,0:T(8,128)(2,1)S(1)}, u32[]{:S(2)}, u32[]{:S(2)}) collective-permute-start(s16[272,1024]{1,0:T(8,128)(2,1)S(1)} %copy-done.10), channel_id=1, source_target_pairs={{0,12},{4,0},{8,4},{12,8},{1,13},{5,1},{9,5},{13,9},{2,14},{6,2},{... | collective-permute-start | bytes 1671176 | tf_op jit(solution)/shard_map/ppermute | solution.py:263
  34.9 13.8 %collective-permute-start.10 = (s16[272,1024]{1,0:T(8,128)(2,1)}, s16[272,1024]{1,0:T(8,128)(2,1)S(1)}, u32[]{:S(2)}, u32[]{:S(2)}) collective-permute-start(s16[272,1024]{1,0:T(8,128)(2,1)} %get-tuple-element.25.after), channel_id=1, source_target_pairs={{0,1},{1,2},{2,3},{3,0},{4,5},{5,6},{6,7},{7,4},{8,9},{9,10},{10,1... | collective-permute-start | bytes 1671176 | tf_op jit(solution)/shard_map/ppermute | solution.py:263
  35.3 16.1 %collective-permute-start.11 = (s16[272,1024]{1,0:T(8,128)(2,1)}, s16[272,1024]{1,0:T(8,128)(2,1)S(1)}, u32[]{:S(2)}, u32[]{:S(2)}) collective-permute-start(s16[272,1024]{1,0:T(8,128)(2,1)} %get-tuple-element.31), channel_id=1, source_target_pairs={{0,3},{1,0},{2,1},{3,2},{4,7},{5,4},{6,5},{7,6},{8,11},{9,8},{10,9... | collective-permute-start | bytes 1671176 | tf_op jit(solution)/shard_map/ppermute | solution.py:263
  46.0 13.8 %collective-permute-start.14 = (s16[272,1024]{1,0:T(8,128)(2,1)}, s16[272,1024]{1,0:T(8,128)(2,1)S(1)}, u32[]{:S(2)}, u32[]{:S(2)}) collective-permute-start(s16[272,1024]{1,0:T(8,128)(2,1)} %get-tuple-element.34), channel_id=1, source_target_pairs={{0,1},{1,2},{2,3},{3,0},{4,5},{5,6},{6,7},{7,4},{8,9},{9,10},{10,1... | collective-permute-start | bytes 1671176 | tf_op jit(solution)/shard_map/ppermute | solution.py:263
  46.1 14.1 %collective-permute-start.15 = (s16[272,1024]{1,0:T(8,128)(2,1)}, s16[272,1024]{1,0:T(8,128)(2,1)S(1)}, u32[]{:S(2)}, u32[]{:S(2)}) collective-permute-start(s16[272,1024]{1,0:T(8,128)(2,1)} %get-tuple-element.35), channel_id=1, source_target_pairs={{0,3},{1,0},{2,1},{3,2},{4,7},{5,4},{6,5},{7,6},{8,11},{9,8},{10,9... | collective-permute-start | bytes 1671176 | tf_op jit(solution)/shard_map/ppermute | solution.py:263
  48.7 11.6 %collective-permute-start.6 = (s16[272,1024]{1,0:T(8,128)(2,1)}, s16[272,1024]{1,0:T(8,128)(2,1)S(1)}, u32[]{:S(2)}, u32[]{:S(2)}) collective-permute-start(s16[272,1024]{1,0:T(8,128)(2,1)} %get-tuple-element.27), channel_id=1, source_target_pairs={{0,4},{4,8},{8,12},{12,0},{1,5},{5,9},{9,13},{13,1},{2,6},{6,10},{... | collective-permute-start | bytes 1671176 | tf_op jit(solution)/shard_map/ppermute | solution.py:263
  48.7 17.8 %collective-permute-start.7 = (s16[272,1024]{1,0:T(8,128)(2,1)}, s16[272,1024]{1,0:T(8,128)(2,1)S(1)}, u32[]{:S(2)}, u32[]{:S(2)}) collective-permute-start(s16[272,1024]{1,0:T(8,128)(2,1)} %get-tuple-element.28), channel_id=1, source_target_pairs={{0,12},{4,0},{8,4},{12,8},{1,13},{5,1},{9,5},{13,9},{2,14},{6,2},{... | collective-permute-start | bytes 1671176 | tf_op jit(solution)/shard_map/ppermute | solution.py:263
  55.3 16.9 %collective-permute-start.12 = (s16[272,1024]{1,0:T(8,128)(2,1)}, s16[272,1024]{1,0:T(8,128)(2,1)S(1)}, u32[]{:S(2)}, u32[]{:S(2)}) collective-permute-start(s16[272,1024]{1,0:T(8,128)(2,1)} %get-tuple-element.32), channel_id=1, source_target_pairs={{0,4},{4,8},{8,12},{12,0},{1,5},{5,9},{9,13},{13,1},{2,6},{6,10},{... | collective-permute-start | bytes 1671176 | tf_op jit(solution)/shard_map/ppermute | solution.py:263
  59.9 13.1 %collective-permute-start.13 = (s16[272,1024]{1,0:T(8,128)(2,1)}, s16[272,1024]{1,0:T(8,128)(2,1)S(1)}, u32[]{:S(2)}, u32[]{:S(2)}) collective-permute-start(s16[272,1024]{1,0:T(8,128)(2,1)} %get-tuple-element.33), channel_id=1, source_target_pairs={{0,12},{4,0},{8,4},{12,8},{1,13},{5,1},{9,5},{13,9},{2,14},{6,2},{... | collective-permute-start | bytes 1671176 | tf_op jit(solution)/shard_map/ppermute | solution.py:263
  60.2 12.8 %collective-permute-start.16 = (s16[272,1024]{1,0:T(8,128)(2,1)}, s16[272,1024]{1,0:T(8,128)(2,1)S(1)}, u32[]{:S(2)}, u32[]{:S(2)}) collective-permute-start(s16[272,1024]{1,0:T(8,128)(2,1)} %get-tuple-element.36), channel_id=1, source_target_pairs={{0,1},{1,2},{2,3},{3,0},{4,5},{5,6},{6,7},{7,4},{8,9},{9,10},{10,1... | collective-permute-start | bytes 1671176 | tf_op jit(solution)/shard_map/ppermute | solution.py:263
  60.3 12.6 %collective-permute-start.17 = (s16[272,1024]{1,0:T(8,128)(2,1)}, s16[272,1024]{1,0:T(8,128)(2,1)S(1)}, u32[]{:S(2)}, u32[]{:S(2)}) collective-permute-start(s16[272,1024]{1,0:T(8,128)(2,1)} %get-tuple-element.37), channel_id=1, source_target_pairs={{0,3},{1,0},{2,1},{3,2},{4,7},{5,4},{6,5},{7,6},{8,11},{9,8},{10,9... | collective-permute-start | bytes 1671176 | tf_op jit(solution)/shard_map/ppermute | solution.py:263
  66.5 33.6 %copy-start.2 = (s32[256,1024]{1,0:T(8,128)S(1)}, s32[256,1024]{1,0:T(8,128)}, u32[]{:S(2)}) copy-start(s32[256,1024]{1,0:T(8,128)} %signs.3) | copy-start | bytes 3145732
  66.6 33.6 %copy-start.3 = (bf16[128,128]{1,0:T(8,128)(2,1)S(1)}, bf16[128,128]{1,0:T(8,128)(2,1)}, u32[]{:S(2)}) copy-start(bf16[128,128]{1,0:T(8,128)(2,1)} %constant.188.clone.inner) | copy-start | bytes 98308
  66.6 33.6 %copy-start.4 = (bf16[128,128]{1,0:T(8,128)(2,1)S(1)}, bf16[128,128]{1,0:T(8,128)(2,1)}, u32[]{:S(2)}) copy-start(bf16[128,128]{1,0:T(8,128)(2,1)} %constant.189.clone.rows) | copy-start | bytes 98308
  77.2 10.2 %collective-permute-start.18 = (s16[144,1024]{1,0:T(8,128)(2,1)}, s16[144,1024]{1,0:T(8,128)(2,1)S(1)}, u32[]{:S(2)}, u32[]{:S(2)}) collective-permute-start(s16[144,1024]{1,0:T(8,128)(2,1)} %get-tuple-element.40), channel_id=1, source_target_pairs={{0,1},{1,2},{2,3},{3,0},{4,5},{5,6},{6,7},{7,4},{8,9},{9,10},{10,1... | collective-permute-start | bytes 884744 | tf_op jit(solution)/shard_map/ppermute | solution.py:263
  77.2 18.4 %collective-permute-start.19 = (s16[144,1024]{1,0:T(8,128)(2,1)}, s16[144,1024]{1,0:T(8,128)(2,1)S(1)}, u32[]{:S(2)}, u32[]{:S(2)}) collective-permute-start(s16[144,1024]{1,0:T(8,128)(2,1)} %get-tuple-element.41), channel_id=1, source_target_pairs={{0,2},{1,3},{2,0},{3,1},{4,6},{5,7},{6,4},{7,5},{8,10},{9,11},{10,... | collective-permute-start | bytes 884744 | tf_op jit(solution)/shard_map/ppermute | solution.py:263
  78.9 16.8 %collective-permute-start.20 = (s16[144,1024]{1,0:T(8,128)(2,1)}, s16[144,1024]{1,0:T(8,128)(2,1)S(1)}, u32[]{:S(2)}, u32[]{:S(2)}) collective-permute-start(s16[144,1024]{1,0:T(8,128)(2,1)} %get-tuple-element.42), channel_id=1, source_target_pairs={{0,3},{1,0},{2,1},{3,2},{4,7},{5,4},{6,5},{7,6},{8,11},{9,8},{10,9... | collective-permute-start | bytes 884744 | tf_op jit(solution)/shard_map/ppermute | solution.py:263
  79.9 15.7 %collective-permute-start.21 = (s16[144,1024]{1,0:T(8,128)(2,1)}, s16[144,1024]{1,0:T(8,128)(2,1)S(1)}, u32[]{:S(2)}, u32[]{:S(2)}) collective-permute-start(s16[144,1024]{1,0:T(8,128)(2,1)} %get-tuple-element.43), channel_id=1, source_target_pairs={{0,4},{4,8},{8,12},{12,0},{1,5},{5,9},{9,13},{13,1},{2,6},{6,10},{... | collective-permute-start | bytes 884744 | tf_op jit(solution)/shard_map/ppermute | solution.py:263
  81.0 14.6 %collective-permute-start.22 = (s16[144,1024]{1,0:T(8,128)(2,1)}, s16[144,1024]{1,0:T(8,128)(2,1)S(1)}, u32[]{:S(2)}, u32[]{:S(2)}) collective-permute-start(s16[144,1024]{1,0:T(8,128)(2,1)} %get-tuple-element.44), channel_id=1, source_target_pairs={{0,8},{4,12},{8,0},{12,4},{1,9},{5,13},{9,1},{13,5},{2,10},{6,14},... | collective-permute-start | bytes 884744 | tf_op jit(solution)/shard_map/ppermute | solution.py:263
  87.4 12.7 %collective-permute-start.23 = (s16[144,1024]{1,0:T(8,128)(2,1)}, s16[144,1024]{1,0:T(8,128)(2,1)S(1)}, u32[]{:S(2)}, u32[]{:S(2)}) collective-permute-start(s16[144,1024]{1,0:T(8,128)(2,1)} %get-tuple-element.45), channel_id=1, source_target_pairs={{0,12},{4,0},{8,4},{12,8},{1,13},{5,1},{9,5},{13,9},{2,14},{6,2},{... | collective-permute-start | bytes 884744 | tf_op jit(solution)/shard_map/ppermute | solution.py:263
  104.3 11.9 %copy-start = (bf16[512,1024]{1,0:T(8,128)(2,1)S(1)}, bf16[512,1024]{1,0:T(8,128)(2,1)}, u32[]{:S(2)}) copy-start(bf16[512,1024]{1,0:T(8,128)(2,1)} %c.9) | copy-start | bytes 3145732
  104.3 11.9 %collective-permute-start.24 = (bf16[2048,1024]{1,0:T(8,128)(2,1)}, bf16[2048,1024]{1,0:T(8,128)(2,1)}, u32[]{:S(2)}, u32[]{:S(2)}) collective-permute-start(bf16[2048,1024]{1,0:T(8,128)(2,1)} %tie.5), channel_id=1, source_target_pairs={{0,16},{16,0},{1,17},{17,1},{2,18},{18,2},{3,19},{19,3},{4,20},{20... | collective-permute-start | bytes 12582920 | tf_op jit(solution)/shard_map/ppermute | solution.py:381
  107.3 26.8 %all-to-all-start = ((s16[16,16,1152]{2,1,0:T(8,128)(2,1)}), s16[16,16,1152]{2,1,0:T(8,128)(2,1)S(1)}, u32[]{:S(2)}, u32[]{:S(2)}) async-start(s16[16,16,1152]{2,1,0:T(8,128)(2,1)} %bitcast.38), calls=%async_computation | async-start | bytes 1179648 | tf_op jit(solution)/shard_map/all_to_all | solution.py:378
  116.2 2.2 %copy-start.1 = (bf16[2048,1024]{1,0:T(8,128)(2,1)S(1)}, bf16[2048,1024]{1,0:T(8,128)(2,1)}, u32[]{:S(2)}) copy-start(bf16[2048,1024]{1,0:T(8,128)(2,1)} %tie.5) | copy-start | bytes 12582916
  118.4 15.7 %copy-start.5 = (bf16[16,16]{1,0:T(8,128)(2,1)S(1)}, bf16[16,16]{1,0:T(8,128)(2,1)}, u32[]{:S(2)}) copy-start(bf16[16,16]{1,0:T(8,128)(2,1)} %constant.190.clone.rows) | copy-start | bytes 1540
Sparse Core Ops, SparseCore 0:
  32.3 54.5 all-gather.1

commit v6 on v5

--- a/solution.py
+++ b/solution.py
@@ -168,15 +168,14 @@
     return split_dot_left(rows, mixed) * (1.0 / 64.0)
 
 
-def rotate_kernel(own_x, own_y, x1, x2, x3, y1, y2, y3, signs, inner, rows, out):
-    for k, (own, msgs) in enumerate(((own_x, (x1, x2, x3)), (own_y, (y1, y2, y3)))):
-        here = slice(k * 128, k * 128 + 128)
-        total = own[...]
-        for msg in msgs:
-            total = total + read(msg)
-        q, e = encode(rotate(total * signs[here, :].astype(F32), inner[...], rows[...]), None)
-        out[here, 0:KV] = q
-        out[here, KV : KV + 128] = jnp.broadcast_to(e, (128, 128)).astype(I32).astype(I16)
+def rotate_kernel(own, n1, n2, n3, signs, inner, rows, *refs):
+    out = refs[-1]
+    total = own[...]
+    for msg in (n1, n2, n3):
+        total = total + read(msg)
+    q, e = encode(rotate(total * signs[...].astype(F32), inner[...], rows[...]), None)
+    out[:, 0:KV] = q
+    out[:, KV : KV + 128] = jnp.broadcast_to(e, (128, 128)).astype(I32).astype(I16)
 
 
 def levels_kernel(count, x, inner, rows, after, out):
@@ -366,15 +365,25 @@
 
     inner = jnp.asarray(hadamard(128), BF16)
     quad = hadamard(4)
-    spun = pl.pallas_call(
-        rotate_kernel,
-        out_shape=sds((256, KV + 128), I16),
-        in_specs=[in_vmem] * 11,
-        out_specs=in_vmem,
-        compiler_params=params(SMALL),
-        cost_estimate=cost(1 << 28, 4 << 20),
-        name="rotate",
-    )(in_hbm(own_x), in_hbm(own_y), *last, sign_flips, inner, jnp.asarray(np.kron(np.eye(32), quad), BF16))
+    eights = jnp.asarray(np.kron(np.eye(32), quad), BF16)
+
+    def rotated(axis, own, msgs, *before):
+        return pl.pallas_call(
+            rotate_kernel,
+            out_shape=pltpu.HBM((256, KV + 128), I16),
+            grid=(1,),
+            in_specs=[whole((128, KV))]
+            + [whole((144, KV))] * 3
+            + [pl.BlockSpec((128, KV), lambda k: (axis, 0)), whole((128, 128)), whole((128, 128))]
+            + [anywhere] * len(before),
+            out_specs=pl.BlockSpec((128, KV + 128), lambda k: (axis, 0)),
+            input_output_aliases={7: 0} if before else {},
+            compiler_params=params(SMALL),
+            cost_estimate=cost(1 << 27, 2 << 20),
+            name="rotate",
+        )(in_hbm(own), *msgs, sign_flips, inner, eights, *before)
+
+    spun = rotated(1, own_y, last[3:], rotated(0, own_x, last[:3]))
     groups = lax.all_to_all(spun, ("z", "core"), 0, 0, tiled=True)
 
     w_own = tie(w_own, spun)

time: 160 us -> 159 us (level)
  waiting for transfers between devices: 25.4 us -> 22.3 us
  Pallas kernels: 44.1 us -> 46 us
    ppermute x18, waiting for transfers between devices: 18.4 us -> 15.4 us  [send(): return lax.ppermute(v, 'xy'[axis], shift((NX, NY)[axis], s))]
    pallas_call x1 -> x2, Pallas kernels: 4.13 us -> 6.01 us  [rotated(): pl.pallas_call(rotate_kernel, out_shape=pltpu.HBM((256, KV + 128), I16),...]
  transfers between devices with their start and end apart: 27 -> 27, of which waited for: 7 -> 7; matrix products, arithmetic and copies ran while one was open for 1% -> 1% of each run, Pallas kernels for 26% -> 28%
where the time goes in v6:
time: 159 us; the launch traced here: 158 us
  starting transfers between devices  51 us (32%)
  Pallas kernels  46 us (29%)
  waiting for transfers between devices  22.3 us (14%)
  blocking collectives  16.1 us (10%)
  between operations  14.9 us (9%)
  local copies, waits for them, and re-layouts  6.92 us (4%)
    ppermute x18, starting transfers between devices, send(): return lax.ppermute(v, 'xy'[axis], shift((NX, NY)[axis], s))  29.1 us
    all_gather x1, blocking collectives, shards(): gathered = lax.all_gather(back, ('z', 'core'), axis=0, tiled=True)  16.1 us
    ppermute x18, waiting for transfers between devices, send(): return lax.ppermute(v, 'xy'[axis], shift((NX, NY)[axis], s))  15.4 us
    ppermute x6, starting transfers between devices, spread(): return [lax.ppermute(piece, axis, shift(4, s)) for s in (1, 2, 3)]  10.7 us
    pallas_call x1, Pallas kernels, shards(): pl.pallas_call(input_grad_kernel, out_shape=pltpu.HBM((TOK, 4096), BF16),...  8.85 us
    pallas_call x2, Pallas kernels, far(): pl.pallas_call(far_kernel, out_shape=(message, message, sds((8, KV), F32)...  8.65 us
    pallas_call x1, Pallas kernels, shards(): pl.pallas_call(near_kernel, out_shape=(message,) * 4 + (sds((1024, KV), F...  8.44 us
    all_to_all x1, starting transfers between devices, shards(): groups = lax.all_to_all(spun, ('z', 'core'), 0, 0, tiled=True)  8.09 us
  transfers between devices with their start and end apart: 27, of which 7 were waited for; matrix products, arithmetic and copies ran while one was open for 1% of the time, Pallas kernels for 28%

profile of v6, /device:TPU:1, one launch (start us, length us, event | category | flops | bytes accessed | tf_op | source)
XLA Modules:
  0.0 158.1 jit_solution(1970133025286768515)
XLA Ops:
  7.2 0.0 all-gather.2.cloned.1.call-start
  7.2 0.8 constant_dynamic-update-slice_fusion.6
  8.0 2.0 %collective-permute-start = (bf16[16,1024]{1,0:T(8,128)(2,1)S(1)}, bf16[16,1024]{1,0:T(8,128)(2,1)S(1)}, u32[]{:S(2)}, u32[]{:S(2)}) collective-permute-start(bf16[16,1024]{1,0:T(8,128)(2,1)S(1)} %get-tuple-element.47), channel_id=1, source_target_pairs={{0,4},{4,8},{8,12},{12,0},{1,5},{5,9},{9,13},{13,1},{2,6},{6,10},{... | collective-permute-start | bytes 98312 | tf_op jit(solution)/shard_map/ppermute | solution.py:276
  10.0 2.5 %collective-permute-start.1 = (bf16[16,1024]{1,0:T(8,128)(2,1)S(1)}, bf16[16,1024]{1,0:T(8,128)(2,1)S(1)}, u32[]{:S(2)}, u32[]{:S(2)}) collective-permute-start(bf16[16,1024]{1,0:T(8,128)(2,1)S(1)} %get-tuple-element.47), channel_id=1, source_target_pairs={{0,8},{4,12},{8,0},{12,4},{1,9},{5,13},{9,1},{13,5},{2,10},{6,14},... | collective-permute-start | bytes 98312 | tf_op jit(solution)/shard_map/ppermute | solution.py:276
  12.5 1.2 collective-permute-start.2
  13.6 0.1 stack.147.idx
  13.7 4.3 %far.2 = (s16[272,1024]{1,0:T(8,128)(2,1)}, s16[272,1024]{1,0:T(8,128)(2,1)}, f32[8,1024]{1,0:T(8,128)S(1)}) custom-call(s32[32]{0:T(128)S(1)} %stack.147.idx, bf16[512,4096]{1,0:T(8,128)(2,1)} %t3.7, bf16[512,4096]{1,0:T(8,128)(2,1)} %t3.7, bf16[512,4096]{1,0:T(8,128)(2,1)} %t3.7, bf16[512,4096]{1,0:T(8,128)(2,1)} %t3.7, bf16[512,1024]{1,0:T(8,128)(2,1)} %c.9), custom_call_target="tpu_custom_call" | custom-call | flops 536870912 | bytes 3145728 | tf_op jit(solution)/shard_map/far/pallas_call | solution.py:290
  18.0 0.0 collective-permute-done.w
  18.0 0.6 copy-done.9
  18.6 0.0 collective-permute-done.1
  18.6 0.0 collective-permute-done.2
  18.6 0.8 pad_maximum_fusion.refs_0_
  19.4 1.4 collective-permute-start.3
  20.8 2.6 %collective-permute-start.4 = (bf16[64,1024]{1,0:T(8,128)(2,1)S(1)}, bf16[64,1024]{1,0:T(8,128)(2,1)S(1)}, u32[]{:S(2)}, u32[]{:S(2)}) collective-permute-start(bf16[64,1024]{1,0:T(8,128)(2,1)S(1)} %pad_maximum_fusion.refs_0_), channel_id=1, source_target_pairs={{0,2},{1,3},{2,0},{3,1},{4,6},{5,7},{6,4},{7,5},{8,10},{9,11},{10,... | collective-permute-start | bytes 393224 | tf_op jit(solution)/shard_map/ppermute | solution.py:276
  23.4 1.1 collective-permute-start.5
  24.5 0.8 constant_dynamic-update-slice_fusion.5
  25.2 0.0 copy-start.7
  25.3 0.0 copy-start.10
  25.3 4.4 %far.3 = (s16[272,1024]{1,0:T(8,128)(2,1)}, s16[272,1024]{1,0:T(8,128)(2,1)}, f32[8,1024]{1,0:T(8,128)}) custom-call(s32[32]{0:T(128)S(1)} %stack.147.idx, bf16[512,4096]{1,0:T(8,128)(2,1)} %t3.7, bf16[512,4096]{1,0:T(8,128)(2,1)} %t3.7, bf16[512,4096]{1,0:T(8,128)(2,1)} %t3.7, bf16[512,4096]{1,0:T(8,128)(2,1)} %t3.7, bf16[512,1024]{1,0:T(8,128)(2,1)} %c.9, ...), custom_call_target="tpu_custom_call" | custom-call | flops 536870912 | bytes 3145728 | tf_op jit(solution)/shard_map/far/pallas_call | solution.py:290
  29.6 0.0 collective-permute-done.3.w
  29.6 0.6 copy-done.8
  30.3 0.9 constant_dynamic-update-slice_fusion.2
  31.2 0.0 collective-permute-done.5
  31.3 0.9 copy-done.6
  32.1 0.0 all-gather.2.cloned.1.call-update
  32.2 0.4 collective-permute-start.8
  32.6 2.4 %collective-permute-start.9 = (s16[272,1024]{1,0:T(8,128)(2,1)S(1)}, s16[272,1024]{1,0:T(8,128)(2,1)S(1)}, u32[]{:S(2)}, u32[]{:S(2)}) collective-permute-start(s16[272,1024]{1,0:T(8,128)(2,1)S(1)} %copy-done.10), channel_id=1, source_target_pairs={{0,12},{4,0},{8,4},{12,8},{1,13},{5,1},{9,5},{13,9},{2,14},{6,2},{... | collective-permute-start | bytes 1671176 | tf_op jit(solution)/shard_map/ppermute | solution.py:262
  34.9 0.4 collective-permute-start.10
  35.3 2.3 %collective-permute-start.11 = (s16[272,1024]{1,0:T(8,128)(2,1)}, s16[272,1024]{1,0:T(8,128)(2,1)S(1)}, u32[]{:S(2)}, u32[]{:S(2)}) collective-permute-start(s16[272,1024]{1,0:T(8,128)(2,1)} %get-tuple-element.31), channel_id=1, source_target_pairs={{0,3},{1,0},{2,1},{3,2},{4,7},{5,4},{6,5},{7,6},{8,11},{9,8},{10,9... | collective-permute-start | bytes 1671176 | tf_op jit(solution)/shard_map/ppermute | solution.py:262
  37.6 8.4 %near.1 = (s16[272,1024]{1,0:T(8,128)(2,1)}, s16[272,1024]{1,0:T(8,128)(2,1)}, s16[272,1024]{1,0:T(8,128)(2,1)}, s16[272,1024]{1,0:T(8,128)(2,1)}, f32[1024,1024]{1,0:T(8,128)S(1)}) custom-call(s32[32]{0:T(128)S(1)} %stack.147.idx, bf16[512,4096]{1,0:T(8,128)(2,1)} %t3.7, bf16[512,4096]{1,0:T(8,128)(2,1)} %t3.7, bf16[512,4096]{1,0:T(8,128)(2,1)} %t3.7, ...), custom_call_target="tpu_custom_call" | custom-call | flops 2147483648 | bytes 11534336 | tf_op jit(solution)/shard_map/near/pallas_call | solution.py:312
  46.0 0.0 collective-permute-start.14
  46.1 2.7 %collective-permute-start.15 = (s16[272,1024]{1,0:T(8,128)(2,1)}, s16[272,1024]{1,0:T(8,128)(2,1)S(1)}, u32[]{:S(2)}, u32[]{:S(2)}) collective-permute-start(s16[272,1024]{1,0:T(8,128)(2,1)} %get-tuple-element.35), channel_id=1, source_target_pairs={{0,3},{1,0},{2,1},{3,2},{4,7},{5,4},{6,5},{7,6},{8,11},{9,8},{10,9... | collective-permute-start | bytes 1671176 | tf_op jit(solution)/shard_map/ppermute | solution.py:262
  48.7 0.0 collective-permute-done.9.refs_1_
  48.7 2.7 %collective-permute-start.7 = (s16[272,1024]{1,0:T(8,128)(2,1)}, s16[272,1024]{1,0:T(8,128)(2,1)S(1)}, u32[]{:S(2)}, u32[]{:S(2)}) collective-permute-start(s16[272,1024]{1,0:T(8,128)(2,1)} %get-tuple-element.28), channel_id=1, source_target_pairs={{0,12},{4,0},{8,4},{12,8},{1,13},{5,1},{9,5},{13,9},{2,14},{6,2},{... | collective-permute-start | bytes 1671176 | tf_op jit(solution)/shard_map/ppermute | solution.py:262
  51.4 3.9 %relay.1 = (s16[272,1024]{1,0:T(8,128)(2,1)}, s16[272,1024]{1,0:T(8,128)(2,1)}, s16[272,1024]{1,0:T(8,128)(2,1)}, s16[272,1024]{1,0:T(8,128)(2,1)}) custom-call(f32[1024,1024]{1,0:T(8,128)S(1)} %get-tuple-element.29.keep, f32[8,1024]{1,0:T(8,128)S(1)} %get-tuple-element.26.ce, s16[272,1024]{1,0:T(8,128)(2,1)S(1)} %collective-permute-done.8.refs_0_, ...), custom_call_target="tpu_custom_call" | custom-call | flops 1048576 | bytes 8388608 | tf_op jit(solution)/shard_map/relay/pallas_call | solution.py:341
  55.3 4.5 %collective-permute-done.14.refs_4_ = s16[272,1024]{1,0:T(8,128)(2,1)S(1)} collective-permute-done((s16[272,1024]{1,0:T(8,128)(2,1)}, s16[272,1024]{1,0:T(8,128)(2,1)S(1)}, u32[]{:S(2)}, u32[]{:S(2)}) %collective-permute-start.14) | collective-permute-done | bytes 557088 | tf_op jit(solution)/shard_map/ppermute | solution.py:262
  59.9 0.3 collective-permute-start.13
  60.2 0.2 collective-permute-done.6.refs_0_
  60.3 2.5 %collective-permute-start.17 = (s16[272,1024]{1,0:T(8,128)(2,1)}, s16[272,1024]{1,0:T(8,128)(2,1)S(1)}, u32[]{:S(2)}, u32[]{:S(2)}) collective-permute-start(s16[272,1024]{1,0:T(8,128)(2,1)} %get-tuple-element.37), channel_id=1, source_target_pairs={{0,3},{1,0},{2,1},{3,2},{4,7},{5,4},{6,5},{7,6},{8,11},{9,8},{10,9... | collective-permute-start | bytes 1671176 | tf_op jit(solution)/shard_map/ppermute | solution.py:262
  62.8 3.7 %own.1.keep = f32[1024,1024]{1,0:T(8,128)S(1)} custom-call(s32[32]{0:T(128)S(1)} %stack.147.idx, bf16[512,4096]{1,0:T(8,128)(2,1)} %t3.7, bf16[512,4096]{1,0:T(8,128)(2,1)} %t3.7, bf16[512,4096]{1,0:T(8,128)(2,1)} %t3.7, bf16[512,4096]{1,0:T(8,128)(2,1)} %t3.7, bf16[512,1024]{1,0:T(8,128)(2,1)} %c.9), custom_call_target="tpu_custom_call" | custom-call | flops 1073741824 | bytes 8388608 | tf_op jit(solution)/shard_map/own/pallas_call | solution.py:327
  66.5 0.0 copy-start.1
  66.6 0.0 copy-start.3
  66.6 0.0 copy-start.4
  66.6 5.7 %collective-permute-done.12.refs_2_ = s16[272,1024]{1,0:T(8,128)(2,1)S(1)} collective-permute-done((s16[272,1024]{1,0:T(8,128)(2,1)}, s16[272,1024]{1,0:T(8,128)(2,1)S(1)}, u32[]{:S(2)}, u32[]{:S(2)}) %collective-permute-start.12) | collective-permute-done | bytes 557088 | tf_op jit(solution)/shard_map/ppermute | solution.py:262
  72.3 0.7 collective-permute-done.13.refs_3_
  73.0 4.3 %cross.1 = (f32[128,1024]{1,0:T(8,128)}, s16[144,1024]{1,0:T(8,128)(2,1)}, s16[144,1024]{1,0:T(8,128)(2,1)}, s16[144,1024]{1,0:T(8,128)(2,1)}, f32[128,1024]{1,0...) custom-call(f32[1024,1024]{1,0:T(8,128)S(1)} %own.1.keep, ...), custom_call_target="tpu_custom_call" | custom-call | flops 1048576 | bytes 12582912 | tf_op jit(solution)/shard_map/cross/pallas_call | solution.py:353
  77.2 1.6 %collective-permute-start.22 = (s16[144,1024]{1,0:T(8,128)(2,1)}, s16[144,1024]{1,0:T(8,128)(2,1)S(1)}, u32[]{:S(2)}, u32[]{:S(2)}) collective-permute-start(s16[144,1024]{1,0:T(8,128)(2,1)} %get-tuple-element.44), channel_id=1, source_target_pairs={{0,2},{1,3},{2,0},{3,1},{4,6},{5,7},{6,4},{7,5},{8,10},{9,11},{10,... | collective-permute-start | bytes 884744 | tf_op jit(solution)/shard_map/ppermute | solution.py:262
  78.9 1.0 collective-permute-start.23
  79.9 1.1 collective-permute-start.18
  81.0 3.5 %collective-permute-start.19 = (s16[144,1024]{1,0:T(8,128)(2,1)}, s16[144,1024]{1,0:T(8,128)(2,1)S(1)}, u32[]{:S(2)}, u32[]{:S(2)}) collective-permute-start(s16[144,1024]{1,0:T(8,128)(2,1)} %get-tuple-element.40), channel_id=1, source_target_pairs={{0,8},{4,12},{8,0},{12,4},{1,9},{5,13},{9,1},{13,5},{2,10},{6,14},... | collective-permute-start | bytes 884744 | tf_op jit(solution)/shard_map/ppermute | solution.py:262
  84.5 2.9 %collective-permute-done.21.n1 = s16[144,1024]{1,0:T(8,128)(2,1)S(1)} collective-permute-done((s16[144,1024]{1,0:T(8,128)(2,1)}, s16[144,1024]{1,0:T(8,128)(2,1)S(1)}, u32[]{:S(2)}, u32[]{:S(2)}) %collective-permute-start.21) | collective-permute-done | bytes 294944 | tf_op jit(solution)/shard_map/ppermute | solution.py:262
  87.4 8.3 %collective-permute-start.20 = (s16[144,1024]{1,0:T(8,128)(2,1)}, s16[144,1024]{1,0:T(8,128)(2,1)S(1)}, u32[]{:S(2)}, u32[]{:S(2)}) collective-permute-start(s16[144,1024]{1,0:T(8,128)(2,1)} %get-tuple-element.41), channel_id=1, source_target_pairs={{0,12},{4,0},{8,4},{12,8},{1,13},{5,1},{9,5},{13,9},{2,14},{6,2},{... | collective-permute-start | bytes 884744 | tf_op jit(solution)/shard_map/ppermute | solution.py:262
  95.7 3.0 %rotate.2.refs_0_ = s16[256,1152]{1,0:T(8,128)(2,1)} custom-call(f32[128,1024]{1,0:T(8,128)} %get-tuple-element.42.own, s16[144,1024]{1,0:T(8,128)(2,1)S(1)} %collective-permute-done.21.n1, s16[144,1024]{1,0:T(8,128)(2,1)S(1)} %collective-permute-done.22.n2, s16[144,1024]{1,0:T(8,128)(2,1)S(1)} %collective-permute-done.23.n3, s32[256,1024]{1,0:T(8,128)S(1)} %copy-done.1, ...), custom_call_target="tpu_custom_call" | custom-call | flops 134217728 | bytes 2097152 | tf_op jit(solution)/shard_map/rotate/pallas_call | solution.py:371
  98.7 1.4 collective-permute-done.20.n3
  100.1 3.0 %rotate.3.after = s16[256,1152]{1,0:T(8,128)(2,1)} custom-call(f32[128,1024]{1,0:T(8,128)} %get-tuple-element.38.own, s16[144,1024]{1,0:T(8,128)(2,1)S(1)} %collective-permute-done.18.n1, s16[144,1024]{1,0:T(8,128)(2,1)S(1)} %collective-permute-done.19.n2, s16[144,1024]{1,0:T(8,128)(2,1)S(1)} %collective-permute-done.20.n3, ...), custom_call_target="tpu_custom_call", output_to_operand_aliasing={{}: (7, {})} | custom-call | flops 134217728 | bytes 2097152 | tf_op jit(solution)/shard_map/rotate/pallas_call | solution.py:371
  103.1 3.1 %collective-permute-start.24 = (bf16[2048,1024]{1,0:T(8,128)(2,1)}, bf16[2048,1024]{1,0:T(8,128)(2,1)}, u32[]{:S(2)}, u32[]{:S(2)}) collective-permute-start(bf16[2048,1024]{1,0:T(8,128)(2,1)} %tie.5), channel_id=1, source_target_pairs={{0,16},{16,0},{1,17},{17,1},{2,18},{18,2},{3,19},{19,3},{4,20},{20... | collective-permute-start | bytes 12582920 | tf_op jit(solution)/shard_map/ppermute | solution.py:390
  106.2 8.1 %all-to-all-start = ((s16[16,16,1152]{2,1,0:T(8,128)(2,1)}), s16[16,16,1152]{2,1,0:T(8,128)(2,1)S(1)}, u32[]{:S(2)}, u32[]{:S(2)}) async-start(s16[16,16,1152]{2,1,0:T(8,128)(2,1)} %bitcast.38), calls=%async_computation | async-start | bytes 1179648 | tf_op jit(solution)/shard_map/all_to_all | solution.py:387
  114.9 0.1 pad_add_fusion.at
  115.0 2.2 %copy-done.2 = bf16[2048,1024]{1,0:T(8,128)(2,1)S(1)} copy-done((bf16[2048,1024]{1,0:T(8,128)(2,1)S(1)}, bf16[2048,1024]{1,0:T(8,128)(2,1)}, u32[]{:S(2)}) %copy-start.2) | copy-done | bytes 4194328
  117.2 8.8 %input_grad.1.after = bf16[512,4096]{1,0:T(8,128)(2,1)} custom-call(s32[3]{0:T(128)S(1)} %pad_add_fusion.at, bf16[512,1024]{1,0:T(8,128)(2,1)S(1)} %copy-done, bf16[8,4,4,16,1024]{4,3,2,1,0:T(8,128)(2,1)S(1)} %bitcast.41, bf16[8,4,4,16,1024]{4,3,2,1,0:T(8,128)(2,1)} %bitcast.36.w_oth), custom_call_target="tpu_custom_call" | custom-call | flops 4294967296 | bytes 13631488 | tf_op jit(solution)/shard_map/input_grad/pallas_call | solution.py:393
  126.1 6.9 %all-to-all-done = s16[16,16,1152]{2,1,0:T(8,128)(2,1)S(1)} async-done(((s16[16,16,1152]{2,1,0:T(8,128)(2,1)}), s16[16,16,1152]{2,1,0:T(8,128)(2,1)S(1)}, u32[]{:S(2)}, u32[]{:S(2)}) %all-to-all-start) | async-done | bytes 589856 | tf_op jit(solution)/shard_map/all_to_all | solution.py:387
  133.0 1.0 levels.1
  133.9 16.1 %all_gather.7.q = s16[256,1152]{1,0:T(8,128)(2,1)S(1)} all-gather(s16[16,1152]{1,0:T(8,128)(2,1)S(1)} %levels.1), channel_id=1, replica_groups=mesh['z'=8,'core'=2,'x'=4,'y'=4] {'z','core'}, dimensions={0}, use_global_device_ids=true | all-gather | bytes 626688 | tf_op jit(solution)/shard_map/all_gather | solution.py:417
  150.0 1.2 finish.1
  (38 shorter events, 0.1 us)
Async XLA Ops:
  7.2 96.0 %all-gather.2.cloned.1.call-start = ((), (), s32[]{:S(2)}) async-start(), calls=%async_computation.1 | async-start | bytes 4718592 | tf_op jit(solution)/shard_map/all_gather | solution.py:309
  8.0 10.0 %collective-permute-start = (bf16[16,1024]{1,0:T(8,128)(2,1)S(1)}, bf16[16,1024]{1,0:T(8,128)(2,1)S(1)}, u32[]{:S(2)}, u32[]{:S(2)}) collective-permute-start(bf16[16,1024]{1,0:T(8,128)(2,1)S(1)} %get-tuple-element.47), channel_id=1, source_target_pairs={{0,4},{4,8},{8,12},{12,0},{1,5},{5,9},{9,13},{13,1},{2,6},{6,10},{... | collective-permute-start | bytes 98312 | tf_op jit(solution)/shard_map/ppermute | solution.py:276
  10.0 8.6 %collective-permute-start.1 = (bf16[16,1024]{1,0:T(8,128)(2,1)S(1)}, bf16[16,1024]{1,0:T(8,128)(2,1)S(1)}, u32[]{:S(2)}, u32[]{:S(2)}) collective-permute-start(bf16[16,1024]{1,0:T(8,128)(2,1)S(1)} %get-tuple-element.47), channel_id=1, source_target_pairs={{0,8},{4,12},{8,0},{12,4},{1,9},{5,13},{9,1},{13,5},{2,10},{6,14},... | collective-permute-start | bytes 98312 | tf_op jit(solution)/shard_map/ppermute | solution.py:276
  12.5 6.2 %collective-permute-start.2 = (bf16[16,1024]{1,0:T(8,128)(2,1)S(1)}, bf16[16,1024]{1,0:T(8,128)(2,1)S(1)}, u32[]{:S(2)}, u32[]{:S(2)}) collective-permute-start(bf16[16,1024]{1,0:T(8,128)(2,1)S(1)} %get-tuple-element.47), channel_id=1, source_target_pairs={{0,12},{4,0},{8,4},{12,8},{1,13},{5,1},{9,5},{13,9},{2,14},{6,2},{... | collective-permute-start | bytes 98312 | tf_op jit(solution)/shard_map/ppermute | solution.py:276
  18.0 0.6 copy-start.9
  19.4 10.2 %collective-permute-start.3 = (bf16[64,1024]{1,0:T(8,128)(2,1)S(1)}, bf16[64,1024]{1,0:T(8,128)(2,1)S(1)}, u32[]{:S(2)}, u32[]{:S(2)}) collective-permute-start(bf16[64,1024]{1,0:T(8,128)(2,1)S(1)} %pad_maximum_fusion.refs_0_), channel_id=1, source_target_pairs={{0,1},{1,2},{2,3},{3,0},{4,5},{5,6},{6,7},{7,4},{8,9},{9,10},{10,1... | collective-permute-start | bytes 393224 | tf_op jit(solution)/shard_map/ppermute | solution.py:276
  20.8 10.4 %collective-permute-start.4 = (bf16[64,1024]{1,0:T(8,128)(2,1)S(1)}, bf16[64,1024]{1,0:T(8,128)(2,1)S(1)}, u32[]{:S(2)}, u32[]{:S(2)}) collective-permute-start(bf16[64,1024]{1,0:T(8,128)(2,1)S(1)} %pad_maximum_fusion.refs_0_), channel_id=1, source_target_pairs={{0,2},{1,3},{2,0},{3,1},{4,6},{5,7},{6,4},{7,5},{8,10},{9,11},{10,... | collective-permute-start | bytes 393224 | tf_op jit(solution)/shard_map/ppermute | solution.py:276
  23.4 7.8 %collective-permute-start.5 = (bf16[64,1024]{1,0:T(8,128)(2,1)S(1)}, bf16[64,1024]{1,0:T(8,128)(2,1)S(1)}, u32[]{:S(2)}, u32[]{:S(2)}) collective-permute-start(bf16[64,1024]{1,0:T(8,128)(2,1)S(1)} %pad_maximum_fusion.refs_0_), channel_id=1, source_target_pairs={{0,3},{1,0},{2,1},{3,2},{4,7},{5,4},{6,5},{7,6},{8,11},{9,8},{10,9... | collective-permute-start | bytes 393224 | tf_op jit(solution)/shard_map/ppermute | solution.py:276
  25.2 6.9 %copy-start.7 = (s16[272,1024]{1,0:T(8,128)(2,1)S(1)}, s16[272,1024]{1,0:T(8,128)(2,1)}, u32[]{:S(2)}) copy-start(s16[272,1024]{1,0:T(8,128)(2,1)} %get-tuple-element.24.after) | copy-start | bytes 1671172
  25.3 7.3 %copy-start.10 = (s16[272,1024]{1,0:T(8,128)(2,1)S(1)}, s16[272,1024]{1,0:T(8,128)(2,1)}, u32[]{:S(2)}) copy-start(s16[272,1024]{1,0:T(8,128)(2,1)} %get-tuple-element.30) | copy-start | bytes 1671172
  29.6 0.7 copy-start.8
  31.3 0.9 copy-start.6
  32.2 13.9 %collective-permute-start.8 = (s16[272,1024]{1,0:T(8,128)(2,1)S(1)}, s16[272,1024]{1,0:T(8,128)(2,1)S(1)}, u32[]{:S(2)}, u32[]{:S(2)}) collective-permute-start(s16[272,1024]{1,0:T(8,128)(2,1)S(1)} %copy-done.7), channel_id=1, source_target_pairs={{0,4},{4,8},{8,12},{12,0},{1,5},{5,9},{9,13},{13,1},{2,6},{6,10},{... | collective-permute-start | bytes 1671176 | tf_op jit(solution)/shard_map/ppermute | solution.py:262
  32.6 16.2 %collective-permute-start.9 = (s16[272,1024]{1,0:T(8,128)(2,1)S(1)}, s16[272,1024]{1,0:T(8,128)(2,1)S(1)}, u32[]{:S(2)}, u32[]{:S(2)}) collective-permute-start(s16[272,1024]{1,0:T(8,128)(2,1)S(1)} %copy-done.10), channel_id=1, source_target_pairs={{0,12},{4,0},{8,4},{12,8},{1,13},{5,1},{9,5},{13,9},{2,14},{6,2},{... | collective-permute-start | bytes 1671176 | tf_op jit(solution)/shard_map/ppermute | solution.py:262
  34.9 13.8 %collective-permute-start.10 = (s16[272,1024]{1,0:T(8,128)(2,1)}, s16[272,1024]{1,0:T(8,128)(2,1)S(1)}, u32[]{:S(2)}, u32[]{:S(2)}) collective-permute-start(s16[272,1024]{1,0:T(8,128)(2,1)} %get-tuple-element.25.after), channel_id=1, source_target_pairs={{0,1},{1,2},{2,3},{3,0},{4,5},{5,6},{6,7},{7,4},{8,9},{9,10},{10,1... | collective-permute-start | bytes 1671176 | tf_op jit(solution)/shard_map/ppermute | solution.py:262
  35.3 16.1 %collective-permute-start.11 = (s16[272,1024]{1,0:T(8,128)(2,1)}, s16[272,1024]{1,0:T(8,128)(2,1)S(1)}, u32[]{:S(2)}, u32[]{:S(2)}) collective-permute-start(s16[272,1024]{1,0:T(8,128)(2,1)} %get-tuple-element.31), channel_id=1, source_target_pairs={{0,3},{1,0},{2,1},{3,2},{4,7},{5,4},{6,5},{7,6},{8,11},{9,8},{10,9... | collective-permute-start | bytes 1671176 | tf_op jit(solution)/shard_map/ppermute | solution.py:262
  46.0 13.8 %collective-permute-start.14 = (s16[272,1024]{1,0:T(8,128)(2,1)}, s16[272,1024]{1,0:T(8,128)(2,1)S(1)}, u32[]{:S(2)}, u32[]{:S(2)}) collective-permute-start(s16[272,1024]{1,0:T(8,128)(2,1)} %get-tuple-element.34), channel_id=1, source_target_pairs={{0,1},{1,2},{2,3},{3,0},{4,5},{5,6},{6,7},{7,4},{8,9},{9,10},{10,1... | collective-permute-start | bytes 1671176 | tf_op jit(solution)/shard_map/ppermute | solution.py:262
  46.1 14.1 %collective-permute-start.15 = (s16[272,1024]{1,0:T(8,128)(2,1)}, s16[272,1024]{1,0:T(8,128)(2,1)S(1)}, u32[]{:S(2)}, u32[]{:S(2)}) collective-permute-start(s16[272,1024]{1,0:T(8,128)(2,1)} %get-tuple-element.35), channel_id=1, source_target_pairs={{0,3},{1,0},{2,1},{3,2},{4,7},{5,4},{6,5},{7,6},{8,11},{9,8},{10,9... | collective-permute-start | bytes 1671176 | tf_op jit(solution)/shard_map/ppermute | solution.py:262
  48.7 11.6 %collective-permute-start.6 = (s16[272,1024]{1,0:T(8,128)(2,1)}, s16[272,1024]{1,0:T(8,128)(2,1)S(1)}, u32[]{:S(2)}, u32[]{:S(2)}) collective-permute-start(s16[272,1024]{1,0:T(8,128)(2,1)} %get-tuple-element.27), channel_id=1, source_target_pairs={{0,4},{4,8},{8,12},{12,0},{1,5},{5,9},{9,13},{13,1},{2,6},{6,10},{... | collective-permute-start | bytes 1671176 | tf_op jit(solution)/shard_map/ppermute | solution.py:262
  48.7 17.8 %collective-permute-start.7 = (s16[272,1024]{1,0:T(8,128)(2,1)}, s16[272,1024]{1,0:T(8,128)(2,1)S(1)}, u32[]{:S(2)}, u32[]{:S(2)}) collective-permute-start(s16[272,1024]{1,0:T(8,128)(2,1)} %get-tuple-element.28), channel_id=1, source_target_pairs={{0,12},{4,0},{8,4},{12,8},{1,13},{5,1},{9,5},{13,9},{2,14},{6,2},{... | collective-permute-start | bytes 1671176 | tf_op jit(solution)/shard_map/ppermute | solution.py:262
  55.3 16.9 %collective-permute-start.12 = (s16[272,1024]{1,0:T(8,128)(2,1)}, s16[272,1024]{1,0:T(8,128)(2,1)S(1)}, u32[]{:S(2)}, u32[]{:S(2)}) collective-permute-start(s16[272,1024]{1,0:T(8,128)(2,1)} %get-tuple-element.32), channel_id=1, source_target_pairs={{0,4},{4,8},{8,12},{12,0},{1,5},{5,9},{9,13},{13,1},{2,6},{6,10},{... | collective-permute-start | bytes 1671176 | tf_op jit(solution)/shard_map/ppermute | solution.py:262
  59.9 13.1 %collective-permute-start.13 = (s16[272,1024]{1,0:T(8,128)(2,1)}, s16[272,1024]{1,0:T(8,128)(2,1)S(1)}, u32[]{:S(2)}, u32[]{:S(2)}) collective-permute-start(s16[272,1024]{1,0:T(8,128)(2,1)} %get-tuple-element.33), channel_id=1, source_target_pairs={{0,12},{4,0},{8,4},{12,8},{1,13},{5,1},{9,5},{13,9},{2,14},{6,2},{... | collective-permute-start | bytes 1671176 | tf_op jit(solution)/shard_map/ppermute | solution.py:262
  60.2 12.8 %collective-permute-start.16 = (s16[272,1024]{1,0:T(8,128)(2,1)}, s16[272,1024]{1,0:T(8,128)(2,1)S(1)}, u32[]{:S(2)}, u32[]{:S(2)}) collective-permute-start(s16[272,1024]{1,0:T(8,128)(2,1)} %get-tuple-element.36), channel_id=1, source_target_pairs={{0,1},{1,2},{2,3},{3,0},{4,5},{5,6},{6,7},{7,4},{8,9},{9,10},{10,1... | collective-permute-start | bytes 1671176 | tf_op jit(solution)/shard_map/ppermute | solution.py:262
  60.3 12.6 %collective-permute-start.17 = (s16[272,1024]{1,0:T(8,128)(2,1)}, s16[272,1024]{1,0:T(8,128)(2,1)S(1)}, u32[]{:S(2)}, u32[]{:S(2)}) collective-permute-start(s16[272,1024]{1,0:T(8,128)(2,1)} %get-tuple-element.37), channel_id=1, source_target_pairs={{0,3},{1,0},{2,1},{3,2},{4,7},{5,4},{6,5},{7,6},{8,11},{9,8},{10,9... | collective-permute-start | bytes 1671176 | tf_op jit(solution)/shard_map/ppermute | solution.py:262
  66.5 29.1 %copy-start.1 = (s32[256,1024]{1,0:T(8,128)S(1)}, s32[256,1024]{1,0:T(8,128)}, u32[]{:S(2)}) copy-start(s32[256,1024]{1,0:T(8,128)} %signs.5) | copy-start | bytes 3145732
  66.6 29.1 %copy-start.3 = (bf16[128,128]{1,0:T(8,128)(2,1)S(1)}, bf16[128,128]{1,0:T(8,128)(2,1)}, u32[]{:S(2)}) copy-start(bf16[128,128]{1,0:T(8,128)(2,1)} %constant.188.clone.inner) | copy-start | bytes 98308
  66.6 29.1 %copy-start.4 = (bf16[128,128]{1,0:T(8,128)(2,1)S(1)}, bf16[128,128]{1,0:T(8,128)(2,1)}, u32[]{:S(2)}) copy-start(bf16[128,128]{1,0:T(8,128)(2,1)} %constant.189.clone.rows) | copy-start | bytes 98308
  77.2 10.2 %collective-permute-start.21 = (s16[144,1024]{1,0:T(8,128)(2,1)}, s16[144,1024]{1,0:T(8,128)(2,1)S(1)}, u32[]{:S(2)}, u32[]{:S(2)}) collective-permute-start(s16[144,1024]{1,0:T(8,128)(2,1)} %get-tuple-element.43), channel_id=1, source_target_pairs={{0,1},{1,2},{2,3},{3,0},{4,5},{5,6},{6,7},{7,4},{8,9},{9,10},{10,1... | collective-permute-start | bytes 884744 | tf_op jit(solution)/shard_map/ppermute | solution.py:262
  77.2 18.4 %collective-permute-start.22 = (s16[144,1024]{1,0:T(8,128)(2,1)}, s16[144,1024]{1,0:T(8,128)(2,1)S(1)}, u32[]{:S(2)}, u32[]{:S(2)}) collective-permute-start(s16[144,1024]{1,0:T(8,128)(2,1)} %get-tuple-element.44), channel_id=1, source_target_pairs={{0,2},{1,3},{2,0},{3,1},{4,6},{5,7},{6,4},{7,5},{8,10},{9,11},{10,... | collective-permute-start | bytes 884744 | tf_op jit(solution)/shard_map/ppermute | solution.py:262
  78.9 16.8 %collective-permute-start.23 = (s16[144,1024]{1,0:T(8,128)(2,1)}, s16[144,1024]{1,0:T(8,128)(2,1)S(1)}, u32[]{:S(2)}, u32[]{:S(2)}) collective-permute-start(s16[144,1024]{1,0:T(8,128)(2,1)} %get-tuple-element.45), channel_id=1, source_target_pairs={{0,3},{1,0},{2,1},{3,2},{4,7},{5,4},{6,5},{7,6},{8,11},{9,8},{10,9... | collective-permute-start | bytes 884744 | tf_op jit(solution)/shard_map/ppermute | solution.py:262
  79.9 18.8 %collective-permute-start.18 = (s16[144,1024]{1,0:T(8,128)(2,1)}, s16[144,1024]{1,0:T(8,128)(2,1)S(1)}, u32[]{:S(2)}, u32[]{:S(2)}) collective-permute-start(s16[144,1024]{1,0:T(8,128)(2,1)} %get-tuple-element.39), channel_id=1, source_target_pairs={{0,4},{4,8},{8,12},{12,0},{1,5},{5,9},{9,13},{13,1},{2,6},{6,10},{... | collective-permute-start | bytes 884744 | tf_op jit(solution)/shard_map/ppermute | solution.py:262
  81.0 17.7 %collective-permute-start.19 = (s16[144,1024]{1,0:T(8,128)(2,1)}, s16[144,1024]{1,0:T(8,128)(2,1)S(1)}, u32[]{:S(2)}, u32[]{:S(2)}) collective-permute-start(s16[144,1024]{1,0:T(8,128)(2,1)} %get-tuple-element.40), channel_id=1, source_target_pairs={{0,8},{4,12},{8,0},{12,4},{1,9},{5,13},{9,1},{13,5},{2,10},{6,14},... | collective-permute-start | bytes 884744 | tf_op jit(solution)/shard_map/ppermute | solution.py:262
  87.4 12.7 %collective-permute-start.20 = (s16[144,1024]{1,0:T(8,128)(2,1)}, s16[144,1024]{1,0:T(8,128)(2,1)S(1)}, u32[]{:S(2)}, u32[]{:S(2)}) collective-permute-start(s16[144,1024]{1,0:T(8,128)(2,1)} %get-tuple-element.41), channel_id=1, source_target_pairs={{0,12},{4,0},{8,4},{12,8},{1,13},{5,1},{9,5},{13,9},{2,14},{6,2},{... | collective-permute-start | bytes 884744 | tf_op jit(solution)/shard_map/ppermute | solution.py:262
  103.1 11.9 %copy-start = (bf16[512,1024]{1,0:T(8,128)(2,1)S(1)}, bf16[512,1024]{1,0:T(8,128)(2,1)}, u32[]{:S(2)}) copy-start(bf16[512,1024]{1,0:T(8,128)(2,1)} %c.9) | copy-start | bytes 3145732
  103.1 11.9 %collective-permute-start.24 = (bf16[2048,1024]{1,0:T(8,128)(2,1)}, bf16[2048,1024]{1,0:T(8,128)(2,1)}, u32[]{:S(2)}, u32[]{:S(2)}) collective-permute-start(bf16[2048,1024]{1,0:T(8,128)(2,1)} %tie.5), channel_id=1, source_target_pairs={{0,16},{16,0},{1,17},{17,1},{2,18},{18,2},{3,19},{19,3},{4,20},{20... | collective-permute-start | bytes 12582920 | tf_op jit(solution)/shard_map/ppermute | solution.py:390
  106.2 26.7 %all-to-all-start = ((s16[16,16,1152]{2,1,0:T(8,128)(2,1)}), s16[16,16,1152]{2,1,0:T(8,128)(2,1)S(1)}, u32[]{:S(2)}, u32[]{:S(2)}) async-start(s16[16,16,1152]{2,1,0:T(8,128)(2,1)} %bitcast.38), calls=%async_computation | async-start | bytes 1179648 | tf_op jit(solution)/shard_map/all_to_all | solution.py:387
  115.0 2.2 %copy-start.2 = (bf16[2048,1024]{1,0:T(8,128)(2,1)S(1)}, bf16[2048,1024]{1,0:T(8,128)(2,1)}, u32[]{:S(2)}) copy-start(bf16[2048,1024]{1,0:T(8,128)(2,1)} %tie.5) | copy-start | bytes 12582916
  117.2 15.7 %copy-start.5 = (bf16[16,16]{1,0:T(8,128)(2,1)S(1)}, bf16[16,16]{1,0:T(8,128)(2,1)}, u32[]{:S(2)}) copy-start(bf16[16,16]{1,0:T(8,128)(2,1)} %constant.190.clone.rows) | copy-start | bytes 1540
Sparse Core Ops, SparseCore 0:
  32.3 54.5 all-gather.1

commit v7 on v6

--- a/solution.py
+++ b/solution.py
@@ -211,11 +211,12 @@
 
 
 def input_grad_kernel(at, c, w_own, w_oth, out, w):
-    for j in range(4):
-        chip = ((at[1] + 4 - j) % 4) * 256
+    for j in range(2):
+        here = ((at[1] + 4 - j - 2 * at[2]) % 4) * 256
+        there = ((at[1] + 2 - j + 2 * at[2]) % 4) * 256
         for z in range(NZ):
-            w[pl.ds(pl.multiple_of(chip + z * 32 + at[2] * 16, 16), 16), :] = w_own[z, j, 0]
-            w[pl.ds(pl.multiple_of(chip + z * 32 + 16 - at[2] * 16, 16), 16), :] = w_oth[z, j, 0]
+            w[pl.ds(pl.multiple_of(here + z * 32, 32), 32), :] = w_own[z, j, 0]
+            w[pl.ds(pl.multiple_of(there + z * 32, 32), 32), :] = w_oth[z, j, 0]
     out[...] = lax.dot_general(c[...], w[...], (((1,), (1,)), ((), ())), preferred_element_type=F32).astype(BF16)
 
 
@@ -272,11 +273,16 @@
 
     z = lax.axis_index("z").astype(I32)
 
-    def spread(piece, axis):
-        return [lax.ppermute(piece, axis, shift(4, s)) for s in (1, 2, 3)]
-
-    piece = lax.dynamic_slice_in_dim(value_weights, (2 * z + core) * 16, 16, 0)
-    round1 = spread(piece, "x")
+    def along_y(v, steps):
+        pairs = []
+        for c, step in enumerate(steps):
+            if step is not None:
+                for k in range(NY):
+                    pairs.append((c * NY + k, c * NY + (k + step) % NY))
+        return lax.ppermute(v, ("core", "y"), pairs)
+
+    piece = lax.dynamic_slice_in_dim(value_weights, z * 32, 32, 0)
+    round1 = [lax.ppermute(piece, "x", shift(NX, s)) for s in (1, 2, 3)]
 
     def operands(where):
         tiles = [pl.BlockSpec((TOK, 128), lambda k, ids, t=t: (0, ids[where(k) + t])) for t in range(4)]
@@ -303,9 +309,11 @@
 
     up1x, down1x, ce = far(0)
     piece = jnp.concatenate([piece, tie(round1[0], up1x)] + round1[1:], 0)
-    round2 = spread(piece, "y")
+    came1 = along_y(piece, (1, 2))
+    came2 = along_y(piece, (None, 3))
     up1y, down1y, _ = far(1, piece)
-    piece = jnp.concatenate([piece, tie(round2[0], up1y)] + round2[1:], 0)
+    came1 = tie(came1, up1y)
+    piece = jnp.concatenate([jnp.where(core == 0, piece, came1), jnp.where(core == 0, came1, came2)], 0)
     w_own = lax.all_gather(piece, "z", axis=0, tiled=True)
     got1 = [send(up1x, 0, 1), send(down1x, 0, -1), send(up1y, 1, 1), send(down1y, 1, -1)]
 
@@ -389,7 +397,7 @@
     w_own = tie(w_own, spun)
     w_oth = lax.ppermute(w_own, "core", shift(NC, 1))
     place = jnp.stack([x, y, core]).astype(I32)
-    w_block = pl.BlockSpec((NZ, 4, 1, 16, KV), lambda k, at: (0, 0, k, 0, 0))
+    w_block = pl.BlockSpec((NZ, 2, 1, 32, KV), lambda k, at: (0, 0, k, 0, 0))
     input_grad = pl.pallas_call(
         input_grad_kernel,
         out_shape=pltpu.HBM((TOK, 4096), BF16),
@@ -403,7 +411,7 @@
         compiler_params=params(SMALL),
         cost_estimate=cost(4 * mm, 13 << 20),
         name="input_grad",
-    )(place, cotangent, w_own.reshape(NZ, 4, 4, 16, KV), w_oth.reshape(NZ, 4, 4, 16, KV))
+    )(place, cotangent, w_own.reshape(NZ, 2, 4, 32, KV), w_oth.reshape(NZ, 2, 4, 32, KV))
 
     back = pl.pallas_call(
         levels_kernel,

time: 159 us -> 162 us (1.019)
  waiting for transfers between devices: 22.3 us -> 32.9 us
  starting transfers between devices: 51 us -> 43.3 us
  local copies, waits for them, and re-layouts: 6.92 us -> 4.67 us
  other arithmetic: 0.85 us -> 2.94 us
    ppermute x18, starting transfers between devices: 29.1 us -> 18.2 us  [send(): return lax.ppermute(v, 'xy'[axis], shift((NX, NY)[axis], s))]
    ppermute x18, waiting for transfers between devices: 15.4 us -> 26 us  [send(): return lax.ppermute(v, 'xy'[axis], shift((NX, NY)[axis], s))]
    unnamed x28 -> x24, local copies, waits for them, and re-layouts: 6.8 us -> 4.56 us
    ppermute x1, starting transfers between devices: 3.07 us -> 5.19 us  [shards(): w_oth = lax.ppermute(w_own, 'core', shift(NC, 1))]
    ppermute x6 -> x5, starting transfers between devices: 10.7 us -> 11.3 us  [the longest x2 5.66 us: along_y(): return lax.ppermute(v, ('core', 'y'), pairs)]
  transfers between devices with their start and end apart: 27 -> 26, of which waited for: 7 -> 10; matrix products, arithmetic and copies ran while one was open for 1% -> 0% of each run, Pallas kernels for 28% -> 27%
where the time goes in v7:
time: 162 us; the launch traced here: 161 us
  Pallas kernels  46 us (28%)
  starting transfers between devices  43.3 us (27%)
  waiting for transfers between devices  32.9 us (20%)
  blocking collectives  16.1 us (10%)
  between operations  14.9 us (9%)
  local copies, waits for them, and re-layouts  4.67 us (3%)
  other arithmetic  2.94 us (2%)
    ppermute x18, waiting for transfers between devices, send(): return lax.ppermute(v, 'xy'[axis], shift((NX, NY)[axis], s))  26 us
    ppermute x18, starting transfers between devices, send(): return lax.ppermute(v, 'xy'[axis], shift((NX, NY)[axis], s))  18.2 us
    all_gather x1, blocking collectives, shards(): gathered = lax.all_gather(back, ('z', 'core'), axis=0, tiled=True)  16.1 us
    pallas_call x1, Pallas kernels, shards(): pl.pallas_call(input_grad_kernel, out_shape=pltpu.HBM((TOK, 4096), BF16),...  8.85 us
    all_to_all x1, starting transfers between devices, shards(): groups = lax.all_to_all(spun, ('z', 'core'), 0, 0, tiled=True)  8.65 us
    pallas_call x2, Pallas kernels, far(): pl.pallas_call(far_kernel, out_shape=(message, message, sds((8, KV), F32)...  8.64 us
    pallas_call x1, Pallas kernels, shards(): pl.pallas_call(near_kernel, out_shape=(message,) * 4 + (sds((1024, KV), F...  8.43 us
    all_to_all x1, waiting for transfers between devices, shards(): groups = lax.all_to_all(spun, ('z', 'core'), 0, 0, tiled=True)  6.88 us
  transfers between devices with their start and end apart: 26, of which 10 were waited for; matrix products, arithmetic and copies ran while one was open for 0% of the time, Pallas kernels for 27%

profile of v7, /device:TPU:1, one launch (start us, length us, event | category | flops | bytes accessed | tf_op | source)
XLA Modules:
  0.0 160.8 jit_solution(17684316906486179262)
XLA Ops:
  7.2 0.0 copy-start
  7.2 0.0 all-gather.2.cloned.1.call-start
  7.2 1.0 copy-done
  8.2 2.0 %collective-permute-start = (bf16[32,1024]{1,0:T(8,128)(2,1)S(1)}, bf16[32,1024]{1,0:T(8,128)(2,1)S(1)}, u32[]{:S(2)}, u32[]{:S(2)}) collective-permute-start(bf16[32,1024]{1,0:T(8,128)(2,1)S(1)} %constant_dynamic-slice_fusion), channel_id=1, source_target_pairs={{0,4},{4,8},{8,12},{12,0},{1,5},{5,9},{9,13},{13,1},{2,6},{6,10},{... | collective-permute-start | bytes 196616 | tf_op jit(solution)/shard_map/ppermute | solution.py:285
  10.3 2.5 %collective-permute-start.1 = (bf16[32,1024]{1,0:T(8,128)(2,1)S(1)}, bf16[32,1024]{1,0:T(8,128)(2,1)S(1)}, u32[]{:S(2)}, u32[]{:S(2)}) collective-permute-start(bf16[32,1024]{1,0:T(8,128)(2,1)S(1)} %constant_dynamic-slice_fusion), channel_id=1, source_target_pairs={{0,8},{4,12},{8,0},{12,4},{1,9},{5,13},{9,1},{13,5},{2,10},{6,14},... | collective-permute-start | bytes 196616 | tf_op jit(solution)/shard_map/ppermute | solution.py:285
  12.7 1.2 collective-permute-start.2
  13.9 0.1 stack.147.idx
  14.0 4.3 %far.2 = (s16[272,1024]{1,0:T(8,128)(2,1)}, s16[272,1024]{1,0:T(8,128)(2,1)}, f32[8,1024]{1,0:T(8,128)S(1)}) custom-call(s32[32]{0:T(128)S(1)} %stack.147.idx, bf16[512,4096]{1,0:T(8,128)(2,1)} %t3.7, bf16[512,4096]{1,0:T(8,128)(2,1)} %t3.7, bf16[512,4096]{1,0:T(8,128)(2,1)} %t3.7, bf16[512,4096]{1,0:T(8,128)(2,1)} %t3.7, bf16[512,1024]{1,0:T(8,128)(2,1)} %c.9), custom_call_target="tpu_custom_call" | custom-call | flops 536870912 | bytes 3145728 | tf_op jit(solution)/shard_map/far/pallas_call | solution.py:296
  18.3 0.0 collective-permute-done.w
  18.3 0.6 copy-done.8
  18.9 0.9 pad_maximum_fusion.1.refs_0_
  19.8 3.0 %collective-permute-start.3 = (bf16[128,1024]{1,0:T(8,128)(2,1)S(1)}, bf16[128,1024]{1,0:T(8,128)(2,1)S(1)}, u32[]{:S(2)}, u32[]{:S(2)}) collective-permute-start(bf16[128,1024]{1,0:T(8,128)(2,1)S(1)} %pad_maximum_fusion.1.refs_0_), channel_id=1, source_target_pairs={{0,1},{1,2},{2,3},{3,0},{16,18},{17,19},{18,16},{19,17},{4,5},{5,6... | collective-permute-start | bytes 786440 | tf_op jit(solution)/shard_map/ppermute | solution.py:282
  22.7 2.7 %collective-permute-start.4 = (bf16[128,1024]{1,0:T(8,128)(2,1)S(1)}, bf16[128,1024]{1,0:T(8,128)(2,1)S(1)}, u32[]{:S(2)}, u32[]{:S(2)}) collective-permute-start(bf16[128,1024]{1,0:T(8,128)(2,1)S(1)} %pad_maximum_fusion.1.refs_0_), channel_id=1, source_target_pairs={{16,19},{17,16},{18,17},{19,18},{20,23},{21,20},{22,21},{23,22},{2... | collective-permute-start | bytes 786440 | tf_op jit(solution)/shard_map/ppermute | solution.py:282
  25.4 0.0 copy-start.10
  25.5 0.0 copy-start.11
  25.5 4.4 %far.3 = (s16[272,1024]{1,0:T(8,128)(2,1)}, s16[272,1024]{1,0:T(8,128)(2,1)}, f32[8,1024]{1,0:T(8,128)}) custom-call(s32[32]{0:T(128)S(1)} %stack.147.idx, bf16[512,4096]{1,0:T(8,128)(2,1)} %t3.7, bf16[512,4096]{1,0:T(8,128)(2,1)} %t3.7, bf16[512,4096]{1,0:T(8,128)(2,1)} %t3.7, bf16[512,4096]{1,0:T(8,128)(2,1)} %t3.7, bf16[512,1024]{1,0:T(8,128)(2,1)} %c.9, ...), custom_call_target="tpu_custom_call" | custom-call | flops 536870912 | bytes 3145728 | tf_op jit(solution)/shard_map/far/pallas_call | solution.py:296
  29.8 0.0 collective-permute-done.3.w
  29.8 0.7 copy-done.7
  30.5 0.0 collective-permute-done.4
  30.6 1.1 broadcast_select_fusion.1
  31.7 0.9 pad_maximum_fusion
  32.6 0.0 all-gather.2.cloned.1.call-update
  32.6 0.4 collective-permute-start.7
  33.0 2.4 %collective-permute-start.8 = (s16[272,1024]{1,0:T(8,128)(2,1)S(1)}, s16[272,1024]{1,0:T(8,128)(2,1)S(1)}, u32[]{:S(2)}, u32[]{:S(2)}) collective-permute-start(s16[272,1024]{1,0:T(8,128)(2,1)S(1)} %copy-done.11), channel_id=1, source_target_pairs={{0,12},{4,0},{8,4},{12,8},{1,13},{5,1},{9,5},{13,9},{2,14},{6,2},{... | collective-permute-start | bytes 1671176 | tf_op jit(solution)/shard_map/ppermute | solution.py:263
  35.4 0.7 collective-permute-start.9
  36.0 2.0 %collective-permute-start.10 = (s16[272,1024]{1,0:T(8,128)(2,1)}, s16[272,1024]{1,0:T(8,128)(2,1)S(1)}, u32[]{:S(2)}, u32[]{:S(2)}) collective-permute-start(s16[272,1024]{1,0:T(8,128)(2,1)} %get-tuple-element.31), channel_id=1, source_target_pairs={{0,3},{1,0},{2,1},{3,2},{4,7},{5,4},{6,5},{7,6},{8,11},{9,8},{10,9... | collective-permute-start | bytes 1671176 | tf_op jit(solution)/shard_map/ppermute | solution.py:263
  38.0 8.4 %near.1 = (s16[272,1024]{1,0:T(8,128)(2,1)}, s16[272,1024]{1,0:T(8,128)(2,1)}, s16[272,1024]{1,0:T(8,128)(2,1)}, s16[272,1024]{1,0:T(8,128)(2,1)}, f32[1024,1024]{1,0:T(8,128)S(1)}) custom-call(s32[32]{0:T(128)S(1)} %stack.147.idx, bf16[512,4096]{1,0:T(8,128)(2,1)} %t3.7, bf16[512,4096]{1,0:T(8,128)(2,1)} %t3.7, bf16[512,4096]{1,0:T(8,128)(2,1)} %t3.7, ...), custom_call_target="tpu_custom_call" | custom-call | flops 2147483648 | bytes 11534336 | tf_op jit(solution)/shard_map/near/pallas_call | solution.py:320
  46.5 0.0 collective-permute-start.13
  46.5 1.4 collective-permute-done.7.refs_0_
  47.9 1.7 %collective-permute-start.14 = (s16[272,1024]{1,0:T(8,128)(2,1)}, s16[272,1024]{1,0:T(8,128)(2,1)S(1)}, u32[]{:S(2)}, u32[]{:S(2)}) collective-permute-start(s16[272,1024]{1,0:T(8,128)(2,1)} %get-tuple-element.35), channel_id=1, source_target_pairs={{0,3},{1,0},{2,1},{3,2},{4,7},{5,4},{6,5},{7,6},{8,11},{9,8},{10,9... | collective-permute-start | bytes 1671176 | tf_op jit(solution)/shard_map/ppermute | solution.py:263
  49.6 0.0 collective-permute-done.8.refs_1_
  49.6 2.7 %collective-permute-start.6 = (s16[272,1024]{1,0:T(8,128)(2,1)}, s16[272,1024]{1,0:T(8,128)(2,1)S(1)}, u32[]{:S(2)}, u32[]{:S(2)}) collective-permute-start(s16[272,1024]{1,0:T(8,128)(2,1)} %get-tuple-element.28), channel_id=1, source_target_pairs={{0,12},{4,0},{8,4},{12,8},{1,13},{5,1},{9,5},{13,9},{2,14},{6,2},{... | collective-permute-start | bytes 1671176 | tf_op jit(solution)/shard_map/ppermute | solution.py:263
  52.3 3.9 %relay.1 = (s16[272,1024]{1,0:T(8,128)(2,1)}, s16[272,1024]{1,0:T(8,128)(2,1)}, s16[272,1024]{1,0:T(8,128)(2,1)}, s16[272,1024]{1,0:T(8,128)(2,1)}) custom-call(f32[1024,1024]{1,0:T(8,128)S(1)} %get-tuple-element.29.keep, f32[8,1024]{1,0:T(8,128)S(1)} %get-tuple-element.26.ce, s16[272,1024]{1,0:T(8,128)(2,1)S(1)} %collective-permute-done.7.refs_0_, ...), custom_call_target="tpu_custom_call" | custom-call | flops 1048576 | bytes 8388608 | tf_op jit(solution)/shard_map/relay/pallas_call | solution.py:349
  56.2 6.2 %collective-permute-done.13.refs_4_ = s16[272,1024]{1,0:T(8,128)(2,1)S(1)} collective-permute-done((s16[272,1024]{1,0:T(8,128)(2,1)}, s16[272,1024]{1,0:T(8,128)(2,1)S(1)}, u32[]{:S(2)}, u32[]{:S(2)}) %collective-permute-start.13) | collective-permute-done | bytes 557088 | tf_op jit(solution)/shard_map/ppermute | solution.py:263
  62.4 0.3 collective-permute-start.12
  62.7 0.1 collective-permute-start.15
  62.8 1.0 collective-permute-done.5.refs_0_
  63.8 1.6 collective-permute-start.16
  65.4 3.7 %own.1.keep = f32[1024,1024]{1,0:T(8,128)S(1)} custom-call(s32[32]{0:T(128)S(1)} %stack.147.idx, bf16[512,4096]{1,0:T(8,128)(2,1)} %t3.7, bf16[512,4096]{1,0:T(8,128)(2,1)} %t3.7, bf16[512,4096]{1,0:T(8,128)(2,1)} %t3.7, bf16[512,4096]{1,0:T(8,128)(2,1)} %t3.7, bf16[512,1024]{1,0:T(8,128)(2,1)} %c.9), custom_call_target="tpu_custom_call" | custom-call | flops 1073741824 | bytes 8388608 | tf_op jit(solution)/shard_map/own/pallas_call | solution.py:335
  69.1 0.0 copy-start.2
  69.1 0.0 copy-start.4
  69.1 0.0 copy-start.5
  69.1 6.6 %collective-permute-done.11.refs_2_ = s16[272,1024]{1,0:T(8,128)(2,1)S(1)} collective-permute-done((s16[272,1024]{1,0:T(8,128)(2,1)}, s16[272,1024]{1,0:T(8,128)(2,1)S(1)}, u32[]{:S(2)}, u32[]{:S(2)}) %collective-permute-start.11) | collective-permute-done | bytes 557088 | tf_op jit(solution)/shard_map/ppermute | solution.py:263
  75.8 1.3 collective-permute-done.15.refs_6_
  77.0 4.2 %cross.1 = (f32[128,1024]{1,0:T(8,128)}, s16[144,1024]{1,0:T(8,128)(2,1)}, s16[144,1024]{1,0:T(8,128)(2,1)}, s16[144,1024]{1,0:T(8,128)(2,1)}, f32[128,1024]{1,0...) custom-call(f32[1024,1024]{1,0:T(8,128)S(1)} %own.1.keep, ...), custom_call_target="tpu_custom_call" | custom-call | flops 1048576 | bytes 12582912 | tf_op jit(solution)/shard_map/cross/pallas_call | solution.py:361
  81.3 1.9 %collective-permute-start.21 = (s16[144,1024]{1,0:T(8,128)(2,1)}, s16[144,1024]{1,0:T(8,128)(2,1)S(1)}, u32[]{:S(2)}, u32[]{:S(2)}) collective-permute-start(s16[144,1024]{1,0:T(8,128)(2,1)} %get-tuple-element.44), channel_id=1, source_target_pairs={{0,2},{1,3},{2,0},{3,1},{4,6},{5,7},{6,4},{7,5},{8,10},{9,11},{10,... | collective-permute-start | bytes 884744 | tf_op jit(solution)/shard_map/ppermute | solution.py:263
  83.2 0.9 collective-permute-start.22
  84.1 1.7 %collective-permute-start.17 = (s16[144,1024]{1,0:T(8,128)(2,1)}, s16[144,1024]{1,0:T(8,128)(2,1)S(1)}, u32[]{:S(2)}, u32[]{:S(2)}) collective-permute-start(s16[144,1024]{1,0:T(8,128)(2,1)} %get-tuple-element.39), channel_id=1, source_target_pairs={{0,4},{4,8},{8,12},{12,0},{1,5},{5,9},{9,13},{13,1},{2,6},{6,10},{... | collective-permute-start | bytes 884744 | tf_op jit(solution)/shard_map/ppermute | solution.py:263
  85.7 1.9 %collective-permute-start.18 = (s16[144,1024]{1,0:T(8,128)(2,1)}, s16[144,1024]{1,0:T(8,128)(2,1)S(1)}, u32[]{:S(2)}, u32[]{:S(2)}) collective-permute-start(s16[144,1024]{1,0:T(8,128)(2,1)} %get-tuple-element.40), channel_id=1, source_target_pairs={{0,8},{4,12},{8,0},{12,4},{1,9},{5,13},{9,1},{13,5},{2,10},{6,14},... | collective-permute-start | bytes 884744 | tf_op jit(solution)/shard_map/ppermute | solution.py:263
  87.7 4.2 %collective-permute-done.20.n1 = s16[144,1024]{1,0:T(8,128)(2,1)S(1)} collective-permute-done((s16[144,1024]{1,0:T(8,128)(2,1)}, s16[144,1024]{1,0:T(8,128)(2,1)S(1)}, u32[]{:S(2)}, u32[]{:S(2)}) %collective-permute-start.20) | collective-permute-done | bytes 294944 | tf_op jit(solution)/shard_map/ppermute | solution.py:263
  91.9 0.6 collective-permute-done.21.n2
  92.5 4.3 %collective-permute-done.22.n3 = s16[144,1024]{1,0:T(8,128)(2,1)S(1)} collective-permute-done((s16[144,1024]{1,0:T(8,128)(2,1)}, s16[144,1024]{1,0:T(8,128)(2,1)S(1)}, u32[]{:S(2)}, u32[]{:S(2)}) %collective-permute-start.22) | collective-permute-done | bytes 294944 | tf_op jit(solution)/shard_map/ppermute | solution.py:263
  96.8 3.0 %rotate.2.refs_0_ = s16[256,1152]{1,0:T(8,128)(2,1)} custom-call(f32[128,1024]{1,0:T(8,128)} %get-tuple-element.42.own, s16[144,1024]{1,0:T(8,128)(2,1)S(1)} %collective-permute-done.20.n1, s16[144,1024]{1,0:T(8,128)(2,1)S(1)} %collective-permute-done.21.n2, s16[144,1024]{1,0:T(8,128)(2,1)S(1)} %collective-permute-done.22.n3, s32[256,1024]{1,0:T(8,128)S(1)} %copy-done.2, ...), custom_call_target="tpu_custom_call" | custom-call | flops 134217728 | bytes 2097152 | tf_op jit(solution)/shard_map/rotate/pallas_call | solution.py:379
  99.8 0.3 collective-permute-done.19.n3
  100.2 3.0 %rotate.3.after = s16[256,1152]{1,0:T(8,128)(2,1)} custom-call(f32[128,1024]{1,0:T(8,128)} %get-tuple-element.38.own, s16[144,1024]{1,0:T(8,128)(2,1)S(1)} %collective-permute-done.17.n1, s16[144,1024]{1,0:T(8,128)(2,1)S(1)} %collective-permute-done.18.n2, s16[144,1024]{1,0:T(8,128)(2,1)S(1)} %collective-permute-done.19.n3, ...), custom_call_target="tpu_custom_call", output_to_operand_aliasing={{}: (7, {})} | custom-call | flops 134217728 | bytes 2097152 | tf_op jit(solution)/shard_map/rotate/pallas_call | solution.py:379
  103.2 5.2 %collective-permute-start.23 = (bf16[2048,1024]{1,0:T(8,128)(2,1)}, bf16[2048,1024]{1,0:T(8,128)(2,1)}, u32[]{:S(2)}, u32[]{:S(2)}) collective-permute-start(bf16[2048,1024]{1,0:T(8,128)(2,1)} %tie.5), channel_id=1, source_target_pairs={{0,16},{16,0},{1,17},{17,1},{2,18},{18,2},{3,19},{19,3},{4,20},{20... | collective-permute-start | bytes 12582920 | tf_op jit(solution)/shard_map/ppermute | solution.py:398
  108.4 8.7 %all-to-all-start = ((s16[16,16,1152]{2,1,0:T(8,128)(2,1)}), s16[16,16,1152]{2,1,0:T(8,128)(2,1)S(1)}, u32[]{:S(2)}, u32[]{:S(2)}) async-start(s16[16,16,1152]{2,1,0:T(8,128)(2,1)} %bitcast.43), calls=%async_computation | async-start | bytes 1179648 | tf_op jit(solution)/shard_map/all_to_all | solution.py:395
  117.7 0.1 pad_add_fusion.at
  117.8 2.2 %copy-done.3 = bf16[2048,1024]{1,0:T(8,128)(2,1)S(1)} copy-done((bf16[2048,1024]{1,0:T(8,128)(2,1)S(1)}, bf16[2048,1024]{1,0:T(8,128)(2,1)}, u32[]{:S(2)}) %copy-start.3) | copy-done | bytes 4194328
  120.0 8.8 %input_grad.1.after = bf16[512,4096]{1,0:T(8,128)(2,1)} custom-call(s32[3]{0:T(128)S(1)} %pad_add_fusion.at, bf16[512,1024]{1,0:T(8,128)(2,1)S(1)} %copy-done.1, bf16[8,2,4,32,1024]{4,3,2,1,0:T(8,128)(2,1)S(1)} %bitcast.41, bf16[8,2,4,32,1024]{4,3,2,1,0:T(8,128)(2,1)} %bitcast.36.w_oth), custom_call_target="tpu_custom_call" | custom-call | flops 4294967296 | bytes 13631488 | tf_op jit(solution)/shard_map/input_grad/pallas_call | solution.py:401
  128.8 6.9 %all-to-all-done = s16[16,16,1152]{2,1,0:T(8,128)(2,1)S(1)} async-done(((s16[16,16,1152]{2,1,0:T(8,128)(2,1)}), s16[16,16,1152]{2,1,0:T(8,128)(2,1)S(1)}, u32[]{:S(2)}, u32[]{:S(2)}) %all-to-all-start) | async-done | bytes 589856 | tf_op jit(solution)/shard_map/all_to_all | solution.py:395
  135.7 1.0 levels.1
  136.7 16.1 %all_gather.7.q = s16[256,1152]{1,0:T(8,128)(2,1)S(1)} all-gather(s16[16,1152]{1,0:T(8,128)(2,1)S(1)} %levels.1), channel_id=1, replica_groups=mesh['z'=8,'core'=2,'x'=4,'y'=4] {'z','core'}, dimensions={0}, use_global_device_ids=true | all-gather | bytes 626688 | tf_op jit(solution)/shard_map/all_gather | solution.py:425
  152.8 1.2 finish.1
  (34 shorter events, 0.1 us)
Async XLA Ops:
  7.2 1.0 copy-start
  7.2 96.0 %all-gather.2.cloned.1.call-start = ((), (), s32[]{:S(2)}) async-start(), calls=%async_computation.1 | async-start | bytes 4718592 | tf_op jit(solution)/shard_map/all_gather | solution.py:317
  8.2 10.0 %collective-permute-start = (bf16[32,1024]{1,0:T(8,128)(2,1)S(1)}, bf16[32,1024]{1,0:T(8,128)(2,1)S(1)}, u32[]{:S(2)}, u32[]{:S(2)}) collective-permute-start(bf16[32,1024]{1,0:T(8,128)(2,1)S(1)} %constant_dynamic-slice_fusion), channel_id=1, source_target_pairs={{0,4},{4,8},{8,12},{12,0},{1,5},{5,9},{9,13},{13,1},{2,6},{6,10},{... | collective-permute-start | bytes 196616 | tf_op jit(solution)/shard_map/ppermute | solution.py:285
  10.3 8.6 %collective-permute-start.1 = (bf16[32,1024]{1,0:T(8,128)(2,1)S(1)}, bf16[32,1024]{1,0:T(8,128)(2,1)S(1)}, u32[]{:S(2)}, u32[]{:S(2)}) collective-permute-start(bf16[32,1024]{1,0:T(8,128)(2,1)S(1)} %constant_dynamic-slice_fusion), channel_id=1, source_target_pairs={{0,8},{4,12},{8,0},{12,4},{1,9},{5,13},{9,1},{13,5},{2,10},{6,14},... | collective-permute-start | bytes 196616 | tf_op jit(solution)/shard_map/ppermute | solution.py:285
  12.7 6.2 %collective-permute-start.2 = (bf16[32,1024]{1,0:T(8,128)(2,1)S(1)}, bf16[32,1024]{1,0:T(8,128)(2,1)S(1)}, u32[]{:S(2)}, u32[]{:S(2)}) collective-permute-start(bf16[32,1024]{1,0:T(8,128)(2,1)S(1)} %constant_dynamic-slice_fusion), channel_id=1, source_target_pairs={{0,12},{4,0},{8,4},{12,8},{1,13},{5,1},{9,5},{13,9},{2,14},{6,2},{... | collective-permute-start | bytes 196616 | tf_op jit(solution)/shard_map/ppermute | solution.py:285
  18.3 0.6 copy-start.8
  19.8 10.1 %collective-permute-start.3 = (bf16[128,1024]{1,0:T(8,128)(2,1)S(1)}, bf16[128,1024]{1,0:T(8,128)(2,1)S(1)}, u32[]{:S(2)}, u32[]{:S(2)}) collective-permute-start(bf16[128,1024]{1,0:T(8,128)(2,1)S(1)} %pad_maximum_fusion.1.refs_0_), channel_id=1, source_target_pairs={{0,1},{1,2},{2,3},{3,0},{16,18},{17,19},{18,16},{19,17},{4,5},{5,6... | collective-permute-start | bytes 786440 | tf_op jit(solution)/shard_map/ppermute | solution.py:282
  22.7 7.8 %collective-permute-start.4 = (bf16[128,1024]{1,0:T(8,128)(2,1)S(1)}, bf16[128,1024]{1,0:T(8,128)(2,1)S(1)}, u32[]{:S(2)}, u32[]{:S(2)}) collective-permute-start(bf16[128,1024]{1,0:T(8,128)(2,1)S(1)} %pad_maximum_fusion.1.refs_0_), channel_id=1, source_target_pairs={{16,19},{17,16},{18,17},{19,18},{20,23},{21,20},{22,21},{23,22},{2... | collective-permute-start | bytes 786440 | tf_op jit(solution)/shard_map/ppermute | solution.py:282
  25.4 5.1 %copy-start.9 = (bf16[32,1024]{1,0:T(8,128)(2,1)S(1)}, bf16[32,1024]{1,0:T(8,128)(2,1)}, u32[]{:S(2)}) copy-start(bf16[32,1024]{1,0:T(8,128)(2,1)} %tie.3) | copy-start | bytes 196612
  25.4 7.1 %copy-start.10 = (s16[272,1024]{1,0:T(8,128)(2,1)S(1)}, s16[272,1024]{1,0:T(8,128)(2,1)}, u32[]{:S(2)}) copy-start(s16[272,1024]{1,0:T(8,128)(2,1)} %get-tuple-element.24.after) | copy-start | bytes 1671172
  25.5 7.5 %copy-start.11 = (s16[272,1024]{1,0:T(8,128)(2,1)S(1)}, s16[272,1024]{1,0:T(8,128)(2,1)}, u32[]{:S(2)}) copy-start(s16[272,1024]{1,0:T(8,128)(2,1)} %get-tuple-element.30) | copy-start | bytes 1671172
  29.8 0.7 copy-start.7
  32.6 15.3 %collective-permute-start.7 = (s16[272,1024]{1,0:T(8,128)(2,1)S(1)}, s16[272,1024]{1,0:T(8,128)(2,1)S(1)}, u32[]{:S(2)}, u32[]{:S(2)}) collective-permute-start(s16[272,1024]{1,0:T(8,128)(2,1)S(1)} %copy-done.10), channel_id=1, source_target_pairs={{0,4},{4,8},{8,12},{12,0},{1,5},{5,9},{9,13},{13,1},{2,6},{6,10},{... | collective-permute-start | bytes 1671176 | tf_op jit(solution)/shard_map/ppermute | solution.py:263
  33.0 16.6 %collective-permute-start.8 = (s16[272,1024]{1,0:T(8,128)(2,1)S(1)}, s16[272,1024]{1,0:T(8,128)(2,1)S(1)}, u32[]{:S(2)}, u32[]{:S(2)}) collective-permute-start(s16[272,1024]{1,0:T(8,128)(2,1)S(1)} %copy-done.11), channel_id=1, source_target_pairs={{0,12},{4,0},{8,4},{12,8},{1,13},{5,1},{9,5},{13,9},{2,14},{6,2},{... | collective-permute-start | bytes 1671176 | tf_op jit(solution)/shard_map/ppermute | solution.py:263
  35.4 16.9 %collective-permute-start.9 = (s16[272,1024]{1,0:T(8,128)(2,1)}, s16[272,1024]{1,0:T(8,128)(2,1)S(1)}, u32[]{:S(2)}, u32[]{:S(2)}) collective-permute-start(s16[272,1024]{1,0:T(8,128)(2,1)} %get-tuple-element.25.after), channel_id=1, source_target_pairs={{0,1},{1,2},{2,3},{3,0},{4,5},{5,6},{6,7},{7,4},{8,9},{9,10},{10,1... | collective-permute-start | bytes 1671176 | tf_op jit(solution)/shard_map/ppermute | solution.py:263
  36.0 13.6 %collective-permute-start.10 = (s16[272,1024]{1,0:T(8,128)(2,1)}, s16[272,1024]{1,0:T(8,128)(2,1)S(1)}, u32[]{:S(2)}, u32[]{:S(2)}) collective-permute-start(s16[272,1024]{1,0:T(8,128)(2,1)} %get-tuple-element.31), channel_id=1, source_target_pairs={{0,3},{1,0},{2,1},{3,2},{4,7},{5,4},{6,5},{7,6},{8,11},{9,8},{10,9... | collective-permute-start | bytes 1671176 | tf_op jit(solution)/shard_map/ppermute | solution.py:263
  46.5 16.0 %collective-permute-start.13 = (s16[272,1024]{1,0:T(8,128)(2,1)}, s16[272,1024]{1,0:T(8,128)(2,1)S(1)}, u32[]{:S(2)}, u32[]{:S(2)}) collective-permute-start(s16[272,1024]{1,0:T(8,128)(2,1)} %get-tuple-element.34), channel_id=1, source_target_pairs={{0,1},{1,2},{2,3},{3,0},{4,5},{5,6},{6,7},{7,4},{8,9},{9,10},{10,1... | collective-permute-start | bytes 1671176 | tf_op jit(solution)/shard_map/ppermute | solution.py:263
  47.9 14.8 %collective-permute-start.14 = (s16[272,1024]{1,0:T(8,128)(2,1)}, s16[272,1024]{1,0:T(8,128)(2,1)S(1)}, u32[]{:S(2)}, u32[]{:S(2)}) collective-permute-start(s16[272,1024]{1,0:T(8,128)(2,1)} %get-tuple-element.35), channel_id=1, source_target_pairs={{0,3},{1,0},{2,1},{3,2},{4,7},{5,4},{6,5},{7,6},{8,11},{9,8},{10,9... | collective-permute-start | bytes 1671176 | tf_op jit(solution)/shard_map/ppermute | solution.py:263
  49.6 14.2 %collective-permute-start.5 = (s16[272,1024]{1,0:T(8,128)(2,1)}, s16[272,1024]{1,0:T(8,128)(2,1)S(1)}, u32[]{:S(2)}, u32[]{:S(2)}) collective-permute-start(s16[272,1024]{1,0:T(8,128)(2,1)} %get-tuple-element.27), channel_id=1, source_target_pairs={{0,4},{4,8},{8,12},{12,0},{1,5},{5,9},{9,13},{13,1},{2,6},{6,10},{... | collective-permute-start | bytes 1671176 | tf_op jit(solution)/shard_map/ppermute | solution.py:263
  49.6 19.5 %collective-permute-start.6 = (s16[272,1024]{1,0:T(8,128)(2,1)}, s16[272,1024]{1,0:T(8,128)(2,1)S(1)}, u32[]{:S(2)}, u32[]{:S(2)}) collective-permute-start(s16[272,1024]{1,0:T(8,128)(2,1)} %get-tuple-element.28), channel_id=1, source_target_pairs={{0,12},{4,0},{8,4},{12,8},{1,13},{5,1},{9,5},{13,9},{2,14},{6,2},{... | collective-permute-start | bytes 1671176 | tf_op jit(solution)/shard_map/ppermute | solution.py:263
  56.2 19.5 %collective-permute-start.11 = (s16[272,1024]{1,0:T(8,128)(2,1)}, s16[272,1024]{1,0:T(8,128)(2,1)S(1)}, u32[]{:S(2)}, u32[]{:S(2)}) collective-permute-start(s16[272,1024]{1,0:T(8,128)(2,1)} %get-tuple-element.32), channel_id=1, source_target_pairs={{0,4},{4,8},{8,12},{12,0},{1,5},{5,9},{9,13},{13,1},{2,6},{6,10},{... | collective-permute-start | bytes 1671176 | tf_op jit(solution)/shard_map/ppermute | solution.py:263
  62.4 13.3 %collective-permute-start.12 = (s16[272,1024]{1,0:T(8,128)(2,1)}, s16[272,1024]{1,0:T(8,128)(2,1)S(1)}, u32[]{:S(2)}, u32[]{:S(2)}) collective-permute-start(s16[272,1024]{1,0:T(8,128)(2,1)} %get-tuple-element.33), channel_id=1, source_target_pairs={{0,12},{4,0},{8,4},{12,8},{1,13},{5,1},{9,5},{13,9},{2,14},{6,2},{... | collective-permute-start | bytes 1671176 | tf_op jit(solution)/shard_map/ppermute | solution.py:263
  62.7 14.3 %collective-permute-start.15 = (s16[272,1024]{1,0:T(8,128)(2,1)}, s16[272,1024]{1,0:T(8,128)(2,1)S(1)}, u32[]{:S(2)}, u32[]{:S(2)}) collective-permute-start(s16[272,1024]{1,0:T(8,128)(2,1)} %get-tuple-element.36), channel_id=1, source_target_pairs={{0,1},{1,2},{2,3},{3,0},{4,5},{5,6},{6,7},{7,4},{8,9},{9,10},{10,1... | collective-permute-start | bytes 1671176 | tf_op jit(solution)/shard_map/ppermute | solution.py:263
  63.8 13.2 %collective-permute-start.16 = (s16[272,1024]{1,0:T(8,128)(2,1)}, s16[272,1024]{1,0:T(8,128)(2,1)S(1)}, u32[]{:S(2)}, u32[]{:S(2)}) collective-permute-start(s16[272,1024]{1,0:T(8,128)(2,1)} %get-tuple-element.37), channel_id=1, source_target_pairs={{0,3},{1,0},{2,1},{3,2},{4,7},{5,4},{6,5},{7,6},{8,11},{9,8},{10,9... | collective-permute-start | bytes 1671176 | tf_op jit(solution)/shard_map/ppermute | solution.py:263
  69.1 27.7 %copy-start.2 = (s32[256,1024]{1,0:T(8,128)S(1)}, s32[256,1024]{1,0:T(8,128)}, u32[]{:S(2)}) copy-start(s32[256,1024]{1,0:T(8,128)} %signs.5) | copy-start | bytes 3145732
  69.1 27.7 %copy-start.4 = (bf16[128,128]{1,0:T(8,128)(2,1)S(1)}, bf16[128,128]{1,0:T(8,128)(2,1)}, u32[]{:S(2)}) copy-start(bf16[128,128]{1,0:T(8,128)(2,1)} %constant.188.clone.inner) | copy-start | bytes 98308
  69.1 27.7 %copy-start.5 = (bf16[128,128]{1,0:T(8,128)(2,1)S(1)}, bf16[128,128]{1,0:T(8,128)(2,1)}, u32[]{:S(2)}) copy-start(bf16[128,128]{1,0:T(8,128)(2,1)} %constant.189.clone.rows) | copy-start | bytes 98308
  81.3 10.6 %collective-permute-start.20 = (s16[144,1024]{1,0:T(8,128)(2,1)}, s16[144,1024]{1,0:T(8,128)(2,1)S(1)}, u32[]{:S(2)}, u32[]{:S(2)}) collective-permute-start(s16[144,1024]{1,0:T(8,128)(2,1)} %get-tuple-element.43), channel_id=1, source_target_pairs={{0,1},{1,2},{2,3},{3,0},{4,5},{5,6},{6,7},{7,4},{8,9},{9,10},{10,1... | collective-permute-start | bytes 884744 | tf_op jit(solution)/shard_map/ppermute | solution.py:263
  81.3 11.2 %collective-permute-start.21 = (s16[144,1024]{1,0:T(8,128)(2,1)}, s16[144,1024]{1,0:T(8,128)(2,1)S(1)}, u32[]{:S(2)}, u32[]{:S(2)}) collective-permute-start(s16[144,1024]{1,0:T(8,128)(2,1)} %get-tuple-element.44), channel_id=1, source_target_pairs={{0,2},{1,3},{2,0},{3,1},{4,6},{5,7},{6,4},{7,5},{8,10},{9,11},{10,... | collective-permute-start | bytes 884744 | tf_op jit(solution)/shard_map/ppermute | solution.py:263
  83.2 13.6 %collective-permute-start.22 = (s16[144,1024]{1,0:T(8,128)(2,1)}, s16[144,1024]{1,0:T(8,128)(2,1)S(1)}, u32[]{:S(2)}, u32[]{:S(2)}) collective-permute-start(s16[144,1024]{1,0:T(8,128)(2,1)} %get-tuple-element.45), channel_id=1, source_target_pairs={{0,3},{1,0},{2,1},{3,2},{4,7},{5,4},{6,5},{7,6},{8,11},{9,8},{10,9... | collective-permute-start | bytes 884744 | tf_op jit(solution)/shard_map/ppermute | solution.py:263
  84.1 15.8 %collective-permute-start.17 = (s16[144,1024]{1,0:T(8,128)(2,1)}, s16[144,1024]{1,0:T(8,128)(2,1)S(1)}, u32[]{:S(2)}, u32[]{:S(2)}) collective-permute-start(s16[144,1024]{1,0:T(8,128)(2,1)} %get-tuple-element.39), channel_id=1, source_target_pairs={{0,4},{4,8},{8,12},{12,0},{1,5},{5,9},{9,13},{13,1},{2,6},{6,10},{... | collective-permute-start | bytes 884744 | tf_op jit(solution)/shard_map/ppermute | solution.py:263
  85.7 14.1 %collective-permute-start.18 = (s16[144,1024]{1,0:T(8,128)(2,1)}, s16[144,1024]{1,0:T(8,128)(2,1)S(1)}, u32[]{:S(2)}, u32[]{:S(2)}) collective-permute-start(s16[144,1024]{1,0:T(8,128)(2,1)} %get-tuple-element.40), channel_id=1, source_target_pairs={{0,8},{4,12},{8,0},{12,4},{1,9},{5,13},{9,1},{13,5},{2,10},{6,14},... | collective-permute-start | bytes 884744 | tf_op jit(solution)/shard_map/ppermute | solution.py:263
  91.9 8.3 %collective-permute-start.19 = (s16[144,1024]{1,0:T(8,128)(2,1)}, s16[144,1024]{1,0:T(8,128)(2,1)S(1)}, u32[]{:S(2)}, u32[]{:S(2)}) collective-permute-start(s16[144,1024]{1,0:T(8,128)(2,1)} %get-tuple-element.41), channel_id=1, source_target_pairs={{0,12},{4,0},{8,4},{12,8},{1,13},{5,1},{9,5},{13,9},{2,14},{6,2},{... | collective-permute-start | bytes 884744 | tf_op jit(solution)/shard_map/ppermute | solution.py:263
  103.2 14.6 %copy-start.1 = (bf16[512,1024]{1,0:T(8,128)(2,1)S(1)}, bf16[512,1024]{1,0:T(8,128)(2,1)}, u32[]{:S(2)}) copy-start(bf16[512,1024]{1,0:T(8,128)(2,1)} %c.9) | copy-start | bytes 3145732
  103.2 14.6 %collective-permute-start.23 = (bf16[2048,1024]{1,0:T(8,128)(2,1)}, bf16[2048,1024]{1,0:T(8,128)(2,1)}, u32[]{:S(2)}, u32[]{:S(2)}) collective-permute-start(bf16[2048,1024]{1,0:T(8,128)(2,1)} %tie.5), channel_id=1, source_target_pairs={{0,16},{16,0},{1,17},{17,1},{2,18},{18,2},{3,19},{19,3},{4,20},{20... | collective-permute-start | bytes 12582920 | tf_op jit(solution)/shard_map/ppermute | solution.py:398
  108.4 27.3 %all-to-all-start = ((s16[16,16,1152]{2,1,0:T(8,128)(2,1)}), s16[16,16,1152]{2,1,0:T(8,128)(2,1)S(1)}, u32[]{:S(2)}, u32[]{:S(2)}) async-start(s16[16,16,1152]{2,1,0:T(8,128)(2,1)} %bitcast.43), calls=%async_computation | async-start | bytes 1179648 | tf_op jit(solution)/shard_map/all_to_all | solution.py:395
  117.8 2.2 %copy-start.3 = (bf16[2048,1024]{1,0:T(8,128)(2,1)S(1)}, bf16[2048,1024]{1,0:T(8,128)(2,1)}, u32[]{:S(2)}) copy-start(bf16[2048,1024]{1,0:T(8,128)(2,1)} %tie.5) | copy-start | bytes 12582916
  120.0 15.7 %copy-start.6 = (bf16[16,16]{1,0:T(8,128)(2,1)S(1)}, bf16[16,16]{1,0:T(8,128)(2,1)}, u32[]{:S(2)}) copy-start(bf16[16,16]{1,0:T(8,128)(2,1)} %constant.190.clone.rows) | copy-start | bytes 1540
Sparse Core Ops, SparseCore 0:
  32.7 55.0 all-gather.1

commit v8 on v6

--- a/solution.py
+++ b/solution.py
@@ -403,7 +403,7 @@
         compiler_params=params(SMALL),
         cost_estimate=cost(4 * mm, 13 << 20),
         name="input_grad",
-    )(place, cotangent, w_own.reshape(NZ, 4, 4, 16, KV), w_oth.reshape(NZ, 4, 4, 16, KV))
+    )(place, cotangent, in_hbm(w_own.reshape(NZ, 4, 4, 16, KV)), in_hbm(w_oth.reshape(NZ, 4, 4, 16, KV)))
 
     back = pl.pallas_call(
         levels_kernel,

time: 159 us -> 159 us (level)
  local copies, waits for them, and re-layouts: 6.92 us -> 4.7 us
  waiting for transfers between devices: 22.3 us -> 23.9 us
    unnamed x28 -> x26, local copies, waits for them, and re-layouts: 6.8 us -> 4.58 us
where the time goes in v8:
time: 159 us; the launch traced here: 158 us
  starting transfers between devices  51 us (32%)
  Pallas kernels  46.6 us (29%)
  waiting for transfers between devices  23.9 us (15%)
  blocking collectives  16.1 us (10%)
  between operations  14.9 us (9%)
  local copies, waits for them, and re-layouts  4.7 us (3%)
    ppermute x18, starting transfers between devices, send(): return lax.ppermute(v, 'xy'[axis], shift((NX, NY)[axis], s))  29.1 us
    all_gather x1, blocking collectives, shards(): gathered = lax.all_gather(back, ('z', 'core'), axis=0, tiled=True)  16.1 us
    ppermute x18, waiting for transfers between devices, send(): return lax.ppermute(v, 'xy'[axis], shift((NX, NY)[axis], s))  15.4 us
    ppermute x6, starting transfers between devices, spread(): return [lax.ppermute(piece, axis, shift(4, s)) for s in (1, 2, 3)]  10.7 us
    pallas_call x1, Pallas kernels, shards(): pl.pallas_call(input_grad_kernel, out_shape=pltpu.HBM((TOK, 4096), BF16),...  9.47 us
    pallas_call x2, Pallas kernels, far(): pl.pallas_call(far_kernel, out_shape=(message, message, sds((8, KV), F32)...  8.65 us
    all_to_all x1, waiting for transfers between devices, shards(): groups = lax.all_to_all(spun, ('z', 'core'), 0, 0, tiled=True)  8.45 us
    pallas_call x1, Pallas kernels, shards(): pl.pallas_call(near_kernel, out_shape=(message,) * 4 + (sds((1024, KV), F...  8.43 us
  transfers between devices with their start and end apart: 27, of which 7 were waited for; matrix products, arithmetic and copies ran while one was open for 1% of the time, Pallas kernels for 28%

profile of v8, /device:TPU:1, one launch (start us, length us, event | category | flops | bytes accessed | tf_op | source)
XLA Modules:
  0.0 158.1 jit_solution(6497121264661200160)
XLA Ops:
  7.2 0.0 all-gather.2.cloned.1.call-start
  7.2 0.8 constant_dynamic-update-slice_fusion.6
  8.0 2.0 %collective-permute-start = (bf16[16,1024]{1,0:T(8,128)(2,1)S(1)}, bf16[16,1024]{1,0:T(8,128)(2,1)S(1)}, u32[]{:S(2)}, u32[]{:S(2)}) collective-permute-start(bf16[16,1024]{1,0:T(8,128)(2,1)S(1)} %get-tuple-element.47), channel_id=1, source_target_pairs={{0,4},{4,8},{8,12},{12,0},{1,5},{5,9},{9,13},{13,1},{2,6},{6,10},{... | collective-permute-start | bytes 98312 | tf_op jit(solution)/shard_map/ppermute | solution.py:276
  10.0 2.5 %collective-permute-start.1 = (bf16[16,1024]{1,0:T(8,128)(2,1)S(1)}, bf16[16,1024]{1,0:T(8,128)(2,1)S(1)}, u32[]{:S(2)}, u32[]{:S(2)}) collective-permute-start(bf16[16,1024]{1,0:T(8,128)(2,1)S(1)} %get-tuple-element.47), channel_id=1, source_target_pairs={{0,8},{4,12},{8,0},{12,4},{1,9},{5,13},{9,1},{13,5},{2,10},{6,14},... | collective-permute-start | bytes 98312 | tf_op jit(solution)/shard_map/ppermute | solution.py:276
  12.5 1.2 collective-permute-start.2
  13.6 0.1 stack.147.idx
  13.7 4.3 %far.2 = (s16[272,1024]{1,0:T(8,128)(2,1)}, s16[272,1024]{1,0:T(8,128)(2,1)}, f32[8,1024]{1,0:T(8,128)S(1)}) custom-call(s32[32]{0:T(128)S(1)} %stack.147.idx, bf16[512,4096]{1,0:T(8,128)(2,1)} %t3.7, bf16[512,4096]{1,0:T(8,128)(2,1)} %t3.7, bf16[512,4096]{1,0:T(8,128)(2,1)} %t3.7, bf16[512,4096]{1,0:T(8,128)(2,1)} %t3.7, bf16[512,1024]{1,0:T(8,128)(2,1)} %c.9), custom_call_target="tpu_custom_call" | custom-call | flops 536870912 | bytes 3145728 | tf_op jit(solution)/shard_map/far/pallas_call | solution.py:290
  18.0 0.0 collective-permute-done.w
  18.0 0.6 copy-done.8
  18.6 0.8 pad_maximum_fusion.refs_0_
  19.4 1.4 collective-permute-start.3
  20.8 2.6 %collective-permute-start.4 = (bf16[64,1024]{1,0:T(8,128)(2,1)S(1)}, bf16[64,1024]{1,0:T(8,128)(2,1)S(1)}, u32[]{:S(2)}, u32[]{:S(2)}) collective-permute-start(bf16[64,1024]{1,0:T(8,128)(2,1)S(1)} %pad_maximum_fusion.refs_0_), channel_id=1, source_target_pairs={{0,2},{1,3},{2,0},{3,1},{4,6},{5,7},{6,4},{7,5},{8,10},{9,11},{10,... | collective-permute-start | bytes 393224 | tf_op jit(solution)/shard_map/ppermute | solution.py:276
  23.4 1.1 collective-permute-start.5
  24.5 0.8 constant_dynamic-update-slice_fusion.5
  25.2 0.0 copy-start.6
  25.3 0.0 copy-start.9
  25.3 4.4 %far.3 = (s16[272,1024]{1,0:T(8,128)(2,1)}, s16[272,1024]{1,0:T(8,128)(2,1)}, f32[8,1024]{1,0:T(8,128)}) custom-call(s32[32]{0:T(128)S(1)} %stack.147.idx, bf16[512,4096]{1,0:T(8,128)(2,1)} %t3.7, bf16[512,4096]{1,0:T(8,128)(2,1)} %t3.7, bf16[512,4096]{1,0:T(8,128)(2,1)} %t3.7, bf16[512,4096]{1,0:T(8,128)(2,1)} %t3.7, bf16[512,1024]{1,0:T(8,128)(2,1)} %c.9, ...), custom_call_target="tpu_custom_call" | custom-call | flops 536870912 | bytes 3145728 | tf_op jit(solution)/shard_map/far/pallas_call | solution.py:290
  29.6 0.0 collective-permute-done.3.w
  29.6 0.6 copy-done.7
  30.3 0.9 constant_dynamic-update-slice_fusion.2
  31.3 0.8 copy-done.5
  32.1 0.0 all-gather.2.cloned.1.call-update
  32.1 0.4 collective-permute-start.8
  32.5 2.4 %collective-permute-start.9 = (s16[272,1024]{1,0:T(8,128)(2,1)S(1)}, s16[272,1024]{1,0:T(8,128)(2,1)S(1)}, u32[]{:S(2)}, u32[]{:S(2)}) collective-permute-start(s16[272,1024]{1,0:T(8,128)(2,1)S(1)} %copy-done.9), channel_id=1, source_target_pairs={{0,12},{4,0},{8,4},{12,8},{1,13},{5,1},{9,5},{13,9},{2,14},{6,2},{... | collective-permute-start | bytes 1671176 | tf_op jit(solution)/shard_map/ppermute | solution.py:262
  34.9 0.4 collective-permute-start.10
  35.3 2.3 %collective-permute-start.11 = (s16[272,1024]{1,0:T(8,128)(2,1)}, s16[272,1024]{1,0:T(8,128)(2,1)S(1)}, u32[]{:S(2)}, u32[]{:S(2)}) collective-permute-start(s16[272,1024]{1,0:T(8,128)(2,1)} %get-tuple-element.31), channel_id=1, source_target_pairs={{0,3},{1,0},{2,1},{3,2},{4,7},{5,4},{6,5},{7,6},{8,11},{9,8},{10,9... | collective-permute-start | bytes 1671176 | tf_op jit(solution)/shard_map/ppermute | solution.py:262
  37.6 8.4 %near.1 = (s16[272,1024]{1,0:T(8,128)(2,1)}, s16[272,1024]{1,0:T(8,128)(2,1)}, s16[272,1024]{1,0:T(8,128)(2,1)}, s16[272,1024]{1,0:T(8,128)(2,1)}, f32[1024,1024]{1,0:T(8,128)S(1)}) custom-call(s32[32]{0:T(128)S(1)} %stack.147.idx, bf16[512,4096]{1,0:T(8,128)(2,1)} %t3.7, bf16[512,4096]{1,0:T(8,128)(2,1)} %t3.7, bf16[512,4096]{1,0:T(8,128)(2,1)} %t3.7, ...), custom_call_target="tpu_custom_call" | custom-call | flops 2147483648 | bytes 11534336 | tf_op jit(solution)/shard_map/near/pallas_call | solution.py:312
  46.0 0.0 collective-permute-start.14
  46.0 0.0 collective-permute-done.8.refs_0_
  46.0 2.7 %collective-permute-start.15 = (s16[272,1024]{1,0:T(8,128)(2,1)}, s16[272,1024]{1,0:T(8,128)(2,1)S(1)}, u32[]{:S(2)}, u32[]{:S(2)}) collective-permute-start(s16[272,1024]{1,0:T(8,128)(2,1)} %get-tuple-element.35), channel_id=1, source_target_pairs={{0,3},{1,0},{2,1},{3,2},{4,7},{5,4},{6,5},{7,6},{8,11},{9,8},{10,9... | collective-permute-start | bytes 1671176 | tf_op jit(solution)/shard_map/ppermute | solution.py:262
  48.7 0.0 collective-permute-done.9.refs_1_
  48.7 0.0 collective-permute-start.6
  48.7 0.0 collective-permute-done.10.refs_2_
  48.7 2.7 %collective-permute-start.7 = (s16[272,1024]{1,0:T(8,128)(2,1)}, s16[272,1024]{1,0:T(8,128)(2,1)S(1)}, u32[]{:S(2)}, u32[]{:S(2)}) collective-permute-start(s16[272,1024]{1,0:T(8,128)(2,1)} %get-tuple-element.28), channel_id=1, source_target_pairs={{0,12},{4,0},{8,4},{12,8},{1,13},{5,1},{9,5},{13,9},{2,14},{6,2},{... | collective-permute-start | bytes 1671176 | tf_op jit(solution)/shard_map/ppermute | solution.py:262
  51.4 3.9 %relay.1 = (s16[272,1024]{1,0:T(8,128)(2,1)}, s16[272,1024]{1,0:T(8,128)(2,1)}, s16[272,1024]{1,0:T(8,128)(2,1)}, s16[272,1024]{1,0:T(8,128)(2,1)}) custom-call(f32[1024,1024]{1,0:T(8,128)S(1)} %get-tuple-element.29.keep, f32[8,1024]{1,0:T(8,128)S(1)} %get-tuple-element.26.ce, s16[272,1024]{1,0:T(8,128)(2,1)S(1)} %collective-permute-done.8.refs_0_, ...), custom_call_target="tpu_custom_call" | custom-call | flops 1048576 | bytes 8388608 | tf_op jit(solution)/shard_map/relay/pallas_call | solution.py:341
  55.3 0.0 collective-permute-start.12
  55.3 4.5 %collective-permute-done.14.refs_4_ = s16[272,1024]{1,0:T(8,128)(2,1)S(1)} collective-permute-done((s16[272,1024]{1,0:T(8,128)(2,1)}, s16[272,1024]{1,0:T(8,128)(2,1)S(1)}, u32[]{:S(2)}, u32[]{:S(2)}) %collective-permute-start.14) | collective-permute-done | bytes 557088 | tf_op jit(solution)/shard_map/ppermute | solution.py:262
  59.8 0.3 collective-permute-start.13
  60.1 0.2 collective-permute-done.6.refs_0_
  60.3 2.5 %collective-permute-start.17 = (s16[272,1024]{1,0:T(8,128)(2,1)}, s16[272,1024]{1,0:T(8,128)(2,1)S(1)}, u32[]{:S(2)}, u32[]{:S(2)}) collective-permute-start(s16[272,1024]{1,0:T(8,128)(2,1)} %get-tuple-element.37), channel_id=1, source_target_pairs={{0,3},{1,0},{2,1},{3,2},{4,7},{5,4},{6,5},{7,6},{8,11},{9,8},{10,9... | collective-permute-start | bytes 1671176 | tf_op jit(solution)/shard_map/ppermute | solution.py:262
  62.8 3.7 %own.1.keep = f32[1024,1024]{1,0:T(8,128)S(1)} custom-call(s32[32]{0:T(128)S(1)} %stack.147.idx, bf16[512,4096]{1,0:T(8,128)(2,1)} %t3.7, bf16[512,4096]{1,0:T(8,128)(2,1)} %t3.7, bf16[512,4096]{1,0:T(8,128)(2,1)} %t3.7, bf16[512,4096]{1,0:T(8,128)(2,1)} %t3.7, bf16[512,1024]{1,0:T(8,128)(2,1)} %c.9), custom_call_target="tpu_custom_call" | custom-call | flops 1073741824 | bytes 8388608 | tf_op jit(solution)/shard_map/own/pallas_call | solution.py:327
  66.5 0.0 copy-start.1
  66.5 0.0 copy-start.2
  66.5 0.0 copy-start.3
  66.6 5.7 %collective-permute-done.12.refs_2_ = s16[272,1024]{1,0:T(8,128)(2,1)S(1)} collective-permute-done((s16[272,1024]{1,0:T(8,128)(2,1)}, s16[272,1024]{1,0:T(8,128)(2,1)S(1)}, u32[]{:S(2)}, u32[]{:S(2)}) %collective-permute-start.12) | collective-permute-done | bytes 557088 | tf_op jit(solution)/shard_map/ppermute | solution.py:262
  72.2 0.7 collective-permute-done.13.refs_3_
  73.0 4.3 %cross.1 = (f32[128,1024]{1,0:T(8,128)}, s16[144,1024]{1,0:T(8,128)(2,1)}, s16[144,1024]{1,0:T(8,128)(2,1)}, s16[144,1024]{1,0:T(8,128)(2,1)}, f32[128,1024]{1,0...) custom-call(f32[1024,1024]{1,0:T(8,128)S(1)} %own.1.keep, ...), custom_call_target="tpu_custom_call" | custom-call | flops 1048576 | bytes 12582912 | tf_op jit(solution)/shard_map/cross/pallas_call | solution.py:353
  77.2 1.6 %collective-permute-start.22 = (s16[144,1024]{1,0:T(8,128)(2,1)}, s16[144,1024]{1,0:T(8,128)(2,1)S(1)}, u32[]{:S(2)}, u32[]{:S(2)}) collective-permute-start(s16[144,1024]{1,0:T(8,128)(2,1)} %get-tuple-element.44), channel_id=1, source_target_pairs={{0,2},{1,3},{2,0},{3,1},{4,6},{5,7},{6,4},{7,5},{8,10},{9,11},{10,... | collective-permute-start | bytes 884744 | tf_op jit(solution)/shard_map/ppermute | solution.py:262
  78.8 1.1 collective-permute-start.23
  79.9 1.1 collective-permute-start.18
  81.0 3.5 %collective-permute-start.19 = (s16[144,1024]{1,0:T(8,128)(2,1)}, s16[144,1024]{1,0:T(8,128)(2,1)S(1)}, u32[]{:S(2)}, u32[]{:S(2)}) collective-permute-start(s16[144,1024]{1,0:T(8,128)(2,1)} %get-tuple-element.40), channel_id=1, source_target_pairs={{0,8},{4,12},{8,0},{12,4},{1,9},{5,13},{9,1},{13,5},{2,10},{6,14},... | collective-permute-start | bytes 884744 | tf_op jit(solution)/shard_map/ppermute | solution.py:262
  84.5 2.9 %collective-permute-done.21.n1 = s16[144,1024]{1,0:T(8,128)(2,1)S(1)} collective-permute-done((s16[144,1024]{1,0:T(8,128)(2,1)}, s16[144,1024]{1,0:T(8,128)(2,1)S(1)}, u32[]{:S(2)}, u32[]{:S(2)}) %collective-permute-start.21) | collective-permute-done | bytes 294944 | tf_op jit(solution)/shard_map/ppermute | solution.py:262
  87.4 8.3 %collective-permute-start.20 = (s16[144,1024]{1,0:T(8,128)(2,1)}, s16[144,1024]{1,0:T(8,128)(2,1)S(1)}, u32[]{:S(2)}, u32[]{:S(2)}) collective-permute-start(s16[144,1024]{1,0:T(8,128)(2,1)} %get-tuple-element.41), channel_id=1, source_target_pairs={{0,12},{4,0},{8,4},{12,8},{1,13},{5,1},{9,5},{13,9},{2,14},{6,2},{... | collective-permute-start | bytes 884744 | tf_op jit(solution)/shard_map/ppermute | solution.py:262
  95.7 3.0 %rotate.2.refs_0_ = s16[256,1152]{1,0:T(8,128)(2,1)} custom-call(f32[128,1024]{1,0:T(8,128)} %get-tuple-element.42.own, s16[144,1024]{1,0:T(8,128)(2,1)S(1)} %collective-permute-done.21.n1, s16[144,1024]{1,0:T(8,128)(2,1)S(1)} %collective-permute-done.22.n2, s16[144,1024]{1,0:T(8,128)(2,1)S(1)} %collective-permute-done.23.n3, s32[256,1024]{1,0:T(8,128)S(1)} %copy-done.1, ...), custom_call_target="tpu_custom_call" | custom-call | flops 134217728 | bytes 2097152 | tf_op jit(solution)/shard_map/rotate/pallas_call | solution.py:371
  98.7 1.4 collective-permute-done.20.n3
  100.1 3.0 %rotate.3.after = s16[256,1152]{1,0:T(8,128)(2,1)} custom-call(f32[128,1024]{1,0:T(8,128)} %get-tuple-element.38.own, s16[144,1024]{1,0:T(8,128)(2,1)S(1)} %collective-permute-done.18.n1, s16[144,1024]{1,0:T(8,128)(2,1)S(1)} %collective-permute-done.19.n2, s16[144,1024]{1,0:T(8,128)(2,1)S(1)} %collective-permute-done.20.n3, ...), custom_call_target="tpu_custom_call", output_to_operand_aliasing={{}: (7, {})} | custom-call | flops 134217728 | bytes 2097152 | tf_op jit(solution)/shard_map/rotate/pallas_call | solution.py:371
  103.1 3.1 %collective-permute-start.24 = (bf16[2048,1024]{1,0:T(8,128)(2,1)}, bf16[2048,1024]{1,0:T(8,128)(2,1)}, u32[]{:S(2)}, u32[]{:S(2)}) collective-permute-start(bf16[2048,1024]{1,0:T(8,128)(2,1)} %tie.5), channel_id=1, source_target_pairs={{0,16},{16,0},{1,17},{17,1},{2,18},{18,2},{3,19},{19,3},{4,20},{20... | collective-permute-start | bytes 12582920 | tf_op jit(solution)/shard_map/ppermute | solution.py:390
  106.2 8.1 %all-to-all-start = ((s16[16,16,1152]{2,1,0:T(8,128)(2,1)}), s16[16,16,1152]{2,1,0:T(8,128)(2,1)S(1)}, u32[]{:S(2)}, u32[]{:S(2)}) async-start(s16[16,16,1152]{2,1,0:T(8,128)(2,1)} %bitcast.38), calls=%async_computation | async-start | bytes 1179648 | tf_op jit(solution)/shard_map/all_to_all | solution.py:387
  114.9 0.1 pad_add_fusion.at
  115.0 9.5 %input_grad.1.after = bf16[512,4096]{1,0:T(8,128)(2,1)} custom-call(s32[3]{0:T(128)S(1)} %pad_add_fusion.at, bf16[512,1024]{1,0:T(8,128)(2,1)S(1)} %copy-done, bf16[8,4,4,16,1024]{4,3,2,1,0:T(8,128)(2,1)} %bitcast.42, bf16[8,4,4,16,1024]{4,3,2,1,0:T(8,128)(2,1)} %bitcast.36.w_oth), custom_call_target="tpu_custom_call" | custom-call | flops 4294967296 | bytes 13631488 | tf_op jit(solution)/shard_map/input_grad/pallas_call | solution.py:393
  124.5 8.4 %all-to-all-done = s16[16,16,1152]{2,1,0:T(8,128)(2,1)S(1)} async-done(((s16[16,16,1152]{2,1,0:T(8,128)(2,1)}), s16[16,16,1152]{2,1,0:T(8,128)(2,1)S(1)}, u32[]{:S(2)}, u32[]{:S(2)}) %all-to-all-start) | async-done | bytes 589856 | tf_op jit(solution)/shard_map/all_to_all | solution.py:387
  132.9 1.0 levels.1
  133.9 16.1 %all_gather.7.q = s16[256,1152]{1,0:T(8,128)(2,1)S(1)} all-gather(s16[16,1152]{1,0:T(8,128)(2,1)S(1)} %levels.1), channel_id=1, replica_groups=mesh['z'=8,'core'=2,'x'=4,'y'=4] {'z','core'}, dimensions={0}, use_global_device_ids=true | all-gather | bytes 626688 | tf_op jit(solution)/shard_map/all_gather | solution.py:417
  150.0 1.2 finish.1
  (36 shorter events, 0.1 us)
Async XLA Ops:
  7.2 96.0 %all-gather.2.cloned.1.call-start = ((), (), s32[]{:S(2)}) async-start(), calls=%async_computation.1 | async-start | bytes 4718592 | tf_op jit(solution)/shard_map/all_gather | solution.py:309
  8.0 10.0 %collective-permute-start = (bf16[16,1024]{1,0:T(8,128)(2,1)S(1)}, bf16[16,1024]{1,0:T(8,128)(2,1)S(1)}, u32[]{:S(2)}, u32[]{:S(2)}) collective-permute-start(bf16[16,1024]{1,0:T(8,128)(2,1)S(1)} %get-tuple-element.47), channel_id=1, source_target_pairs={{0,4},{4,8},{8,12},{12,0},{1,5},{5,9},{9,13},{13,1},{2,6},{6,10},{... | collective-permute-start | bytes 98312 | tf_op jit(solution)/shard_map/ppermute | solution.py:276
  10.0 8.6 %collective-permute-start.1 = (bf16[16,1024]{1,0:T(8,128)(2,1)S(1)}, bf16[16,1024]{1,0:T(8,128)(2,1)S(1)}, u32[]{:S(2)}, u32[]{:S(2)}) collective-permute-start(bf16[16,1024]{1,0:T(8,128)(2,1)S(1)} %get-tuple-element.47), channel_id=1, source_target_pairs={{0,8},{4,12},{8,0},{12,4},{1,9},{5,13},{9,1},{13,5},{2,10},{6,14},... | collective-permute-start | bytes 98312 | tf_op jit(solution)/shard_map/ppermute | solution.py:276
  12.5 6.2 %collective-permute-start.2 = (bf16[16,1024]{1,0:T(8,128)(2,1)S(1)}, bf16[16,1024]{1,0:T(8,128)(2,1)S(1)}, u32[]{:S(2)}, u32[]{:S(2)}) collective-permute-start(bf16[16,1024]{1,0:T(8,128)(2,1)S(1)} %get-tuple-element.47), channel_id=1, source_target_pairs={{0,12},{4,0},{8,4},{12,8},{1,13},{5,1},{9,5},{13,9},{2,14},{6,2},{... | collective-permute-start | bytes 98312 | tf_op jit(solution)/shard_map/ppermute | solution.py:276
  18.0 0.6 copy-start.8
  19.4 10.2 %collective-permute-start.3 = (bf16[64,1024]{1,0:T(8,128)(2,1)S(1)}, bf16[64,1024]{1,0:T(8,128)(2,1)S(1)}, u32[]{:S(2)}, u32[]{:S(2)}) collective-permute-start(bf16[64,1024]{1,0:T(8,128)(2,1)S(1)} %pad_maximum_fusion.refs_0_), channel_id=1, source_target_pairs={{0,1},{1,2},{2,3},{3,0},{4,5},{5,6},{6,7},{7,4},{8,9},{9,10},{10,1... | collective-permute-start | bytes 393224 | tf_op jit(solution)/shard_map/ppermute | solution.py:276
  20.8 10.4 %collective-permute-start.4 = (bf16[64,1024]{1,0:T(8,128)(2,1)S(1)}, bf16[64,1024]{1,0:T(8,128)(2,1)S(1)}, u32[]{:S(2)}, u32[]{:S(2)}) collective-permute-start(bf16[64,1024]{1,0:T(8,128)(2,1)S(1)} %pad_maximum_fusion.refs_0_), channel_id=1, source_target_pairs={{0,2},{1,3},{2,0},{3,1},{4,6},{5,7},{6,4},{7,5},{8,10},{9,11},{10,... | collective-permute-start | bytes 393224 | tf_op jit(solution)/shard_map/ppermute | solution.py:276
  23.4 7.8 %collective-permute-start.5 = (bf16[64,1024]{1,0:T(8,128)(2,1)S(1)}, bf16[64,1024]{1,0:T(8,128)(2,1)S(1)}, u32[]{:S(2)}, u32[]{:S(2)}) collective-permute-start(bf16[64,1024]{1,0:T(8,128)(2,1)S(1)} %pad_maximum_fusion.refs_0_), channel_id=1, source_target_pairs={{0,3},{1,0},{2,1},{3,2},{4,7},{5,4},{6,5},{7,6},{8,11},{9,8},{10,9... | collective-permute-start | bytes 393224 | tf_op jit(solution)/shard_map/ppermute | solution.py:276
  25.2 6.9 %copy-start.6 = (s16[272,1024]{1,0:T(8,128)(2,1)S(1)}, s16[272,1024]{1,0:T(8,128)(2,1)}, u32[]{:S(2)}) copy-start(s16[272,1024]{1,0:T(8,128)(2,1)} %get-tuple-element.24.after) | copy-start | bytes 1671172
  25.3 7.3 %copy-start.9 = (s16[272,1024]{1,0:T(8,128)(2,1)S(1)}, s16[272,1024]{1,0:T(8,128)(2,1)}, u32[]{:S(2)}) copy-start(s16[272,1024]{1,0:T(8,128)(2,1)} %get-tuple-element.30) | copy-start | bytes 1671172
  29.6 0.6 copy-start.7
  31.3 0.9 copy-start.5
  32.1 13.9 %collective-permute-start.8 = (s16[272,1024]{1,0:T(8,128)(2,1)S(1)}, s16[272,1024]{1,0:T(8,128)(2,1)S(1)}, u32[]{:S(2)}, u32[]{:S(2)}) collective-permute-start(s16[272,1024]{1,0:T(8,128)(2,1)S(1)} %copy-done.6), channel_id=1, source_target_pairs={{0,4},{4,8},{8,12},{12,0},{1,5},{5,9},{9,13},{13,1},{2,6},{6,10},{... | collective-permute-start | bytes 1671176 | tf_op jit(solution)/shard_map/ppermute | solution.py:262
  32.5 16.2 %collective-permute-start.9 = (s16[272,1024]{1,0:T(8,128)(2,1)S(1)}, s16[272,1024]{1,0:T(8,128)(2,1)S(1)}, u32[]{:S(2)}, u32[]{:S(2)}) collective-permute-start(s16[272,1024]{1,0:T(8,128)(2,1)S(1)} %copy-done.9), channel_id=1, source_target_pairs={{0,12},{4,0},{8,4},{12,8},{1,13},{5,1},{9,5},{13,9},{2,14},{6,2},{... | collective-permute-start | bytes 1671176 | tf_op jit(solution)/shard_map/ppermute | solution.py:262
  34.9 13.8 %collective-permute-start.10 = (s16[272,1024]{1,0:T(8,128)(2,1)}, s16[272,1024]{1,0:T(8,128)(2,1)S(1)}, u32[]{:S(2)}, u32[]{:S(2)}) collective-permute-start(s16[272,1024]{1,0:T(8,128)(2,1)} %get-tuple-element.25.after), channel_id=1, source_target_pairs={{0,1},{1,2},{2,3},{3,0},{4,5},{5,6},{6,7},{7,4},{8,9},{9,10},{10,1... | collective-permute-start | bytes 1671176 | tf_op jit(solution)/shard_map/ppermute | solution.py:262
  35.3 16.1 %collective-permute-start.11 = (s16[272,1024]{1,0:T(8,128)(2,1)}, s16[272,1024]{1,0:T(8,128)(2,1)S(1)}, u32[]{:S(2)}, u32[]{:S(2)}) collective-permute-start(s16[272,1024]{1,0:T(8,128)(2,1)} %get-tuple-element.31), channel_id=1, source_target_pairs={{0,3},{1,0},{2,1},{3,2},{4,7},{5,4},{6,5},{7,6},{8,11},{9,8},{10,9... | collective-permute-start | bytes 1671176 | tf_op jit(solution)/shard_map/ppermute | solution.py:262
  46.0 13.8 %collective-permute-start.14 = (s16[272,1024]{1,0:T(8,128)(2,1)}, s16[272,1024]{1,0:T(8,128)(2,1)S(1)}, u32[]{:S(2)}, u32[]{:S(2)}) collective-permute-start(s16[272,1024]{1,0:T(8,128)(2,1)} %get-tuple-element.34), channel_id=1, source_target_pairs={{0,1},{1,2},{2,3},{3,0},{4,5},{5,6},{6,7},{7,4},{8,9},{9,10},{10,1... | collective-permute-start | bytes 1671176 | tf_op jit(solution)/shard_map/ppermute | solution.py:262
  46.0 14.1 %collective-permute-start.15 = (s16[272,1024]{1,0:T(8,128)(2,1)}, s16[272,1024]{1,0:T(8,128)(2,1)S(1)}, u32[]{:S(2)}, u32[]{:S(2)}) collective-permute-start(s16[272,1024]{1,0:T(8,128)(2,1)} %get-tuple-element.35), channel_id=1, source_target_pairs={{0,3},{1,0},{2,1},{3,2},{4,7},{5,4},{6,5},{7,6},{8,11},{9,8},{10,9... | collective-permute-start | bytes 1671176 | tf_op jit(solution)/shard_map/ppermute | solution.py:262
  48.7 11.6 %collective-permute-start.6 = (s16[272,1024]{1,0:T(8,128)(2,1)}, s16[272,1024]{1,0:T(8,128)(2,1)S(1)}, u32[]{:S(2)}, u32[]{:S(2)}) collective-permute-start(s16[272,1024]{1,0:T(8,128)(2,1)} %get-tuple-element.27), channel_id=1, source_target_pairs={{0,4},{4,8},{8,12},{12,0},{1,5},{5,9},{9,13},{13,1},{2,6},{6,10},{... | collective-permute-start | bytes 1671176 | tf_op jit(solution)/shard_map/ppermute | solution.py:262
  48.7 17.9 %collective-permute-start.7 = (s16[272,1024]{1,0:T(8,128)(2,1)}, s16[272,1024]{1,0:T(8,128)(2,1)S(1)}, u32[]{:S(2)}, u32[]{:S(2)}) collective-permute-start(s16[272,1024]{1,0:T(8,128)(2,1)} %get-tuple-element.28), channel_id=1, source_target_pairs={{0,12},{4,0},{8,4},{12,8},{1,13},{5,1},{9,5},{13,9},{2,14},{6,2},{... | collective-permute-start | bytes 1671176 | tf_op jit(solution)/shard_map/ppermute | solution.py:262
  55.3 16.9 %collective-permute-start.12 = (s16[272,1024]{1,0:T(8,128)(2,1)}, s16[272,1024]{1,0:T(8,128)(2,1)S(1)}, u32[]{:S(2)}, u32[]{:S(2)}) collective-permute-start(s16[272,1024]{1,0:T(8,128)(2,1)} %get-tuple-element.32), channel_id=1, source_target_pairs={{0,4},{4,8},{8,12},{12,0},{1,5},{5,9},{9,13},{13,1},{2,6},{6,10},{... | collective-permute-start | bytes 1671176 | tf_op jit(solution)/shard_map/ppermute | solution.py:262
  59.8 13.1 %collective-permute-start.13 = (s16[272,1024]{1,0:T(8,128)(2,1)}, s16[272,1024]{1,0:T(8,128)(2,1)S(1)}, u32[]{:S(2)}, u32[]{:S(2)}) collective-permute-start(s16[272,1024]{1,0:T(8,128)(2,1)} %get-tuple-element.33), channel_id=1, source_target_pairs={{0,12},{4,0},{8,4},{12,8},{1,13},{5,1},{9,5},{13,9},{2,14},{6,2},{... | collective-permute-start | bytes 1671176 | tf_op jit(solution)/shard_map/ppermute | solution.py:262
  60.1 12.8 %collective-permute-start.16 = (s16[272,1024]{1,0:T(8,128)(2,1)}, s16[272,1024]{1,0:T(8,128)(2,1)S(1)}, u32[]{:S(2)}, u32[]{:S(2)}) collective-permute-start(s16[272,1024]{1,0:T(8,128)(2,1)} %get-tuple-element.36), channel_id=1, source_target_pairs={{0,1},{1,2},{2,3},{3,0},{4,5},{5,6},{6,7},{7,4},{8,9},{9,10},{10,1... | collective-permute-start | bytes 1671176 | tf_op jit(solution)/shard_map/ppermute | solution.py:262
  60.3 12.7 %collective-permute-start.17 = (s16[272,1024]{1,0:T(8,128)(2,1)}, s16[272,1024]{1,0:T(8,128)(2,1)S(1)}, u32[]{:S(2)}, u32[]{:S(2)}) collective-permute-start(s16[272,1024]{1,0:T(8,128)(2,1)} %get-tuple-element.37), channel_id=1, source_target_pairs={{0,3},{1,0},{2,1},{3,2},{4,7},{5,4},{6,5},{7,6},{8,11},{9,8},{10,9... | collective-permute-start | bytes 1671176 | tf_op jit(solution)/shard_map/ppermute | solution.py:262
  66.5 29.1 %copy-start.1 = (s32[256,1024]{1,0:T(8,128)S(1)}, s32[256,1024]{1,0:T(8,128)}, u32[]{:S(2)}) copy-start(s32[256,1024]{1,0:T(8,128)} %signs.5) | copy-start | bytes 3145732
  66.5 29.1 %copy-start.2 = (bf16[128,128]{1,0:T(8,128)(2,1)S(1)}, bf16[128,128]{1,0:T(8,128)(2,1)}, u32[]{:S(2)}) copy-start(bf16[128,128]{1,0:T(8,128)(2,1)} %constant.188.clone.inner) | copy-start | bytes 98308
  66.5 29.1 %copy-start.3 = (bf16[128,128]{1,0:T(8,128)(2,1)S(1)}, bf16[128,128]{1,0:T(8,128)(2,1)}, u32[]{:S(2)}) copy-start(bf16[128,128]{1,0:T(8,128)(2,1)} %constant.189.clone.rows) | copy-start | bytes 98308
  77.2 10.2 %collective-permute-start.21 = (s16[144,1024]{1,0:T(8,128)(2,1)}, s16[144,1024]{1,0:T(8,128)(2,1)S(1)}, u32[]{:S(2)}, u32[]{:S(2)}) collective-permute-start(s16[144,1024]{1,0:T(8,128)(2,1)} %get-tuple-element.43), channel_id=1, source_target_pairs={{0,1},{1,2},{2,3},{3,0},{4,5},{5,6},{6,7},{7,4},{8,9},{9,10},{10,1... | collective-permute-start | bytes 884744 | tf_op jit(solution)/shard_map/ppermute | solution.py:262
  77.2 18.4 %collective-permute-start.22 = (s16[144,1024]{1,0:T(8,128)(2,1)}, s16[144,1024]{1,0:T(8,128)(2,1)S(1)}, u32[]{:S(2)}, u32[]{:S(2)}) collective-permute-start(s16[144,1024]{1,0:T(8,128)(2,1)} %get-tuple-element.44), channel_id=1, source_target_pairs={{0,2},{1,3},{2,0},{3,1},{4,6},{5,7},{6,4},{7,5},{8,10},{9,11},{10,... | collective-permute-start | bytes 884744 | tf_op jit(solution)/shard_map/ppermute | solution.py:262
  78.8 16.8 %collective-permute-start.23 = (s16[144,1024]{1,0:T(8,128)(2,1)}, s16[144,1024]{1,0:T(8,128)(2,1)S(1)}, u32[]{:S(2)}, u32[]{:S(2)}) collective-permute-start(s16[144,1024]{1,0:T(8,128)(2,1)} %get-tuple-element.45), channel_id=1, source_target_pairs={{0,3},{1,0},{2,1},{3,2},{4,7},{5,4},{6,5},{7,6},{8,11},{9,8},{10,9... | collective-permute-start | bytes 884744 | tf_op jit(solution)/shard_map/ppermute | solution.py:262
  79.9 18.8 %collective-permute-start.18 = (s16[144,1024]{1,0:T(8,128)(2,1)}, s16[144,1024]{1,0:T(8,128)(2,1)S(1)}, u32[]{:S(2)}, u32[]{:S(2)}) collective-permute-start(s16[144,1024]{1,0:T(8,128)(2,1)} %get-tuple-element.39), channel_id=1, source_target_pairs={{0,4},{4,8},{8,12},{12,0},{1,5},{5,9},{9,13},{13,1},{2,6},{6,10},{... | collective-permute-start | bytes 884744 | tf_op jit(solution)/shard_map/ppermute | solution.py:262
  81.0 17.7 %collective-permute-start.19 = (s16[144,1024]{1,0:T(8,128)(2,1)}, s16[144,1024]{1,0:T(8,128)(2,1)S(1)}, u32[]{:S(2)}, u32[]{:S(2)}) collective-permute-start(s16[144,1024]{1,0:T(8,128)(2,1)} %get-tuple-element.40), channel_id=1, source_target_pairs={{0,8},{4,12},{8,0},{12,4},{1,9},{5,13},{9,1},{13,5},{2,10},{6,14},... | collective-permute-start | bytes 884744 | tf_op jit(solution)/shard_map/ppermute | solution.py:262
  87.4 12.8 %collective-permute-start.20 = (s16[144,1024]{1,0:T(8,128)(2,1)}, s16[144,1024]{1,0:T(8,128)(2,1)S(1)}, u32[]{:S(2)}, u32[]{:S(2)}) collective-permute-start(s16[144,1024]{1,0:T(8,128)(2,1)} %get-tuple-element.41), channel_id=1, source_target_pairs={{0,12},{4,0},{8,4},{12,8},{1,13},{5,1},{9,5},{13,9},{2,14},{6,2},{... | collective-permute-start | bytes 884744 | tf_op jit(solution)/shard_map/ppermute | solution.py:262
  103.1 11.9 %copy-start = (bf16[512,1024]{1,0:T(8,128)(2,1)S(1)}, bf16[512,1024]{1,0:T(8,128)(2,1)}, u32[]{:S(2)}) copy-start(bf16[512,1024]{1,0:T(8,128)(2,1)} %c.9) | copy-start | bytes 3145732
  103.1 11.9 %collective-permute-start.24 = (bf16[2048,1024]{1,0:T(8,128)(2,1)}, bf16[2048,1024]{1,0:T(8,128)(2,1)}, u32[]{:S(2)}, u32[]{:S(2)}) collective-permute-start(bf16[2048,1024]{1,0:T(8,128)(2,1)} %tie.5), channel_id=1, source_target_pairs={{0,16},{16,0},{1,17},{17,1},{2,18},{18,2},{3,19},{19,3},{4,20},{20... | collective-permute-start | bytes 12582920 | tf_op jit(solution)/shard_map/ppermute | solution.py:390
  106.2 26.7 %all-to-all-start = ((s16[16,16,1152]{2,1,0:T(8,128)(2,1)}), s16[16,16,1152]{2,1,0:T(8,128)(2,1)S(1)}, u32[]{:S(2)}, u32[]{:S(2)}) async-start(s16[16,16,1152]{2,1,0:T(8,128)(2,1)} %bitcast.38), calls=%async_computation | async-start | bytes 1179648 | tf_op jit(solution)/shard_map/all_to_all | solution.py:387
  115.0 17.9 %copy-start.4 = (bf16[16,16]{1,0:T(8,128)(2,1)S(1)}, bf16[16,16]{1,0:T(8,128)(2,1)}, u32[]{:S(2)}) copy-start(bf16[16,16]{1,0:T(8,128)(2,1)} %constant.190.clone.rows) | copy-start | bytes 1540
Sparse Core Ops, SparseCore 0:
  32.3 54.5 all-gather.1
